TPU v7x, 32 devices: a whole 2x2x4 slice. The times are simulated.
32 devices in a mesh: row: 8 (over z, y), col: 4 (over x, core).
Axes of the slice: x: 2, y: 2, z: 4, core: 2. Of those that a mesh axis runs over, the one named last changes fastest.
Arguments:
- diag_block: float32 [2048, 2048], P('row'), as said below
- z_panel: float32 [2048, 2048], P('row', 'col'), may hold values from -0.046875 to 0.046875
- panel_below: float32 [16384, 2048], P('row', 'col'), may hold values from -6 to 6
- z_trail: float32 [16384, 2048], P('row', 'col'), may hold values from -6 to 6
- norm_sq: float32 [2048], P('col'), may hold values from 0.05 to 0.5
Outputs:
- norm_out: float32 [2048], P('col')
- trail_out: float32 [16384, 2048], P('row', 'col')
Inputs may be any that keep to these rules, and one draw needn't show every extreme that they name: diag_block is zero above its diagonal; its diagonal entries are at least 1.
All inputs are finite; a program needn't handle non-finite values.
Results may differ from a plain program's by a relative error of at most 0.00017.
Values sent between devices are 32-bit elements; how exact they have to be, the bound alone decides.
No kernel may reach another device: no remote copies, remote signals or barrier semaphores. Data moves between devices by JAX's collectives and lax.ppermute only.
A program may use at most 64 MiB of HBM per device.

v0:
```python
import jax
import jax.numpy as jnp
from jax import lax
from jax.sharding import PartitionSpec as P


def shards(diag_block, z_panel, panel_below, z_trail, norm_sq):
    highest = lax.Precision.HIGHEST
    row_count = lax.axis_size("row")
    own_row = lax.axis_index("row")
    height = z_panel.shape[0]
    full_width = diag_block.shape[1]
    own_cols = z_panel.shape[1]
    identity = jnp.eye(height, dtype=jnp.float32)

    def advance(section, carry):
        solved, carried = carry
        diag_tile = lax.dynamic_slice_in_dim(diag_block, section * height, height, 1)
        is_owner = own_row == section
        pivot_tile = jnp.where(is_owner, diag_tile, identity)
        candidate = lax.linalg.triangular_solve(
            pivot_tile, z_panel - carried, left_side=True, lower=True
        )
        masked = jnp.where(is_owner, candidate, jnp.zeros_like(candidate))
        received = lax.psum(masked, "row")
        carried = carried + jnp.dot(
            diag_tile, received, precision=highest, preferred_element_type=jnp.float32
        )
        solved = lax.dynamic_update_slice_in_dim(solved, received, section * height, 0)
        return (solved, carried)

    start_solved = jnp.zeros((full_width, own_cols), jnp.float32)
    start_carried = jnp.zeros((height, own_cols), jnp.float32)
    solved, unused_carry = lax.fori_loop(0, row_count, advance, (start_solved, start_carried))
    norm_out = norm_sq + jnp.sum(solved * solved, axis=0)
    update = jnp.dot(
        lax.all_gather(panel_below, "col", axis=1, tiled=True),
        solved,
        precision=highest,
        preferred_element_type=jnp.float32,
    )
    trail_out = z_trail - update
    return (norm_out, trail_out)


def solution(mesh):
    return jax.shard_map(
        shards,
        mesh=mesh,
        in_specs=(P("row", None), P("row", "col"), P("row", "col"), P("row", "col"), P("col")),
        out_specs=(P("col"), P("row", "col")),
        check_vma=False,
    )
```

profile of v0, /device:TPU:0, one launch (start us, length us, event | category | flops | bytes accessed | tf_op | source)
XLA Modules:
  0.0 1010.4 jit_solution(6532698303589509608)
XLA Ops:
  8.0 2.5 broadcast_in_dim.3
  10.6 822.3 %while.20 = (s32[]{:T(128)}, f32[2048,512]{1,0:T(8,128)}, f32[256,512]{1,0:T(8,128)S(1)}, s32[]{:T(128)}, f32[256,2048]{1,0:T(8,128)}, /*index=5*/f32[256,512]{1...) while((s32[]{:T(128)}, f32[2048,512]{1,0:T(8,128)}, ...), condition=%wide.region_2.3_spmd.clone, body=%wide.region_0.2_spmd.clone.sunk | while | flops 705953792 | bytes 11338146 | solution.py:34
  10.6 1.0 fusion.31
  11.7 3.9 while.21
  12.3 1.3 bitcast_dynamic-update-slice_fusion.2
  14.2 1.3 bitcast_dynamic-update-slice_fusion.2
  15.6 19.7 %custom-call.13 = f32[2,128,128]{1,2,0:T(8,128)S(1)} custom-call(f32[2,128,128]{2,1,0:T(8,128)S(1)} %get-tuple-element.252), custom_call_target="InvertDiagBlocksLowerTriangular" | custom-call | tf_op jit(solution)/shard_map/while/body/eval_jaxpr/triangular_solve | solution.py:21
  37.5 75.3 %all-reduce.2.cloned.1.call-done = f32[256,512]{1,0:T(8,128)} async-done(((f32[256,512]{1,0:T(8,128)}), f32[256,512]{1,0:T(8,128)}) %all-reduce.2.cloned.1.call-update) | async-done | bytes 524304 | tf_op jit(solution)/shard_map/while/body/eval_jaxpr/psum | solution.py:25
  112.7 1.8 convolution_add_fusion.2
  114.5 1.9 constant_dynamic-update-slice_fusion.2
  117.5 3.9 while.21
  118.1 1.3 bitcast_dynamic-update-slice_fusion.2
  120.0 1.3 bitcast_dynamic-update-slice_fusion.2
  121.4 19.7 %custom-call.13 = f32[2,128,128]{1,2,0:T(8,128)S(1)} custom-call(f32[2,128,128]{2,1,0:T(8,128)S(1)} %get-tuple-element.252), custom_call_target="InvertDiagBlocksLowerTriangular" | custom-call | tf_op jit(solution)/shard_map/while/body/eval_jaxpr/triangular_solve | solution.py:21
  143.3 71.8 %all-reduce.2.cloned.1.call-done = f32[256,512]{1,0:T(8,128)} async-done(((f32[256,512]{1,0:T(8,128)}), f32[256,512]{1,0:T(8,128)}) %all-reduce.2.cloned.1.call-update) | async-done | bytes 524304 | tf_op jit(solution)/shard_map/while/body/eval_jaxpr/psum | solution.py:25
  215.1 1.8 convolution_add_fusion.2
  216.9 1.9 constant_dynamic-update-slice_fusion.2
  219.8 3.9 while.21
  220.4 1.3 bitcast_dynamic-update-slice_fusion.2
  222.4 1.3 bitcast_dynamic-update-slice_fusion.2
  223.8 19.7 %custom-call.13 = f32[2,128,128]{1,2,0:T(8,128)S(1)} custom-call(f32[2,128,128]{2,1,0:T(8,128)S(1)} %get-tuple-element.252), custom_call_target="InvertDiagBlocksLowerTriangular" | custom-call | tf_op jit(solution)/shard_map/while/body/eval_jaxpr/triangular_solve | solution.py:21
  245.6 71.8 %all-reduce.2.cloned.1.call-done = f32[256,512]{1,0:T(8,128)} async-done(((f32[256,512]{1,0:T(8,128)}), f32[256,512]{1,0:T(8,128)}) %all-reduce.2.cloned.1.call-update) | async-done | bytes 524304 | tf_op jit(solution)/shard_map/while/body/eval_jaxpr/psum | solution.py:25
  317.4 1.8 convolution_add_fusion.2
  319.2 1.9 constant_dynamic-update-slice_fusion.2
  322.2 3.9 while.21
  322.8 1.3 bitcast_dynamic-update-slice_fusion.2
  324.8 1.3 bitcast_dynamic-update-slice_fusion.2
  326.1 19.7 %custom-call.13 = f32[2,128,128]{1,2,0:T(8,128)S(1)} custom-call(f32[2,128,128]{2,1,0:T(8,128)S(1)} %get-tuple-element.252), custom_call_target="InvertDiagBlocksLowerTriangular" | custom-call | tf_op jit(solution)/shard_map/while/body/eval_jaxpr/triangular_solve | solution.py:21
  348.0 71.8 %all-reduce.2.cloned.1.call-done = f32[256,512]{1,0:T(8,128)} async-done(((f32[256,512]{1,0:T(8,128)}), f32[256,512]{1,0:T(8,128)}) %all-reduce.2.cloned.1.call-update) | async-done | bytes 524304 | tf_op jit(solution)/shard_map/while/body/eval_jaxpr/psum | solution.py:25
  419.8 1.8 convolution_add_fusion.2
  421.6 1.9 constant_dynamic-update-slice_fusion.2
  424.5 3.9 while.21
  425.1 1.3 bitcast_dynamic-update-slice_fusion.2
  427.1 1.3 bitcast_dynamic-update-slice_fusion.2
  428.4 19.7 %custom-call.13 = f32[2,128,128]{1,2,0:T(8,128)S(1)} custom-call(f32[2,128,128]{2,1,0:T(8,128)S(1)} %get-tuple-element.252), custom_call_target="InvertDiagBlocksLowerTriangular" | custom-call | tf_op jit(solution)/shard_map/while/body/eval_jaxpr/triangular_solve | solution.py:21
  450.3 71.8 %all-reduce.2.cloned.1.call-done = f32[256,512]{1,0:T(8,128)} async-done(((f32[256,512]{1,0:T(8,128)}), f32[256,512]{1,0:T(8,128)}) %all-reduce.2.cloned.1.call-update) | async-done | bytes 524304 | tf_op jit(solution)/shard_map/while/body/eval_jaxpr/psum | solution.py:25
  522.1 1.8 convolution_add_fusion.2
  523.9 1.9 constant_dynamic-update-slice_fusion.2
  526.8 3.9 while.21
  527.4 1.3 bitcast_dynamic-update-slice_fusion.2
  529.4 1.3 bitcast_dynamic-update-slice_fusion.2
  530.8 19.7 %custom-call.13 = f32[2,128,128]{1,2,0:T(8,128)S(1)} custom-call(f32[2,128,128]{2,1,0:T(8,128)S(1)} %get-tuple-element.252), custom_call_target="InvertDiagBlocksLowerTriangular" | custom-call | tf_op jit(solution)/shard_map/while/body/eval_jaxpr/triangular_solve | solution.py:21
  552.6 71.8 %all-reduce.2.cloned.1.call-done = f32[256,512]{1,0:T(8,128)} async-done(((f32[256,512]{1,0:T(8,128)}), f32[256,512]{1,0:T(8,128)}) %all-reduce.2.cloned.1.call-update) | async-done | bytes 524304 | tf_op jit(solution)/shard_map/while/body/eval_jaxpr/psum | solution.py:25
  624.4 1.8 convolution_add_fusion.2
  626.2 1.9 constant_dynamic-update-slice_fusion.2
  629.2 3.9 while.21
  629.8 1.3 bitcast_dynamic-update-slice_fusion.2
  631.8 1.3 bitcast_dynamic-update-slice_fusion.2
  633.1 19.7 %custom-call.13 = f32[2,128,128]{1,2,0:T(8,128)S(1)} custom-call(f32[2,128,128]{2,1,0:T(8,128)S(1)} %get-tuple-element.252), custom_call_target="InvertDiagBlocksLowerTriangular" | custom-call | tf_op jit(solution)/shard_map/while/body/eval_jaxpr/triangular_solve | solution.py:21
  655.0 71.8 %all-reduce.2.cloned.1.call-done = f32[256,512]{1,0:T(8,128)} async-done(((f32[256,512]{1,0:T(8,128)}), f32[256,512]{1,0:T(8,128)}) %all-reduce.2.cloned.1.call-update) | async-done | bytes 524304 | tf_op jit(solution)/shard_map/while/body/eval_jaxpr/psum | solution.py:25
  726.8 1.8 convolution_add_fusion.2
  728.6 1.9 constant_dynamic-update-slice_fusion.2
  731.6 3.9 while.21
  732.2 1.3 bitcast_dynamic-update-slice_fusion.2
  734.1 1.3 bitcast_dynamic-update-slice_fusion.2
  735.5 19.7 %custom-call.13 = f32[2,128,128]{1,2,0:T(8,128)S(1)} custom-call(f32[2,128,128]{2,1,0:T(8,128)S(1)} %get-tuple-element.252), custom_call_target="InvertDiagBlocksLowerTriangular" | custom-call | tf_op jit(solution)/shard_map/while/body/eval_jaxpr/triangular_solve | solution.py:21
  757.4 71.8 %all-reduce.2.cloned.1.call-done = f32[256,512]{1,0:T(8,128)} async-done(((f32[256,512]{1,0:T(8,128)}), f32[256,512]{1,0:T(8,128)}) %all-reduce.2.cloned.1.call-update) | async-done | bytes 524304 | tf_op jit(solution)/shard_map/while/body/eval_jaxpr/psum | solution.py:25
  829.2 1.8 convolution_add_fusion.2
  831.0 1.9 constant_dynamic-update-slice_fusion.2
  833.4 5.5 copy.7
  838.9 3.2 multiply_reduce_fusion
  842.7 97.3 %all-gather.2.cloned.1.call-done = f32[2048,2048]{1,0:T(8,128)} async-done(((f32[2048,512]{1,0:T(8,128)}), f32[2048,2048]{1,0:T(8,128)}) %all-gather.2.cloned.1.call-update) | async-done | bytes 16777232 | tf_op jit(solution)/shard_map/all_gather | solution.py:37
  939.9 57.7 %bitcast_subtract_fusion = f32[2048,512]{0,1:T(8,128)} fusion(f32[2048,512]{0,1:T(8,128)} %copy.7, f32[2048,512]{1,0:T(8,128)} %get-tuple-element.126, f32[2048,2048]{1,0:T(8,128)} %all-gather.2.cloned.1.call-done), kind=kOutput, calls=%fused_computation.21 | convolution fusion | flops 25770852352 | bytes 29360128 | tf_op jit(solution)/shard_map/dot_general | solution.py:36
  997.6 5.3 copy.8
  (127 shorter events, 35.5 us)
Async XLA Ops:
  8.0 2.6 copy-start
  10.6 102.1 %all-reduce.2.cloned.1.call-start = ((), (), s32[]{:S(2)}) async-start(), calls=%async_computation.1 | async-start | bytes 1048576 | tf_op jit(solution)/shard_map/while/body/eval_jaxpr/psum | solution.py:25
  116.4 98.7 %all-reduce.2.cloned.1.call-start = ((), (), s32[]{:S(2)}) async-start(), calls=%async_computation.1 | async-start | bytes 1048576 | tf_op jit(solution)/shard_map/while/body/eval_jaxpr/psum | solution.py:25
  218.8 98.7 %all-reduce.2.cloned.1.call-start = ((), (), s32[]{:S(2)}) async-start(), calls=%async_computation.1 | async-start | bytes 1048576 | tf_op jit(solution)/shard_map/while/body/eval_jaxpr/psum | solution.py:25
  321.1 98.7 %all-reduce.2.cloned.1.call-start = ((), (), s32[]{:S(2)}) async-start(), calls=%async_computation.1 | async-start | bytes 1048576 | tf_op jit(solution)/shard_map/while/body/eval_jaxpr/psum | solution.py:25
  423.5 98.6 %all-reduce.2.cloned.1.call-start = ((), (), s32[]{:S(2)}) async-start(), calls=%async_computation.1 | async-start | bytes 1048576 | tf_op jit(solution)/shard_map/while/body/eval_jaxpr/psum | solution.py:25
  525.8 98.7 %all-reduce.2.cloned.1.call-start = ((), (), s32[]{:S(2)}) async-start(), calls=%async_computation.1 | async-start | bytes 1048576 | tf_op jit(solution)/shard_map/while/body/eval_jaxpr/psum | solution.py:25
  628.1 98.7 %all-reduce.2.cloned.1.call-start = ((), (), s32[]{:S(2)}) async-start(), calls=%async_computation.1 | async-start | bytes 1048576 | tf_op jit(solution)/shard_map/while/body/eval_jaxpr/psum | solution.py:25
  730.5 98.7 %all-reduce.2.cloned.1.call-start = ((), (), s32[]{:S(2)}) async-start(), calls=%async_computation.1 | async-start | bytes 1048576 | tf_op jit(solution)/shard_map/while/body/eval_jaxpr/psum | solution.py:25
  832.9 107.1 %all-gather.2.cloned.1.call-start = ((), (), s32[]{:S(2)}) async-start(), calls=%async_computation | async-start | bytes 20971520 | tf_op jit(solution)/shard_map/all_gather | solution.py:37
  838.9 3.2 copy-start.1
Sparse Core Ops, SparseCore 0:
  37.6 75.1 all-reduce.1
  143.4 71.6 all-reduce.1
  245.7 71.6 all-reduce.1
  348.1 71.6 all-reduce.1
  450.4 71.6 all-reduce.1
  552.8 71.6 all-reduce.1
  655.1 71.6 all-reduce.1
  757.5 71.6 all-reduce.1
Sparse Core Ops, SparseCore 1:
  834.9 105.0 all-gather.1
where the time goes:
time: 1010 us
  waiting for transfers between devices  676 us (67%)
  other arithmetic  176 us (17%)
  matrix products  81.8 us (8%)
  local copies, waits for them, and re-layouts  60 us (6%)
  between operations  15.5 us (2%)
    psum x8, waiting for transfers between devices, advance(): received = lax.psum(masked, 'row')  578 us
    another operation x24, other arithmetic, advance(): lax.linalg.triangular_solve(pivot_tile, z_panel - carried, left_side=True...  165 us
    all_gather x1, waiting for transfers between devices, shards(): lax.all_gather(panel_below, 'col', axis=1, tiled=True)  97.3 us
    dot_general x1, matrix products, shards(): jnp.dot(lax.all_gather(panel_below, 'col', axis=1, tiled=True), solved, p...  57.7 us
    another operation x48, local copies, waits for them, and re-layouts  31.1 us
  transfers between devices with their start and end apart: 9, of which 9 were waited for; matrix products, arithmetic and copies ran while one was open for 1% of the time, Pallas kernels for 0%

commit v1 on v0

v1 whole, which is shorter than its diff:
```python
import jax
import jax.numpy as jnp
from jax import lax
from jax.experimental import pallas as pl
from jax.experimental.pallas import tpu as pltpu
from jax.sharding import PartitionSpec as P

F32 = jnp.float32
BF16 = jnp.bfloat16
HIGHEST = lax.Precision.HIGHEST
CHUNKS = 2
ROW_PIECES = (4, 4, 4, 2, 2)
ANY = pl.BlockSpec(memory_space=pl.ANY)
VMEM = pl.BlockSpec(memory_space=pltpu.VMEM)
LIMIT = 48 * 1024 * 1024


def params(**more):
    return pltpu.CompilerParams(vmem_limit_bytes=LIMIT, **more)


def mul(a, b):
    return jnp.dot(a, b, precision=HIGHEST, preferred_element_type=F32)


def mul_t(a, b):
    return lax.dot_general(
        a, b, (((1,), (1,)), ((), ())), precision=HIGHEST, preferred_element_type=F32
    )


def level_and_half():
    own_row = lax.axis_index("row")
    return own_row // 2, own_row % 2


def run_copies(pairs, sems):
    copies = [pltpu.make_async_copy(s, d, sems.at[i]) for i, (s, d) in enumerate(pairs)]
    for copy in copies:
        copy.start()
    for copy in copies:
        copy.wait()


def stage_kernel(z_ref, diag_ref, own_ref, send_ref, corner_ref, sems):
    level, half = level_and_half()
    size = z_ref.shape[0]
    start = pl.multiple_of(level * 2 * size, 2 * size)
    copy = pltpu.make_async_copy(diag_ref.at[:, pl.ds(start, size)], corner_ref, sems.at[0])
    copy.start()
    width = z_ref.shape[1] // 2
    flipped = z_ref[...].T
    low, high = flipped[:width], flipped[width:]
    own_ref[...] = jnp.where(half == 0, low, high)
    send_ref[...] = jnp.where(half == 0, high, low)
    copy.wait()


def inverse_of(tri):
    size = tri.shape[0]
    base = 16
    count = size // base
    rows = lax.broadcasted_iota(jnp.int32, (size, size), 0)
    cols = lax.broadcasted_iota(jnp.int32, (size, size), 1)
    same = (rows // base) == (cols // base)
    folded = jnp.sum(jnp.where(same, tri, 0.0).reshape(count, base, size), axis=0)
    lane = lax.broadcasted_iota(jnp.int32, (base, size), 1) % base
    line = lax.broadcasted_iota(jnp.int32, (base, size), 0)
    spread = jnp.concatenate([jnp.where(lane == k, folded, 0.0) for k in range(base)], axis=0)
    spread = mul(spread, jnp.where(same, 1.0, 0.0))
    rest = jnp.where(lane == line, 1.0, 0.0)
    done = jnp.zeros((base, size), F32)
    for k in range(base):
        column = spread[k * base:(k + 1) * base]
        solved = rest[k:k + 1] / column[k:k + 1]
        done = jnp.where(line == k, solved, done)
        rest = rest - jnp.where(line > k, column, 0.0) * solved
    full = jnp.where(same, jnp.concatenate([done] * count, axis=0), 0.0)
    step = base
    while step < size:
        pair = (rows // (2 * step)) == (cols // (2 * step))
        below = ((rows // step) % 2 == 1) & ((cols // step) % 2 == 0)
        off = jnp.where(pair & below, tri, 0.0)
        full = full - mul(full, mul(off, full))
        step *= 2
    return full


def inverse_kernel(levels, diag_ref, inv_ref, near_ref, far_ref, tile_ref, sems):
    own_row = lax.axis_index("row")
    level, _ = level_and_half()
    size = tile_ref.shape[0]
    width = 2 * size
    strip = size // 2
    core = lax.axis_index("col") % 2
    lines = pl.ds(pl.multiple_of(core * strip, strip), strip)
    pairs = [(diag_ref.at[:, pl.ds(pl.multiple_of(own_row * size, size), size)], tile_ref)]
    for d in range(1, levels):
        block = jnp.maximum(level - d, 0)
        source = diag_ref.at[lines, pl.ds(pl.multiple_of(block * width, width), width)]
        target = near_ref if d == 1 else far_ref.at[:, pl.ds((d - 2) * width, width)]
        pairs.append((source, target))
    copies = [pltpu.make_async_copy(s, t, sems.at[i]) for i, (s, t) in enumerate(pairs)]
    for copy in copies:
        copy.start()
    copies[0].wait()
    inv_ref[...] = inverse_of(tile_ref[...])
    for copy in copies[1:]:
        copy.wait()


def solve_kernel(turn, chunks, depths, *refs):
    (z_own, z_other, inv_own, inv_other, corner_own, corner_other, diag,
     near_a, near_b, far_a, far_b) = refs[:11]
    ups = dict(zip(depths, refs[11:]))
    out, rest, tiles, low, low_other, came, sems = refs[11 + len(depths):]
    level, half = level_and_half()
    core = lax.axis_index("col") % 2
    part, size = rest.shape[1:]
    width = 2 * size
    strip = size // 2
    chunk = turn - level

    @pl.when((chunk >= 0) & (chunk < chunks))
    def _():
        lines = pl.ds(pl.multiple_of(chunk * part, part), part)
        first = [
            (z_own.at[lines], rest.at[0]),
            (z_other.at[lines], rest.at[1]),
            (inv_own, tiles.at[0]),
            (inv_other, tiles.at[1]),
        ]
        first = [pltpu.make_async_copy(s, t, sems.at[i]) for i, (s, t) in enumerate(first)]
        own_corner = pltpu.make_async_copy(corner_own, tiles.at[2], sems.at[4])
        other_corner = pltpu.make_async_copy(corner_other, tiles.at[2], sems.at[4])
        for copy in first:
            copy.start()

        @pl.when(half == 1)
        def _():
            own_corner.start()

        @pl.when(half == 0)
        def _():
            other_corner.start()

        later = {}
        for d in depths:
            block = jnp.maximum(level - d, 0)
            spot = pl.ds((d - 1) * width, width)
            here = pl.ds(pl.multiple_of(core * strip, strip), strip)
            there = pl.ds(pl.multiple_of((1 - core) * strip, strip), strip)
            side_a = near_a if d == 1 else far_a.at[:, pl.ds((d - 2) * width, width)]
            side_b = near_b if d == 1 else far_b.at[:, pl.ds((d - 2) * width, width)]
            pairs = [
                (ups[d], came.at[d - 1]),
                (diag.at[:, pl.ds(pl.multiple_of(block * width, width), width)], low.at[:, spot]),
                (side_a, low_other.at[here, spot]),
                (side_b, low_other.at[there, spot]),
            ]
            later[d] = [
                pltpu.make_async_copy(s, t, sems.at[5 + 4 * (d - 1) + i])
                for i, (s, t) in enumerate(pairs)
            ]

            @pl.when(level >= d)
            def _(d=d):
                for copy in later[d]:
                    copy.start()

        for copy in first:
            copy.wait()
        own_corner.wait()
        for d in reversed(depths):
            @pl.when(level >= d)
            def _(d=d):
                for copy in later[d]:
                    copy.wait()
                spot = pl.ds((d - 1) * width, width)
                rest[0] -= mul_t(came[d - 1], low[:, spot])
                rest[1] -= mul_t(came[d - 1], low_other[:, spot])

        upper = half == 0
        top = mul_t(
            jnp.where(upper, rest[0], rest[1]), jnp.where(upper, tiles[0], tiles[1])
        )
        bottom = jnp.where(upper, rest[1], rest[0]) - mul_t(top, tiles[2])
        out[:, :size] = top
        out[:, size:] = mul_t(bottom, jnp.where(upper, tiles[1], tiles[0]))


def pack_kernel(plan, width, *refs):
    out, sems = refs[-2:]
    level, _ = level_and_half()
    for phase in (0, 1):
        for slot, choices in enumerate(plan):
            target = out.at[:, pl.ds(slot * width, width)]
            for want, index in choices:
                copy = pltpu.make_async_copy(refs[index], target, sems.at[slot])

                @pl.when(level == want)
                def _(copy=copy):
                    copy.start() if phase == 0 else copy.wait()


def finish_kernel(chunks, slots, *refs):
    ins = refs[:4 * chunks]
    norm, high, low, norm_out, lines, sems = refs[4 * chunks:]
    _, half = level_and_half()
    wide = lines.shape[0]
    part = wide // 2 // chunks
    short = ins[0].shape[1]
    copies = []
    for j in range(chunks):
        for side in (0, 1):
            place = jnp.where(half == side, 0, 1) * (wide // 2) + j * part
            spot = pl.ds(pl.multiple_of(place, part), part)
            for piece, columns in ((0, pl.ds(0, short)), (1, pl.ds(short, lines.shape[1] - short))):
                copies.append(pltpu.make_async_copy(
                    ins[4 * j + 2 * side + piece], lines.at[spot, columns], sems.at[len(copies)]))
    for copy in copies:
        copy.start()
    for copy in copies:
        copy.wait()
    total = norm[...]
    depth = high.shape[0] // slots
    for k in range(slots):
        block = lines[:, k * depth:(k + 1) * depth].T
        coarse = block.astype(BF16)
        high[k * depth:(k + 1) * depth] = coarse
        low[k * depth:(k + 1) * depth] = (block - coarse.astype(F32)).astype(BF16)
        total = total + jnp.sum(block * block, axis=0, keepdims=True)
    norm_out[...] = total


def trail_kernel(flips, *refs):
    parts = refs[:len(flips)]
    z_ref, high, low = refs[len(flips):len(flips) + 3]
    out = refs[-1]
    own_col = lax.axis_index("col")
    total = z_ref[...]
    for flip, part in zip(flips, parts):
        depth = part.shape[1]
        lines = pl.ds(pl.multiple_of(lax.bitwise_xor(own_col, flip) * depth, depth), depth)
        value = part[...]
        coarse = value.astype(BF16)
        fine = (value - coarse.astype(F32)).astype(BF16)
        high_lines = high[lines, :]
        total = total - jnp.dot(coarse, high_lines, preferred_element_type=F32)
        total = total - jnp.dot(coarse, low[lines, :], preferred_element_type=F32)
        total = total - jnp.dot(fine, high_lines, preferred_element_type=F32)
    out[...] = total


def tie_kernel(x_ref, token_ref, out_ref):
    del x_ref, token_ref, out_ref


def tie(x, token):
    return pl.pallas_call(
        tie_kernel,
        out_shape=jax.ShapeDtypeStruct(x.shape, x.dtype),
        in_specs=[ANY, ANY],
        out_specs=ANY,
        input_output_aliases={0: 0},
    )(x, token)


def struct(*shape, dtype=F32):
    return jax.ShapeDtypeStruct(shape, dtype)


def forward_substitution(diag_block, z_panel, norm_sq):
    rows = lax.axis_size("row")
    levels = rows // 2
    cols = lax.axis_size("col")
    size, full = diag_block.shape
    wide = z_panel.shape[1]
    width, half_wide, strip = 2 * size, wide // 2, size // 2
    part = half_wide // CHUNKS
    dma = pltpu.SemaphoreType.DMA

    swap = [(i, i ^ 1) for i in range(rows)]
    cores = [(i, i ^ 1) for i in range(cols)]

    z_own, z_send, corner = pl.pallas_call(
        stage_kernel,
        out_shape=(struct(half_wide, size), struct(half_wide, size), struct(size, size)),
        in_specs=[VMEM, ANY],
        out_specs=(VMEM, VMEM, ANY),
        scratch_shapes=[dma((1,))],
        compiler_params=params(),
    )(z_panel, diag_block)
    z_other = lax.ppermute(z_send, "row", swap)
    corner_other = lax.ppermute(corner, "row", [p for p in swap if p[0] % 2 == 1])
    inv, near, far = pl.pallas_call(
        lambda *refs: inverse_kernel(levels, *refs),
        out_shape=(struct(size, size), struct(strip, width), struct(strip, width * (levels - 2))),
        in_specs=[ANY],
        out_specs=(VMEM, ANY, ANY),
        scratch_shapes=[pltpu.VMEM((size, size), F32), dma((levels,))],
        compiler_params=params(),
    )(diag_block)
    inv_other = lax.ppermute(inv, "row", swap)
    near_a = lax.ppermute(near, "row", [p for p in swap if p[0] >= 2])
    near_b = lax.ppermute(near_a, "col", cores)
    far_a = lax.ppermute(far, "row", [p for p in swap if p[0] >= 4])
    far_b = lax.ppermute(far_a, "col", cores)

    solved, ups, downs = {}, {}, {}
    for turn in range(levels - 1 + CHUNKS):
        depths = [d for d in range(1, levels) if (d, turn - d) in ups]
        args = [z_own, z_other, inv, inv_other, corner, corner_other, diag_block,
                near_a, near_b, far_a, far_b] + [ups[d, turn - d] for d in depths]
        deep = max(depths, default=1)
        solved[turn] = pl.pallas_call(
            lambda *refs, turn=turn, depths=depths: solve_kernel(turn, CHUNKS, depths, *refs),
            out_shape=struct(part, width),
            in_specs=[ANY] * len(args),
            out_specs=VMEM,
            scratch_shapes=[
                pltpu.VMEM((2, part, size), F32),
                pltpu.VMEM((3, size, size), F32),
                pltpu.VMEM((size, deep * width), F32),
                pltpu.VMEM((size, deep * width), F32),
                pltpu.VMEM((deep, part, width), F32),
                dma((5 + 4 * deep,)),
            ],
            compiler_params=params(),
        )(*args)
        busy = [z for z in range(levels) if 0 <= turn - z < CHUNKS]
        for d in range(1, levels):
            up = [(2 * z + y, 2 * (z + d) + y) for z in busy for y in (0, 1) if z + d < levels]
            down = [(2 * z + y, 2 * (z - d) + y) for z in busy for y in (0, 1) if z - d >= 0]
            if up:
                ups[d, turn] = lax.ppermute(solved[turn], "row", up)
            if down:
                downs[d, turn] = lax.ppermute(solved[turn], "row", down)

    def pack(chunk, wanted):
        args, plan = [], []
        for level in wanted:
            turn = level + chunk
            choices = [(level, len(args))]
            args.append(solved[turn])
            for z in range(levels):
                if z != level:
                    choices.append((z, len(args)))
                    args.append(ups[z - level, turn] if z > level else downs[level - z, turn])
            plan.append(choices)
        return pl.pallas_call(
            lambda *refs: pack_kernel(plan, width, *refs),
            out_shape=struct(part, width * len(wanted)),
            in_specs=[ANY] * len(args),
            out_specs=ANY,
            scratch_shapes=[dma((len(wanted),))],
            compiler_params=params(),
        )(*args)

    ready = []
    for chunk in range(CHUNKS):
        early = pack(chunk, range(levels - 1))
        last = pack(chunk, [levels - 1])
        ready += [early, last, lax.ppermute(early, "row", swap), lax.ppermute(last, "row", swap)]

    high, low, norm_out = pl.pallas_call(
        lambda *refs: finish_kernel(CHUNKS, levels, *refs),
        out_shape=(struct(full, wide, dtype=BF16), struct(full, wide, dtype=BF16), struct(1, wide)),
        in_specs=[ANY] * len(ready) + [VMEM],
        out_specs=(VMEM, VMEM, VMEM),
        scratch_shapes=[pltpu.VMEM((wide, full), F32), dma((len(ready),))],
        compiler_params=params(),
    )(*ready, norm_sq.reshape(1, wide))
    return high, low, norm_out.reshape(wide), solved[levels - 2 + CHUNKS]


def trailing(out, piece_start, piece_rows, panels, pieces, z_trail, high, low):
    rows, wide = z_trail.shape
    depth = high.shape[0]
    tile = min(256, piece_rows)
    skip = piece_start // tile
    flips = [flip for flip, _ in panels] + [flip for flip, _ in pieces]
    args = [x for _, x in panels] + [x for _, x in pieces]
    in_specs = [pl.BlockSpec((tile, x.shape[1]), lambda i: (i + skip, 0)) for _, x in panels]
    in_specs += [pl.BlockSpec((tile, x.shape[1]), lambda i: (i, 0)) for _, x in pieces]
    in_specs += [pl.BlockSpec((tile, wide), lambda i: (i + skip, 0))]
    in_specs += [pl.BlockSpec((depth, wide), lambda i: (0, 0))] * 2
    args += [z_trail, high, low]
    aliases = {}
    if out is not None:
        aliases = {len(args): 0}
        args.append(out)
        in_specs.append(ANY)
    return pl.pallas_call(
        lambda *refs: trail_kernel(flips, *refs),
        grid=(piece_rows // tile,),
        out_shape=struct(rows, wide),
        in_specs=in_specs,
        out_specs=pl.BlockSpec((tile, wide), lambda i: (i + skip, 0)),
        input_output_aliases=aliases,
        compiler_params=params(),
        cost_estimate=pl.CostEstimate(
            flops=6 * piece_rows * depth * wide,
            bytes_accessed=4 * piece_rows * (depth + 2 * wide),
            transcendentals=0,
        ),
    )(*args)


def shards(diag_block, z_panel, panel_below, z_trail, norm_sq):
    cols = lax.axis_size("col")
    height = panel_below.shape[0]
    unit = height // sum(ROW_PIECES)
    bounds = []
    start = 0
    for count in ROW_PIECES:
        bounds.append((start, count * unit))
        start += count * unit

    def flipped(x, flip):
        return lax.ppermute(x, "col", [(i, i ^ flip) for i in range(cols)])

    crossed = [
        [(flip, flipped(panel_below[s:s + n], flip)) for flip in range(2, cols, 2)]
        for s, n in bounds
    ]
    mate = flipped(panel_below, 1)
    high, low, norm_out, token = forward_substitution(diag_block, z_panel, norm_sq)
    panels = [(0, panel_below), (1, mate)]
    out = None
    pieces = []
    for index, piece in enumerate(crossed):
        hold = high if index == len(crossed) - 1 else token
        piece = [(flip, tie(x, hold)) for flip, x in piece]
        pieces.append(piece + [(flip ^ 1, flipped(x, 1)) for flip, x in piece])
    for (s, n), piece in zip(bounds, pieces):
        out = trailing(out, s, n, panels, piece, z_trail, high, low)
    return (norm_out, out)


def solution(mesh):
    return jax.shard_map(
        shards,
        mesh=mesh,
        in_specs=(P("row", None), P("row", "col"), P("row", "col"), P("row", "col"), P("col")),
        out_specs=(P("col"), P("row", "col")),
        check_vma=False,
    )
```

time: 1010 us -> 266 us (0.26)
  waiting for transfers between devices: 676 us -> 120 us
  other arithmetic: 176 us -> 0 us
  starting transfers between devices: 0.02 us -> 82.7 us
  matrix products: 81.8 us -> 0 us
  local copies, waits for them, and re-layouts: 60 us -> 14.1 us
  Pallas kernels: 0 us -> 44.7 us
  between operations: 15.5 us -> 1.18 us
    psum x8 -> x0, waiting for transfers between devices: 578 us -> none  [advance(): received = lax.psum(masked, 'row')]
    another operation x24 -> x0, other arithmetic: 165 us -> none  [advance(): lax.linalg.triangular_solve(pivot_tile, z_panel - carried, left_side=True...]
    ppermute x0 -> x40, waiting for transfers between devices: none -> 120 us  [the longest x9 37 us: forward_substitution(): downs[d, turn] = lax.ppermute(solved[turn], 'row', down)]
    all_gather x1 -> x0, waiting for transfers between devices: 97.3 us -> none  [shards(): lax.all_gather(panel_below, 'col', axis=1, tiled=True)]
    ppermute x0 -> x40, starting transfers between devices: none -> 82.7 us  [the longest x9 51.1 us: forward_substitution(): ups[d, turn] = lax.ppermute(solved[turn], 'row', up)]
    dot_general x9 -> x0, matrix products: 72 us -> none  [the longest x1 57.7 us: shards(): jnp.dot(lax.all_gather(panel_below, 'col', axis=1, tiled=True), solved, p...]
    pallas_call x0 -> x22, Pallas kernels: none -> 44.7 us  [the longest x5 30.1 us: trailing(): pl.pallas_call(lambda *refs: trail_kernel(flips, *refs), grid=(piece_rows...]
    another operation x56 -> x0, local copies, waits for them, and re-layouts: 31.6 us -> none
  transfers between devices with their start and end apart: 9 -> 40, of which waited for: 9 -> 15; matrix products, arithmetic and copies ran while one was open for 1% -> 2% of each run, Pallas kernels for 0% -> 14%
where the time goes in v1:
time: 266 us; the launch traced here: 263 us
  waiting for transfers between devices  120 us (45%)
  starting transfers between devices  82.7 us (31%)
  Pallas kernels  44.7 us (17%)
  local copies, waits for them, and re-layouts  14.1 us (5%)
    ppermute x9, starting transfers between devices, forward_substitution(): ups[d, turn] = lax.ppermute(solved[turn], 'row', up)  51.1 us
    ppermute x9, waiting for transfers between devices, forward_substitution(): downs[d, turn] = lax.ppermute(solved[turn], 'row', down)  37 us
    ppermute x2, waiting for transfers between devices, forward_substitution(): lax.ppermute(last, 'row', swap)  36.8 us
    pallas_call x5, Pallas kernels, trailing(): pl.pallas_call(lambda *refs: trail_kernel(flips, *refs), grid=(piece_rows...  30.1 us
    ppermute x11, waiting for transfers between devices, flipped(): return lax.ppermute(x, 'col', [(i, i ^ flip) for i in range(cols)])  30 us
    ppermute x9, waiting for transfers between devices, forward_substitution(): ups[d, turn] = lax.ppermute(solved[turn], 'row', up)  10.6 us
    ppermute x9, starting transfers between devices, forward_substitution(): downs[d, turn] = lax.ppermute(solved[turn], 'row', down)  10.4 us
    unnamed x42, local copies, waits for them, and re-layouts  9.91 us
  transfers between devices with their start and end apart: 40, of which 15 were waited for; matrix products, arithmetic and copies ran while one was open for 2% of the time, Pallas kernels for 14%

profile of v1, /device:TPU:0, one launch (start us, length us, event | category | flops | bytes accessed | tf_op | source)
XLA Modules:
  0.0 263.1 jit_solution(553726234773335874)
XLA Ops:
  0.6 1.6 copy-done
  2.2 4.8 %shard_map.69 = (f32[256,256]{1,0:T(8,128)S(1)}, f32[128,512]{1,0:T(8,128)S(1)}, f32[128,1024]{1,0:T(8,128)S(1)}) custom-call(f32[256,2048]{1,0:T(8,128)S(1)} %copy-done), custom_call_target="tpu_custom_call" | custom-call | tf_op jit(solution)/shard_map/pallas_call | solution.py:296
  7.0 0.7 collective-permute-start.5
  8.2 0.7 collective-permute-start.3
  8.9 2.6 collective-permute-start.1
  11.5 1.6 copy-done.1
  13.1 1.0 copy-done.15
  14.4 1.4 collective-permute-start.2
  16.1 2.2 fusion
  18.3 2.5 collective-permute-start
  20.8 1.5 collective-permute-start.38
  22.3 3.3 %collective-permute-done.2.refs_5_ = f32[256,256]{1,0:T(8,128)S(1)} collective-permute-done((f32[256,256]{1,0:T(8,128)S(1)}, f32[256,256]{1,0:T(8,128)S(1)}, u32[]{:S(2)}, u32[]{:S(2)}) %collective-permute-start.2) | collective-permute-done | bytes 262176 | tf_op jit(solution)/shard_map/ppermute | solution.py:295
  25.6 2.1 fusion.1
  27.7 2.8 %collective-permute-done.refs_1_ = f32[256,256]{1,0:T(8,128)S(1)} collective-permute-done((f32[256,256]{1,0:T(8,128)S(1)}, f32[256,256]{1,0:T(8,128)S(1)}, u32[]{:S(2)}, u32[]{:S(2)}) %collective-permute-start) | collective-permute-done | bytes 262176 | tf_op jit(solution)/shard_map/ppermute | solution.py:294
  30.5 1.5 collective-permute-start.32
  32.5 1.5 collective-permute-start.34
  34.0 1.8 shard_map.70.refs_0_
  35.8 22.4 %collective-permute-done.32.x_ref = f32[256,512]{1,0:T(8,128)} collective-permute-done((f32[256,512]{1,0:T(8,128)S(1)}, f32[256,512]{1,0:T(8,128)}, u32[]{:S(2)}, u32[]{:S(2)}) %collective-permute-start.32) | collective-permute-done | bytes 524320 | tf_op jit(solution)/shard_map/ppermute | solution.py:421
  58.2 8.6 %collective-permute-start.7 = (f32[128,512]{1,0:T(8,128)S(1)}, f32[128,512]{1,0:T(8,128)S(1)}, u32[]{:S(2)}, u32[]{:S(2)}) collective-permute-start(f32[128,512]{1,0:T(8,128)S(1)} %shard_map.70.refs_0_), channel_id=1, source_target_pairs={{0,8},{4,12},{1,9},{5,13},{2,10},{6,14},{3,11},{7,15}} | collective-permute-start | bytes 786440 | tf_op jit(solution)/shard_map/ppermute | solution.py:336
  66.8 3.9 %collective-permute-done.7.refs_11_.refs_1_ = f32[128,512]{1,0:T(8,128)S(1)} collective-permute-done((f32[128,512]{1,0:T(8,128)S(1)}, f32[128,512]{1,0:T(8,128)S(1)}, u32[]{:S(2)}, u32[]{:S(2)}) %collective-permute-start.7) | collective-permute-done | bytes 262176 | tf_op jit(solution)/shard_map/ppermute | solution.py:336
  70.7 8.4 %collective-permute-start.8 = (f32[128,512]{1,0:T(8,128)S(1)}, f32[128,512]{1,0:T(8,128)S(1)}, u32[]{:S(2)}, u32[]{:S(2)}) collective-permute-start(f32[128,512]{1,0:T(8,128)S(1)} %shard_map.70.refs_0_), channel_id=1, source_target_pairs={{0,16},{4,20},{1,17},{5,21},{2,18},{6,22},{3,19},{7,23}} | collective-permute-start | bytes 786440 | tf_op jit(solution)/shard_map/ppermute | solution.py:336
  79.0 1.9 shard_map.71.refs_4_.refs_0_
  80.9 1.3 collective-permute-start.11
  82.2 2.7 %collective-permute-done.8.refs_12_.refs_2_ = f32[128,512]{1,0:T(8,128)S(1)} collective-permute-done((f32[128,512]{1,0:T(8,128)S(1)}, f32[128,512]{1,0:T(8,128)S(1)}, u32[]{:S(2)}, u32[]{:S(2)}) %collective-permute-start.8) | collective-permute-done | bytes 262176 | tf_op jit(solution)/shard_map/ppermute | solution.py:336
  85.0 1.3 collective-permute-start.9
  86.3 3.8 %collective-permute-done.11.refs_11_.refs_6_.refs_1_ = f32[128,512]{1,0:T(8,128)S(1)} collective-permute-done((f32[128,512]{1,0:T(8,128)S(1)}, f32[128,512]{1,0:T(8,128)S(1)}, u32[]{:S(2)}, u32[]{:S(2)}) %collective-permute-start.11) | collective-permute-done | bytes 262176 | tf_op jit(solution)/shard_map/ppermute | solution.py:336
  90.1 10.8 %collective-permute-start.12 = (f32[128,512]{1,0:T(8,128)S(1)}, f32[128,512]{1,0:T(8,128)S(1)}, u32[]{:S(2)}, u32[]{:S(2)}) collective-permute-start(f32[128,512]{1,0:T(8,128)S(1)} %shard_map.71.refs_4_.refs_0_), channel_id=1, source_target_pairs={{0,16},{4,20},{8,24},{12,28},{1,17},{5,21},{9,25},{13,29},{2,18},{... | collective-permute-start | bytes 786440 | tf_op jit(solution)/shard_map/ppermute | solution.py:336
  101.0 0.7 collective-permute-start.15
  101.7 0.6 collective-permute-done.34.x_ref
  102.3 18.7 %collective-permute-start.21 = (f32[128,512]{1,0:T(8,128)S(1)}, f32[128,512]{1,0:T(8,128)S(1)}, u32[]{:S(2)}, u32[]{:S(2)}) collective-permute-start(f32[128,512]{1,0:T(8,128)S(1)} %shard_map.71.refs_4_.refs_0_), channel_id=1, source_target_pairs={{0,24},{4,28},{1,25},{5,29},{2,26},{6,30},{3,27},{7,31}} | collective-permute-start | bytes 786440 | tf_op jit(solution)/shard_map/ppermute | solution.py:336
  121.0 1.3 collective-permute-start.10
  122.3 0.7 collective-permute-start.22
  123.0 1.3 collective-permute-start.14
  124.9 0.7 collective-permute-start.23
  125.6 5.4 %collective-permute-done.10.refs_5_ = f32[128,512]{1,0:T(8,128)S(1)} collective-permute-done((f32[128,512]{1,0:T(8,128)S(1)}, f32[128,512]{1,0:T(8,128)S(1)}, u32[]{:S(2)}, u32[]{:S(2)}) %collective-permute-start.10) | collective-permute-done | bytes 262176 | tf_op jit(solution)/shard_map/ppermute | solution.py:338
  131.0 1.3 collective-permute-start.13
  132.3 1.3 collective-permute-start.17
  133.8 0.7 collective-permute-start.18
  134.5 1.3 collective-permute-start.16
  136.0 13.0 %collective-permute-done.13.refs_9_ = f32[128,512]{1,0:T(8,128)S(1)} collective-permute-done((f32[128,512]{1,0:T(8,128)S(1)}, f32[128,512]{1,0:T(8,128)S(1)}, u32[]{:S(2)}, u32[]{:S(2)}) %collective-permute-start.13) | collective-permute-done | bytes 262176 | tf_op jit(solution)/shard_map/ppermute | solution.py:338
  149.0 1.3 collective-permute-start.24
  150.3 18.4 %collective-permute-done.17.refs_2_.refs_9_ = f32[128,512]{1,0:T(8,128)S(1)} collective-permute-done((f32[128,512]{1,0:T(8,128)S(1)}, f32[128,512]{1,0:T(8,128)S(1)}, u32[]{:S(2)}, u32[]{:S(2)}) %collective-permute-start.17) | collective-permute-done | bytes 262176 | tf_op jit(solution)/shard_map/ppermute | solution.py:338
  168.6 0.7 collective-permute-start.25
  169.5 1.6 collective-permute-start.19
  171.1 1.4 collective-permute-start.26
  172.5 0.6 collective-permute-start.20
  173.2 0.7 copy-done.18
  173.9 1.5 collective-permute-start.27
  175.5 0.9 copy-done.6
  176.4 0.9 copy-done.17
  177.4 0.9 copy-done.19
  178.6 17.0 %collective-permute-done.20.refs_3_ = f32[128,512]{1,0:T(8,128)} collective-permute-done((f32[128,512]{1,0:T(8,128)S(1)}, f32[128,512]{1,0:T(8,128)}, u32[]{:S(2)}, u32[]{:S(2)}) %collective-permute-start.20) | collective-permute-done | bytes 262176 | tf_op jit(solution)/shard_map/ppermute | solution.py:364
  195.7 1.5 collective-permute-start.28
  197.2 19.7 %collective-permute-done.28.refs_7_ = f32[128,512]{1,0:T(8,128)S(1)} collective-permute-done((f32[128,512]{1,0:T(8,128)S(1)}, f32[128,512]{1,0:T(8,128)S(1)}, u32[]{:S(2)}, u32[]{:S(2)}) %collective-permute-start.28) | collective-permute-done | bytes 262176 | tf_op jit(solution)/shard_map/ppermute | solution.py:364
  217.0 0.9 copy-done.13
  217.8 1.5 collective-permute-start.30
  219.6 1.2 copy-done.14
  220.8 4.7 %shard_map.79 = (bf16[2048,512]{1,0:T(8,128)(2,1)}, bf16[2048,512]{1,0:T(8,128)(2,1)}, f32[1,512]{1,0:T(1,128)}) custom-call(f32[128,1536]{1,0:T(8,128)S(1)} %shard_map.73.refs_0_, f32[128,512]{1,0:T(8,128)S(1)} %shard_map.75.refs_1_, f32[128,1536]{1,0:T(8,128)S(1)} %copy-done.14, f32[128,512]{1,0:T(8,128)} %collective-permute-done.20.refs_3_, ...), custom_call_target="tpu_custom_call" | custom-call | tf_op jit(solution)/shard_map/pallas_call | solution.py:366
  225.5 7.0 %collective-permute-done.30.x_ref = f32[256,512]{1,0:T(8,128)} collective-permute-done((f32[256,512]{1,0:T(8,128)}, f32[256,512]{1,0:T(8,128)}, u32[]{:S(2)}, u32[]{:S(2)}) %collective-permute-start.30) | collective-permute-done | bytes 524320 | tf_op jit(solution)/shard_map/ppermute | solution.py:421
  233.0 7.1 %shard_map.85.refs_7_ = f32[2048,512]{1,0:T(8,128)} custom-call(f32[2048,512]{1,0:T(8,128)} %refs_0_.11, f32[2048,512]{1,0:T(8,128)} %collective-permute-done.29.refs_1_, f32[512,512]{1,0:T(8,128)S(1)} %copy-done.8, f32[512,512]{1,0:T(8,128)} %collective-permute-done.39.refs_3_, f32[2048,512]{1,0:T(8,128)} %refs_4_.9, bf16[2048,512]{1,0:T(8,128)(2,1)S(1)} %copy-done.3, ...), custom_call_target="tpu_custom_call" | custom-call | flops 3221225472 | bytes 6291456 | tf_op jit(solution)/shard_map/pallas_call | solution.py:394
  240.1 7.2 %shard_map.86.refs_7_ = f32[2048,512]{1,0:T(8,128)} custom-call(f32[2048,512]{1,0:T(8,128)} %refs_0_.11, f32[2048,512]{1,0:T(8,128)} %collective-permute-done.29.refs_1_, f32[512,512]{1,0:T(8,128)S(1)} %copy-done.12, f32[512,512]{1,0:T(8,128)} %collective-permute-done.37.refs_3_, f32[2048,512]{1,0:T(8,128)} %refs_4_.9, ...), custom_call_target="tpu_custom_call", output_to_operand_aliasing={{}: (7, {})} | custom-call | flops 3221225472 | bytes 6291456 | tf_op jit(solution)/shard_map/pallas_call | solution.py:394
  247.3 7.3 %shard_map.87.refs_7_ = f32[2048,512]{1,0:T(8,128)} custom-call(f32[2048,512]{1,0:T(8,128)} %refs_0_.11, f32[2048,512]{1,0:T(8,128)} %collective-permute-done.29.refs_1_, f32[512,512]{1,0:T(8,128)S(1)} %copy-done.10, f32[512,512]{1,0:T(8,128)} %collective-permute-done.35.refs_3_, f32[2048,512]{1,0:T(8,128)} %refs_4_.9, ...), custom_call_target="tpu_custom_call", output_to_operand_aliasing={{}: (7, {})} | custom-call | flops 3221225472 | bytes 6291456 | tf_op jit(solution)/shard_map/pallas_call | solution.py:394
  254.6 4.3 %shard_map.88.refs_7_ = f32[2048,512]{1,0:T(8,128)} custom-call(f32[2048,512]{1,0:T(8,128)} %refs_0_.11, f32[2048,512]{1,0:T(8,128)} %collective-permute-done.29.refs_1_, f32[256,512]{1,0:T(8,128)} %shard_map.81.refs_2_, f32[256,512]{1,0:T(8,128)} %collective-permute-done.33.refs_3_, f32[2048,512]{1,0:T(8,128)} %refs_4_.9, ...), custom_call_target="tpu_custom_call", output_to_operand_aliasing={{}: (7, {})} | custom-call | flops 1610612736 | bytes 3145728 | tf_op jit(solution)/shard_map/pallas_call | solution.py:394
  259.0 4.2 %shard_map.89 = f32[2048,512]{1,0:T(8,128)} custom-call(f32[2048,512]{1,0:T(8,128)} %refs_0_.11, f32[2048,512]{1,0:T(8,128)} %collective-permute-done.29.refs_1_, f32[256,512]{1,0:T(8,128)} %shard_map.80.refs_2_, f32[256,512]{1,0:T(8,128)S(1)} %collective-permute-done.31.refs_3_, f32[2048,512]{1,0:T(8,128)} %refs_4_.9, ...), custom_call_target="tpu_custom_call", output_to_operand_aliasing={{}: (7, {})} | custom-call | flops 1610612736 | bytes 3145728 | tf_op jit(solution)/shard_map/pallas_call | solution.py:394
  (82 shorter events, 4.2 us)
Async XLA Ops:
  0.6 1.6 copy-start
  7.0 8.8 %collective-permute-start.5 = (f32[128,1024]{1,0:T(8,128)S(1)}, f32[128,1024]{1,0:T(8,128)S(1)}, u32[]{:S(2)}, u32[]{:S(2)}) collective-permute-start(f32[128,1024]{1,0:T(8,128)S(1)} %get-tuple-element.16), channel_id=1, source_target_pairs={{16,20},{20,16},{24,28},{28,24},{17,21},{21,17},{25,29},{29,25},{1... | collective-permute-start | bytes 1572872 | tf_op jit(solution)/shard_map/ppermute | solution.py:307
  7.7 225.3 %collective-permute-start.29 = (f32[2048,512]{1,0:T(8,128)}, f32[2048,512]{1,0:T(8,128)}, u32[]{:S(2)}, u32[]{:S(2)}) collective-permute-start(f32[2048,512]{1,0:T(8,128)} %refs_0_.11), channel_id=1, source_target_pairs={{0,1},{1,0},{2,3},{3,2},{4,5},{5,4},{6,7},{7,6},{8,9},{9,8},{10,11... | collective-permute-start | bytes 12582920 | tf_op jit(solution)/shard_map/ppermute | solution.py:421
  8.2 10.0 %collective-permute-start.3 = (f32[128,512]{1,0:T(8,128)S(1)}, f32[128,512]{1,0:T(8,128)S(1)}, u32[]{:S(2)}, u32[]{:S(2)}) collective-permute-start(f32[128,512]{1,0:T(8,128)S(1)} %get-tuple-element.15), channel_id=1, source_target_pairs={{8,12},{12,8},{16,20},{20,16},{24,28},{28,24},{9,13},{13,9},{17,21... | collective-permute-start | bytes 786440 | tf_op jit(solution)/shard_map/ppermute | solution.py:305
  8.9 11.9 %collective-permute-start.1 = (f32[256,256]{1,0:T(8,128)S(1)}, f32[256,256]{1,0:T(8,128)S(1)}, u32[]{:S(2)}, u32[]{:S(2)}) collective-permute-start(f32[256,256]{1,0:T(8,128)S(1)} %get-tuple-element.13.refs_2_), channel_id=1, source_target_pairs={{0,4},{4,0},{8,12},{12,8},{16,20},{20,16},{24,28},{28,24},{1,5},{5... | collective-permute-start | bytes 786440 | tf_op jit(solution)/shard_map/ppermute | solution.py:304
  11.5 1.6 copy-start.1
  13.1 1.0 copy-start.15
  14.4 19.6 %copy-start.2 = (f32[256,2048]{1,0:T(8,128)S(1)}, f32[256,2048]{1,0:T(8,128)}, u32[]{:S(2)}) copy-start(f32[256,2048]{1,0:T(8,128)} %refs_6_.9) | copy-start | bytes 6291460
  14.4 11.2 %collective-permute-start.2 = (f32[256,256]{1,0:T(8,128)S(1)}, f32[256,256]{1,0:T(8,128)S(1)}, u32[]{:S(2)}, u32[]{:S(2)}) collective-permute-start(f32[256,256]{1,0:T(8,128)S(1)} %get-tuple-element.14.refs_4_), channel_id=1, source_target_pairs={{4,0},{12,8},{20,16},{28,24},{5,1},{13,9},{21,17},{29,25},{6,2},{1... | collective-permute-start | bytes 786440 | tf_op jit(solution)/shard_map/ppermute | solution.py:295
  15.8 16.6 %collective-permute-start.6 = (f32[128,1024]{1,0:T(8,128)S(1)}, f32[128,1024]{1,0:T(8,128)S(1)}, u32[]{:S(2)}, u32[]{:S(2)}) collective-permute-start(f32[128,1024]{1,0:T(8,128)S(1)} %collective-permute-done.5.refs_9_), channel_id=1, source_target_pairs={{0,1},{1,0},{2,3},{3,2},{4,5},{5,4},{6,7},{7,6},{8,9},{9,8},{10,11... | collective-permute-start | bytes 1572872 | tf_op jit(solution)/shard_map/ppermute | solution.py:308
  18.3 12.2 %collective-permute-start = (f32[256,256]{1,0:T(8,128)S(1)}, f32[256,256]{1,0:T(8,128)S(1)}, u32[]{:S(2)}, u32[]{:S(2)}) collective-permute-start(f32[256,256]{1,0:T(8,128)S(1)} %get-tuple-element.12), channel_id=1, source_target_pairs={{0,4},{4,0},{8,12},{12,8},{16,20},{20,16},{24,28},{28,24},{1,5},{5... | collective-permute-start | bytes 786440 | tf_op jit(solution)/shard_map/ppermute | solution.py:294
  20.8 60.1 %collective-permute-start.38 = (f32[512,512]{1,0:T(8,128)S(1)}, f32[512,512]{1,0:T(8,128)S(1)}, u32[]{:S(2)}, u32[]{:S(2)}) collective-permute-start(f32[512,512]{1,0:T(8,128)S(1)} %get-tuple-element.20), channel_id=1, source_target_pairs={{0,2},{1,3},{2,0},{3,1},{4,6},{5,7},{6,4},{7,5},{8,10},{9,11},{10,... | collective-permute-start | bytes 3145736 | tf_op jit(solution)/shard_map/ppermute | solution.py:421
  25.6 6.4 %collective-permute-start.4 = (f32[128,512]{1,0:T(8,128)S(1)}, f32[128,512]{1,0:T(8,128)S(1)}, u32[]{:S(2)}, u32[]{:S(2)}) collective-permute-start(f32[128,512]{1,0:T(8,128)S(1)} %collective-permute-done.3.refs_7_), channel_id=1, source_target_pairs={{0,1},{1,0},{2,3},{3,2},{4,5},{5,4},{6,7},{7,6},{8,9},{9,8},{10,11... | collective-permute-start | bytes 786440 | tf_op jit(solution)/shard_map/ppermute | solution.py:306
  30.5 27.7 %collective-permute-start.32 = (f32[256,512]{1,0:T(8,128)S(1)}, f32[256,512]{1,0:T(8,128)}, u32[]{:S(2)}, u32[]{:S(2)}) collective-permute-start(f32[256,512]{1,0:T(8,128)S(1)} %get-tuple-element.23), channel_id=1, source_target_pairs={{0,2},{1,3},{2,0},{3,1},{4,6},{5,7},{6,4},{7,5},{8,10},{9,11},{10,... | collective-permute-start | bytes 1572872 | tf_op jit(solution)/shard_map/ppermute | solution.py:421
  32.0 69.1 %collective-permute-start.36 = (f32[512,512]{1,0:T(8,128)S(1)}, f32[512,512]{1,0:T(8,128)S(1)}, u32[]{:S(2)}, u32[]{:S(2)}) collective-permute-start(f32[512,512]{1,0:T(8,128)S(1)} %get-tuple-element.21), channel_id=1, source_target_pairs={{0,2},{1,3},{2,0},{3,1},{4,6},{5,7},{6,4},{7,5},{8,10},{9,11},{10,... | collective-permute-start | bytes 3145736 | tf_op jit(solution)/shard_map/ppermute | solution.py:421
  32.5 69.8 %collective-permute-start.34 = (f32[512,512]{1,0:T(8,128)S(1)}, f32[512,512]{1,0:T(8,128)S(1)}, u32[]{:S(2)}, u32[]{:S(2)}) collective-permute-start(f32[512,512]{1,0:T(8,128)S(1)} %get-tuple-element.22), channel_id=1, source_target_pairs={{0,2},{1,3},{2,0},{3,1},{4,6},{5,7},{6,4},{7,5},{8,10},{9,11},{10,... | collective-permute-start | bytes 3145736 | tf_op jit(solution)/shard_map/ppermute | solution.py:421
  58.2 12.5 %collective-permute-start.7 = (f32[128,512]{1,0:T(8,128)S(1)}, f32[128,512]{1,0:T(8,128)S(1)}, u32[]{:S(2)}, u32[]{:S(2)}) collective-permute-start(f32[128,512]{1,0:T(8,128)S(1)} %shard_map.70.refs_0_), channel_id=1, source_target_pairs={{0,8},{4,12},{1,9},{5,13},{2,10},{6,14},{3,11},{7,15}} | collective-permute-start | bytes 786440 | tf_op jit(solution)/shard_map/ppermute | solution.py:336
  70.7 14.3 %collective-permute-start.8 = (f32[128,512]{1,0:T(8,128)S(1)}, f32[128,512]{1,0:T(8,128)S(1)}, u32[]{:S(2)}, u32[]{:S(2)}) collective-permute-start(f32[128,512]{1,0:T(8,128)S(1)} %shard_map.70.refs_0_), channel_id=1, source_target_pairs={{0,16},{4,20},{1,17},{5,21},{2,18},{6,22},{3,19},{7,23}} | collective-permute-start | bytes 786440 | tf_op jit(solution)/shard_map/ppermute | solution.py:336
  80.9 43.8 %copy-start.7 = (f32[512,512]{1,0:T(8,128)}, f32[512,512]{1,0:T(8,128)S(1)}, u32[]{:S(2)}) copy-start(f32[512,512]{1,0:T(8,128)S(1)} %collective-permute-done.38.x_ref) | copy-start | bytes 3145732
  80.9 9.2 %collective-permute-start.11 = (f32[128,512]{1,0:T(8,128)S(1)}, f32[128,512]{1,0:T(8,128)S(1)}, u32[]{:S(2)}, u32[]{:S(2)}) collective-permute-start(f32[128,512]{1,0:T(8,128)S(1)} %shard_map.71.refs_4_.refs_0_), channel_id=1, source_target_pairs={{0,8},{4,12},{8,16},{12,20},{1,9},{5,13},{9,17},{13,21},{2,10},{6,... | collective-permute-start | bytes 786440 | tf_op jit(solution)/shard_map/ppermute | solution.py:336
  85.0 36.0 %collective-permute-start.9 = (f32[128,512]{1,0:T(8,128)S(1)}, f32[128,512]{1,0:T(8,128)S(1)}, u32[]{:S(2)}, u32[]{:S(2)}) collective-permute-start(f32[128,512]{1,0:T(8,128)S(1)} %shard_map.70.refs_0_), channel_id=1, source_target_pairs={{0,24},{4,28},{1,25},{5,29},{2,26},{6,30},{3,27},{7,31}} | collective-permute-start | bytes 786440 | tf_op jit(solution)/shard_map/ppermute | solution.py:336
  90.1 32.2 %collective-permute-start.12 = (f32[128,512]{1,0:T(8,128)S(1)}, f32[128,512]{1,0:T(8,128)S(1)}, u32[]{:S(2)}, u32[]{:S(2)}) collective-permute-start(f32[128,512]{1,0:T(8,128)S(1)} %shard_map.71.refs_4_.refs_0_), channel_id=1, source_target_pairs={{0,16},{4,20},{8,24},{12,28},{1,17},{5,21},{9,25},{13,29},{2,18},{... | collective-permute-start | bytes 786440 | tf_op jit(solution)/shard_map/ppermute | solution.py:336
  101.0 34.9 %copy-start.11 = (f32[512,512]{1,0:T(8,128)}, f32[512,512]{1,0:T(8,128)S(1)}, u32[]{:S(2)}) copy-start(f32[512,512]{1,0:T(8,128)S(1)} %collective-permute-done.36.x_ref) | copy-start | bytes 3145732
  101.0 22.0 %collective-permute-start.15 = (f32[128,512]{1,0:T(8,128)S(1)}, f32[128,512]{1,0:T(8,128)S(1)}, u32[]{:S(2)}, u32[]{:S(2)}) collective-permute-start(f32[128,512]{1,0:T(8,128)S(1)} %shard_map.72.refs_8_.refs_4_), channel_id=1, source_target_pairs={{8,16},{12,20},{16,24},{20,28},{9,17},{13,21},{17,25},{21,29},{10,... | collective-permute-start | bytes 786440 | tf_op jit(solution)/shard_map/ppermute | solution.py:336
  102.3 33.7 %copy-start.9 = (f32[512,512]{1,0:T(8,128)}, f32[512,512]{1,0:T(8,128)S(1)}, u32[]{:S(2)}) copy-start(f32[512,512]{1,0:T(8,128)S(1)} %collective-permute-done.34.x_ref) | copy-start | bytes 3145732
  102.3 22.6 %collective-permute-start.21 = (f32[128,512]{1,0:T(8,128)S(1)}, f32[128,512]{1,0:T(8,128)S(1)}, u32[]{:S(2)}, u32[]{:S(2)}) collective-permute-start(f32[128,512]{1,0:T(8,128)S(1)} %shard_map.71.refs_4_.refs_0_), channel_id=1, source_target_pairs={{0,24},{4,28},{1,25},{5,29},{2,26},{6,30},{3,27},{7,31}} | collective-permute-start | bytes 786440 | tf_op jit(solution)/shard_map/ppermute | solution.py:336
  121.0 10.0 %collective-permute-start.10 = (f32[128,512]{1,0:T(8,128)S(1)}, f32[128,512]{1,0:T(8,128)S(1)}, u32[]{:S(2)}, u32[]{:S(2)}) collective-permute-start(f32[128,512]{1,0:T(8,128)S(1)} %shard_map.71.refs_4_.refs_0_), channel_id=1, source_target_pairs={{8,0},{12,4},{9,1},{13,5},{10,2},{14,6},{11,3},{15,7}} | collective-permute-start | bytes 786440 | tf_op jit(solution)/shard_map/ppermute | solution.py:338
  122.3 10.0 %collective-permute-start.22 = (f32[128,512]{1,0:T(8,128)S(1)}, f32[128,512]{1,0:T(8,128)S(1)}, u32[]{:S(2)}, u32[]{:S(2)}) collective-permute-start(f32[128,512]{1,0:T(8,128)S(1)} %shard_map.72.refs_8_.refs_4_), channel_id=1, source_target_pairs={{8,24},{12,28},{9,25},{13,29},{10,26},{14,30},{11,27},{15,31}} | collective-permute-start | bytes 786440 | tf_op jit(solution)/shard_map/ppermute | solution.py:336
  123.0 10.8 %collective-permute-start.14 = (f32[128,512]{1,0:T(8,128)S(1)}, f32[128,512]{1,0:T(8,128)S(1)}, u32[]{:S(2)}, u32[]{:S(2)}) collective-permute-start(f32[128,512]{1,0:T(8,128)S(1)} %shard_map.72.refs_8_.refs_4_), channel_id=1, source_target_pairs={{8,0},{12,4},{16,8},{20,12},{9,1},{13,5},{17,9},{21,13},{10,2},{14... | collective-permute-start | bytes 786440 | tf_op jit(solution)/shard_map/ppermute | solution.py:338
  124.9 9.6 %collective-permute-start.23 = (f32[128,512]{1,0:T(8,128)S(1)}, f32[128,512]{1,0:T(8,128)S(1)}, u32[]{:S(2)}, u32[]{:S(2)}) collective-permute-start(f32[128,512]{1,0:T(8,128)S(1)} %shard_map.74.refs_0_.refs_8_), channel_id=1, source_target_pairs={{16,24},{20,28},{17,25},{21,29},{18,26},{22,30},{19,27},{23,31}} | collective-permute-start | bytes 786440 | tf_op jit(solution)/shard_map/ppermute | solution.py:336
  131.0 18.0 %collective-permute-start.13 = (f32[128,512]{1,0:T(8,128)S(1)}, f32[128,512]{1,0:T(8,128)S(1)}, u32[]{:S(2)}, u32[]{:S(2)}) collective-permute-start(f32[128,512]{1,0:T(8,128)S(1)} %shard_map.72.refs_8_.refs_4_), channel_id=1, source_target_pairs={{16,0},{20,4},{17,1},{21,5},{18,2},{22,6},{19,3},{23,7}} | collective-permute-start | bytes 786440 | tf_op jit(solution)/shard_map/ppermute | solution.py:338
  132.3 36.3 %collective-permute-start.17 = (f32[128,512]{1,0:T(8,128)S(1)}, f32[128,512]{1,0:T(8,128)S(1)}, u32[]{:S(2)}, u32[]{:S(2)}) collective-permute-start(f32[128,512]{1,0:T(8,128)S(1)} %shard_map.74.refs_0_.refs_8_), channel_id=1, source_target_pairs={{16,0},{20,4},{24,8},{28,12},{17,1},{21,5},{25,9},{29,13},{18,2},{... | collective-permute-start | bytes 786440 | tf_op jit(solution)/shard_map/ppermute | solution.py:338
  133.8 35.7 %collective-permute-start.18 = (f32[128,512]{1,0:T(8,128)S(1)}, f32[128,512]{1,0:T(8,128)S(1)}, u32[]{:S(2)}, u32[]{:S(2)}) collective-permute-start(f32[128,512]{1,0:T(8,128)S(1)} %shard_map.74.refs_0_.refs_8_), channel_id=1, source_target_pairs={{16,8},{20,12},{24,16},{28,20},{17,9},{21,13},{25,17},{29,21},{18,... | collective-permute-start | bytes 786440 | tf_op jit(solution)/shard_map/ppermute | solution.py:338
  134.5 36.6 %collective-permute-start.16 = (f32[128,512]{1,0:T(8,128)S(1)}, f32[128,512]{1,0:T(8,128)S(1)}, u32[]{:S(2)}, u32[]{:S(2)}) collective-permute-start(f32[128,512]{1,0:T(8,128)S(1)} %shard_map.74.refs_0_.refs_8_), channel_id=1, source_target_pairs={{24,0},{28,4},{25,1},{29,5},{26,2},{30,6},{27,3},{31,7}} | collective-permute-start | bytes 786440 | tf_op jit(solution)/shard_map/ppermute | solution.py:338
  136.0 37.2 %copy-start.5 = (f32[128,512]{1,0:T(8,128)}, f32[128,512]{1,0:T(8,128)S(1)}, u32[]{:S(2)}) copy-start(f32[128,512]{1,0:T(8,128)S(1)} %shard_map.77.refs_0_.token_ref) | copy-start | bytes 786436
  149.0 23.5 %collective-permute-start.24 = (f32[128,512]{1,0:T(8,128)S(1)}, f32[128,512]{1,0:T(8,128)S(1)}, u32[]{:S(2)}, u32[]{:S(2)}) collective-permute-start(f32[128,512]{1,0:T(8,128)S(1)} %shard_map.77.refs_0_.token_ref), channel_id=1, source_target_pairs={{24,0},{28,4},{25,1},{29,5},{26,2},{30,6},{27,3},{31,7}} | collective-permute-start | bytes 786440 | tf_op jit(solution)/shard_map/ppermute | solution.py:338
  168.6 4.6 %collective-permute-start.25 = (f32[128,512]{1,0:T(8,128)S(1)}, f32[128,512]{1,0:T(8,128)S(1)}, u32[]{:S(2)}, u32[]{:S(2)}) collective-permute-start(f32[128,512]{1,0:T(8,128)S(1)} %shard_map.77.refs_0_.token_ref), channel_id=1, source_target_pairs={{24,8},{28,12},{25,9},{29,13},{26,10},{30,14},{27,11},{31,15}} | collective-permute-start | bytes 786440 | tf_op jit(solution)/shard_map/ppermute | solution.py:338
  169.5 47.5 %collective-permute-start.19 = (f32[128,1536]{1,0:T(8,128)S(1)}, f32[128,1536]{1,0:T(8,128)S(1)}, u32[]{:S(2)}, u32[]{:S(2)}) collective-permute-start(f32[128,1536]{1,0:T(8,128)S(1)} %shard_map.73.refs_0_), channel_id=1, source_target_pairs={{0,4},{4,0},{8,12},{12,8},{16,20},{20,16},{24,28},{28,24},{1,5},{5... | collective-permute-start | bytes 2359304 | tf_op jit(solution)/shard_map/ppermute | solution.py:364
  171.1 4.4 %collective-permute-start.26 = (f32[128,512]{1,0:T(8,128)S(1)}, f32[128,512]{1,0:T(8,128)}, u32[]{:S(2)}, u32[]{:S(2)}) collective-permute-start(f32[128,512]{1,0:T(8,128)S(1)} %shard_map.77.refs_0_.token_ref), channel_id=1, source_target_pairs={{24,16},{28,20},{25,17},{29,21},{26,18},{30,22},{27,19},{31,23}} | collective-permute-start | bytes 786440 | tf_op jit(solution)/shard_map/ppermute | solution.py:338
  172.5 0.7 copy-start.16
  172.5 23.2 %collective-permute-start.20 = (f32[128,512]{1,0:T(8,128)S(1)}, f32[128,512]{1,0:T(8,128)}, u32[]{:S(2)}, u32[]{:S(2)}) collective-permute-start(f32[128,512]{1,0:T(8,128)S(1)} %shard_map.75.refs_1_), channel_id=1, source_target_pairs={{0,4},{4,0},{8,12},{12,8},{16,20},{20,16},{24,28},{28,24},{1,5},{5... | collective-permute-start | bytes 786440 | tf_op jit(solution)/shard_map/ppermute | solution.py:364
  173.2 0.7 copy-start.18
  173.9 45.4 %collective-permute-start.27 = (f32[128,1536]{1,0:T(8,128)S(1)}, f32[128,1536]{1,0:T(8,128)}, u32[]{:S(2)}, u32[]{:S(2)}) collective-permute-start(f32[128,1536]{1,0:T(8,128)S(1)} %shard_map.76.refs_4_), channel_id=1, source_target_pairs={{0,4},{4,0},{8,12},{12,8},{16,20},{20,16},{24,28},{28,24},{1,5},{5... | collective-permute-start | bytes 2359304 | tf_op jit(solution)/shard_map/ppermute | solution.py:364
  175.5 44.1 %copy-start.20 = (f32[512]{0:T(512)S(1)}, f32[512]{0:T(512)}, u32[]{:S(2)}) copy-start(f32[512]{0:T(512)} %param.9) | copy-start | bytes 6148
  175.5 57.0 %collective-permute-start.39 = (f32[512,512]{1,0:T(8,128)}, f32[512,512]{1,0:T(8,128)}, u32[]{:S(2)}, u32[]{:S(2)}) collective-permute-start(f32[512,512]{1,0:T(8,128)} %shard_map.84.refs_2_), channel_id=1, source_target_pairs={{0,1},{1,0},{2,3},{3,2},{4,5},{5,4},{6,7},{7,6},{8,9},{9,8},{10,11... | collective-permute-start | bytes 3145736 | tf_op jit(solution)/shard_map/ppermute | solution.py:421
  175.5 1.0 copy-start.6
  176.4 0.9 copy-start.17
  177.4 0.9 copy-start.19
  195.7 21.3 %collective-permute-start.28 = (f32[128,512]{1,0:T(8,128)S(1)}, f32[128,512]{1,0:T(8,128)S(1)}, u32[]{:S(2)}, u32[]{:S(2)}) collective-permute-start(f32[128,512]{1,0:T(8,128)S(1)} %shard_map.78.refs_5_), channel_id=1, source_target_pairs={{0,4},{4,0},{8,12},{12,8},{16,20},{20,16},{24,28},{28,24},{1,5},{5... | collective-permute-start | bytes 786440 | tf_op jit(solution)/shard_map/ppermute | solution.py:364
  217.0 23.1 %collective-permute-start.37 = (f32[512,512]{1,0:T(8,128)}, f32[512,512]{1,0:T(8,128)}, u32[]{:S(2)}, u32[]{:S(2)}) collective-permute-start(f32[512,512]{1,0:T(8,128)} %shard_map.83.refs_2_), channel_id=1, source_target_pairs={{0,1},{1,0},{2,3},{3,2},{4,5},{5,4},{6,7},{7,6},{8,9},{9,8},{10,11... | collective-permute-start | bytes 3145736 | tf_op jit(solution)/shard_map/ppermute | solution.py:421
  217.0 0.9 copy-start.13
  217.8 14.7 %collective-permute-start.30 = (f32[256,512]{1,0:T(8,128)}, f32[256,512]{1,0:T(8,128)}, u32[]{:S(2)}, u32[]{:S(2)}) collective-permute-start(f32[256,512]{1,0:T(8,128)} %get-tuple-element.24), channel_id=1, source_target_pairs={{0,2},{1,3},{2,0},{3,1},{4,6},{5,7},{6,4},{7,5},{8,10},{9,11},{10,... | collective-permute-start | bytes 1572872 | tf_op jit(solution)/shard_map/ppermute | solution.py:421
  219.3 13.7 %copy-start.8 = (f32[512,512]{1,0:T(8,128)S(1)}, f32[512,512]{1,0:T(8,128)}, u32[]{:S(2)}) copy-start(f32[512,512]{1,0:T(8,128)} %shard_map.84.refs_2_) | copy-start | bytes 3145732
  219.3 28.0 %collective-permute-start.35 = (f32[512,512]{1,0:T(8,128)}, f32[512,512]{1,0:T(8,128)}, u32[]{:S(2)}, u32[]{:S(2)}) collective-permute-start(f32[512,512]{1,0:T(8,128)} %shard_map.82.refs_2_), channel_id=1, source_target_pairs={{0,1},{1,0},{2,3},{3,2},{4,5},{5,4},{6,7},{7,6},{8,9},{9,8},{10,11... | collective-permute-start | bytes 3145736 | tf_op jit(solution)/shard_map/ppermute | solution.py:421
  219.6 1.2 copy-start.14
  225.5 7.6 %copy-start.3 = (bf16[2048,512]{1,0:T(8,128)(2,1)S(1)}, bf16[2048,512]{1,0:T(8,128)(2,1)}, u32[]{:S(2)}) copy-start(bf16[2048,512]{1,0:T(8,128)(2,1)} %get-tuple-element.18.token_ref.refs_5_) | copy-start | bytes 6291460
  232.5 22.1 %collective-permute-start.33 = (f32[256,512]{1,0:T(8,128)}, f32[256,512]{1,0:T(8,128)}, u32[]{:S(2)}, u32[]{:S(2)}) collective-permute-start(f32[256,512]{1,0:T(8,128)} %shard_map.81.refs_2_), channel_id=1, source_target_pairs={{0,1},{1,0},{2,3},{3,2},{4,5},{5,4},{6,7},{7,6},{8,9},{9,8},{10,11... | collective-permute-start | bytes 1572872 | tf_op jit(solution)/shard_map/ppermute | solution.py:421
  232.5 26.5 %collective-permute-start.31 = (f32[256,512]{1,0:T(8,128)}, f32[256,512]{1,0:T(8,128)S(1)}, u32[]{:S(2)}, u32[]{:S(2)}) collective-permute-start(f32[256,512]{1,0:T(8,128)} %shard_map.80.refs_2_), channel_id=1, source_target_pairs={{0,1},{1,0},{2,3},{3,2},{4,5},{5,4},{6,7},{7,6},{8,9},{9,8},{10,11... | collective-permute-start | bytes 1572872 | tf_op jit(solution)/shard_map/ppermute | solution.py:421
  233.0 7.1 %copy-start.12 = (f32[512,512]{1,0:T(8,128)S(1)}, f32[512,512]{1,0:T(8,128)}, u32[]{:S(2)}) copy-start(f32[512,512]{1,0:T(8,128)} %shard_map.83.refs_2_) | copy-start | bytes 3145732
  240.1 7.2 %copy-start.10 = (f32[512,512]{1,0:T(8,128)S(1)}, f32[512,512]{1,0:T(8,128)}, u32[]{:S(2)}) copy-start(f32[512,512]{1,0:T(8,128)} %shard_map.82.refs_2_) | copy-start | bytes 3145732
  247.3 7.3 %copy-start.4 = (bf16[2048,512]{1,0:T(8,128)(2,1)S(1)}, bf16[2048,512]{1,0:T(8,128)(2,1)}, u32[]{:S(2)}) copy-start(bf16[2048,512]{1,0:T(8,128)(2,1)} %get-tuple-element.19.refs_6_) | copy-start | bytes 6291460

commit v2 on v0

v2 whole, which is shorter than its diff:
```python
import jax
import jax.numpy as jnp
from jax import lax
from jax.experimental import pallas as pl
from jax.experimental.pallas import tpu as pltpu
from jax.sharding import PartitionSpec as P

F32 = jnp.float32
BF16 = jnp.bfloat16
HIGHEST = lax.Precision.HIGHEST
ANY = pl.BlockSpec(memory_space=pl.ANY)
VMEM = pl.BlockSpec(memory_space=pltpu.VMEM)
LIMIT = 62 * 1024 * 1024
RETURNS = 2
TINY = pl.CostEstimate(flops=1, bytes_accessed=1, transcendentals=0)


def params():
    return pltpu.CompilerParams(vmem_limit_bytes=LIMIT)


def mul(a, b):
    return jnp.dot(a, b, precision=HIGHEST, preferred_element_type=F32)


def mul_t(a, b):
    return lax.dot_general(
        a, b, (((1,), (1,)), ((), ())), precision=HIGHEST, preferred_element_type=F32
    )


def level_and_half():
    own_row = lax.axis_index("row")
    return own_row // 2, own_row % 2


def run_copies(pairs, sems):
    copies = [pltpu.make_async_copy(s, d, sems.at[i]) for i, (s, d) in enumerate(pairs)]
    for copy in copies:
        copy.start()
    for copy in copies:
        copy.wait()


def stage_kernel(z_ref, diag_ref, own_ref, send_ref, corner_ref, panel, sems):
    level, half = level_and_half()
    size = z_ref.shape[0]
    start = pl.multiple_of(level * 2 * size, 2 * size)
    run_copies([(z_ref, panel), (diag_ref.at[:, pl.ds(start, size)], corner_ref)], sems)
    width = z_ref.shape[1] // 2
    flipped = panel[...].T
    low, high = flipped[:width], flipped[width:]
    own_ref[...] = jnp.where(half == 0, low, high)
    send_ref[...] = jnp.where(half == 0, high, low)


def inverse_of(tri):
    size = tri.shape[0]
    base = 16
    count = size // base
    rows = lax.broadcasted_iota(jnp.int32, (size, size), 0)
    cols = lax.broadcasted_iota(jnp.int32, (size, size), 1)
    same = (rows // base) == (cols // base)
    folded = jnp.sum(jnp.where(same, tri, 0.0).reshape(count, base, size), axis=0)
    lane = lax.broadcasted_iota(jnp.int32, (base, size), 1) % base
    line = lax.broadcasted_iota(jnp.int32, (base, size), 0)
    spread = jnp.concatenate([jnp.where(lane == k, folded, 0.0) for k in range(base)], axis=0)
    spread = mul(spread, jnp.where(same, 1.0, 0.0))
    rest = jnp.where(lane == line, 1.0, 0.0)
    done = jnp.zeros((base, size), F32)
    for k in range(base):
        column = spread[k * base:(k + 1) * base]
        solved = rest[k:k + 1] / column[k:k + 1]
        done = jnp.where(line == k, solved, done)
        rest = rest - jnp.where(line > k, column, 0.0) * solved
    full = jnp.where(same, jnp.concatenate([done] * count, axis=0), 0.0)
    step = base
    while step < size:
        pair = (rows // (2 * step)) == (cols // (2 * step))
        below = ((rows // step) % 2 == 1) & ((cols // step) % 2 == 0)
        off = jnp.where(pair & below, tri, 0.0)
        full = full - mul(full, mul(off, full))
        step *= 2
    return full


def inverse_kernel(diag_ref, token_ref, inv_ref, tile_ref, sems):
    del token_ref
    own_row = lax.axis_index("row")
    size = tile_ref.shape[0]
    source = diag_ref.at[:, pl.ds(pl.multiple_of(own_row * size, size), size)]
    run_copies([(source, tile_ref)], sems)
    inv_ref[...] = inverse_of(tile_ref[...])


def strips_kernel(distances, diag_ref, *refs):
    out_ref, sems = refs[-2:]
    level, _ = level_and_half()
    strip = out_ref.shape[0]
    width = 4 * strip
    core = lax.axis_index("col") % 2
    lines = pl.ds(pl.multiple_of(core * strip, strip), strip)
    pairs = []
    for slot, d in enumerate(distances):
        block = jnp.maximum(level - d, 0)
        source = diag_ref.at[lines, pl.ds(pl.multiple_of(block * width, width), width)]
        pairs.append((source, out_ref.at[:, pl.ds(slot * width, width)]))
    run_copies(pairs, sems)


def mul_t3(a, b):
    def parts(x):
        coarse = x.astype(BF16)
        return coarse, (x - coarse.astype(F32)).astype(BF16)

    def dot(x, y):
        return lax.dot_general(x, y, (((1,), (1,)), ((), ())), preferred_element_type=F32)

    (a_high, a_low), (b_high, b_low) = parts(a), parts(b)
    return dot(a_high, b_high) + dot(a_high, b_low) + dot(a_low, b_high)


def solve_kernel(turn, n_refs, *refs):
    z_own, z_other, inv_own, inv_other, corner_own, corner_other, diag, *rest_refs = refs[:n_refs]
    came = rest_refs[:turn]
    strips = rest_refs[turn:turn + 2 * min(turn, 2)]
    outs = refs[n_refs:-6]
    rest, tiles, low, low_other, earlier, sems = refs[-6:]
    level, half = level_and_half()
    core = lax.axis_index("col") % 2
    lines, size = rest.shape[1:]
    width = 2 * size
    strip = size // 2

    @pl.when(level == turn)
    def _():
        pairs = [
            (z_own, rest.at[0]),
            (z_other, rest.at[1]),
            (inv_own, tiles.at[0]),
            (inv_other, tiles.at[1]),
        ]
        here = pl.ds(pl.multiple_of(core * strip, strip), strip)
        there = pl.ds(pl.multiple_of((1 - core) * strip, strip), strip)
        if turn:
            pairs.append((diag.at[:, pl.ds(0, turn * width)], low))
        for d in range(1, turn + 1):
            spot = pl.ds((turn - d) * width, width)
            pairs.append((came[d - 1], earlier.at[:, spot]))
            for side, place in zip(strips[:2] if d == 1 else strips[2:], (here, there)):
                if d > 1:
                    side = side.at[:, pl.ds((d - 2) * width, width)]
                pairs.append((side, low_other.at[place, spot]))
        copies = [pltpu.make_async_copy(s, t, sems.at[i + 1]) for i, (s, t) in enumerate(pairs)]
        own_corner = pltpu.make_async_copy(corner_own, tiles.at[2], sems.at[0])
        other_corner = pltpu.make_async_copy(corner_other, tiles.at[2], sems.at[0])
        for copy in copies:
            copy.start()

        @pl.when(half == 1)
        def _():
            own_corner.start()

        @pl.when(half == 0)
        def _():
            other_corner.start()

        for copy in copies:
            copy.wait()
        own_corner.wait()
        first, second = rest[0], rest[1]
        if turn:
            first = first - mul_t3(earlier[...], low[...])
            second = second - mul_t3(earlier[...], low_other[...])
        upper = half == 0
        top = mul_t(jnp.where(upper, first, second), jnp.where(upper, tiles[0], tiles[1]))
        bottom = jnp.where(upper, second, first) - mul_t(top, tiles[2])
        bottom = mul_t(bottom, jnp.where(upper, tiles[1], tiles[0]))
        part = outs[0].shape[0]
        for q, out in enumerate(outs):
            out[:, :size] = top[q * part:(q + 1) * part]
            out[:, size:] = bottom[q * part:(q + 1) * part]


def pick_kernel(levels, *refs):
    out, sems = refs[-2:]
    level, _ = level_and_half()
    for z in range(levels):
        @pl.when(level == z)
        def _(z=z):
            run_copies([(refs[z], out)], sems)


def product(value, high, low):
    coarse = value.astype(BF16)
    fine = (value - coarse.astype(F32)).astype(BF16)
    total = jnp.dot(coarse, high, preferred_element_type=F32)
    total += jnp.dot(coarse, low, preferred_element_type=F32)
    return total + jnp.dot(fine, high, preferred_element_type=F32)


def update_kernel(plan, flips, tile, n_refs, *refs):
    ins = refs[:2 * len(plan)]
    norm, partial = refs[2 * len(plan):2 * len(plan) + 2]
    parts = refs[2 * len(plan) + 2:2 * len(plan) + 2 + len(flips)]
    norm_out, out, lines, high, low, panel, sems, panel_sems = refs[n_refs:]
    own_col = lax.axis_index("col")
    _, half = level_and_half()
    step = pl.program_id(0)
    rows, depth = parts[0].shape
    tiles = rows // tile
    wide, span = lines.shape
    width = span // len({level for level, _, _ in plan})
    count = span // depth
    first = min(level for level, _, _ in plan) * (width // depth)

    def panel_copies(act):
        for flip, part in zip(flips, parts):
            slot = lax.bitwise_xor(own_col, flip) - first

            @pl.when((slot >= 0) & (slot < count))
            def _(part=part, slot=slot):
                for i in range(tiles):
                    spot = pl.ds(i * tile, tile)
                    act(i, pltpu.make_async_copy(
                        part.at[spot], panel.at[slot, spot], panel_sems.at[i, slot]))

    @pl.when(step == 0)
    def _():
        pairs = []
        for index, (_, place, line) in enumerate(plan):
            for side in (0, 1):
                ref = ins[2 * index + side]
                number = ref.shape[0]
                start = jnp.where(half == side, 0, wide // 2) + line
                pairs.append((ref, lines.at[
                    pl.ds(pl.multiple_of(start, number), number), pl.ds(place * width, width)]))
        copies = [pltpu.make_async_copy(s, t, sems.at[i]) for i, (s, t) in enumerate(pairs)]
        for copy in copies:
            copy.start()
        panel_copies(lambda i, copy: copy.start())
        for copy in copies:
            copy.wait()
        total = norm[...]
        for k in range(span // width):
            block = lines[:, k * width:(k + 1) * width].T
            coarse = block.astype(BF16)
            high[k * width:(k + 1) * width] = coarse
            low[k * width:(k + 1) * width] = (block - coarse.astype(F32)).astype(BF16)
            total = total + jnp.sum(block * block, axis=0, keepdims=True)
        norm_out[...] = total

    def wait(i, copy):
        @pl.when(step == i)
        def _():
            copy.wait()

    panel_copies(wait)
    here = pl.ds(pl.multiple_of(step * tile, tile), tile)
    total = partial[...]
    for k in range(count):
        spot = slice(k * depth, (k + 1) * depth)
        total = total - product(panel[k, here, :], high[spot], low[spot])
    out[...] = total


def tie_kernel(x_ref, token_ref, out_ref):
    del x_ref, token_ref, out_ref


def tie(x, token):
    return pl.pallas_call(
        tie_kernel,
        out_shape=jax.ShapeDtypeStruct(x.shape, x.dtype),
        in_specs=[ANY, ANY],
        out_specs=ANY,
        input_output_aliases={0: 0},
        cost_estimate=TINY,
    )(x, token)


def struct(*shape, dtype=F32):
    return jax.ShapeDtypeStruct(shape, dtype)


def forward_substitution(diag_block, z_panel):
    rows = lax.axis_size("row")
    levels = rows // 2
    last = levels - 1
    cols = lax.axis_size("col")
    size, full = diag_block.shape
    wide = z_panel.shape[1]
    width, half_wide, strip = 2 * size, wide // 2, size // 2
    dma = pltpu.SemaphoreType.DMA

    swap = [(i, i ^ 1) for i in range(rows)]
    cores = [(i, i ^ 1) for i in range(cols)]

    def move(x, source, target):
        return lax.ppermute(x, "row", [(2 * source + y, 2 * target + y) for y in (0, 1)])

    def strips(distances, *tokens):
        return pl.pallas_call(
            lambda *refs: strips_kernel(distances, *refs),
            out_shape=struct(strip, width * len(distances)),
            in_specs=[ANY] * (1 + len(tokens)),
            out_specs=VMEM,
            scratch_shapes=[dma((len(distances),))],
            compiler_params=params(),
            cost_estimate=TINY,
        )(diag_block, *tokens)

    z_own, z_send, corner = pl.pallas_call(
        stage_kernel,
        out_shape=(struct(half_wide, size), struct(half_wide, size), struct(size, size)),
        in_specs=[ANY, ANY],
        out_specs=(VMEM, VMEM, VMEM),
        scratch_shapes=[pltpu.VMEM((size, wide), F32), dma((2,))],
        compiler_params=params(),
        cost_estimate=TINY,
    )(z_panel, diag_block)
    z_other = lax.ppermute(z_send, "row", swap)
    corner_other = lax.ppermute(corner, "row", [p for p in swap if p[0] % 2 == 1])
    inv = pl.pallas_call(
        inverse_kernel,
        out_shape=struct(size, size),
        in_specs=[ANY, ANY],
        out_specs=VMEM,
        scratch_shapes=[pltpu.VMEM((size, size), F32), dma((1,))],
        compiler_params=params(),
        cost_estimate=TINY,
    )(diag_block, z_send)
    inv_other = lax.ppermute(inv, "row", swap)
    near_a = lax.ppermute(
        strips([1], inv_other, z_other, corner_other), "row", [p for p in swap if p[0] >= 2])

    def solve(turn, came, strip_pairs, token, n_out=1):
        args = [z_own, z_other, inv, inv_other, corner, corner_other, diag_block]
        args += [*came, *strip_pairs]
        args += [token] if token is not None else []
        deep = max(turn, 1) * width
        return pl.pallas_call(
            lambda *refs: solve_kernel(turn, len(args), *refs),
            out_shape=[struct(half_wide // n_out, width)] * n_out,
            in_specs=[ANY] * len(args),
            out_specs=[VMEM] * n_out,
            scratch_shapes=[
                pltpu.VMEM((2, half_wide, size), F32),
                pltpu.VMEM((3, size, size), F32),
                pltpu.VMEM((size, deep), F32),
                pltpu.VMEM((size, deep), F32),
                pltpu.VMEM((half_wide, deep), F32),
                dma((6 + 3 * turn,)),
            ],
            compiler_params=params(),
            cost_estimate=TINY,
        )(*args)

    def pick(sources, *tokens):
        args = [sources[z] for z in range(levels)]
        return pl.pallas_call(
            lambda *refs: pick_kernel(levels, *refs),
            out_shape=struct(*args[0].shape),
            in_specs=[ANY] * (levels + len(tokens)),
            out_specs=VMEM,
            scratch_shapes=[dma((1,))],
            compiler_params=params(),
            cost_estimate=TINY,
        )(*args, *tokens)

    held, pieces = {}, {}
    strip_pairs = ()
    token = None

    def share(level, index, tokens):
        mine = pick(pieces[level][index], *tokens)
        return mine, lax.ppermute(mine, "row", swap)

    for turn in range(levels):
        came = [held[turn - d][turn] for d in range(1, turn + 1)]
        for k in range(turn):
            if turn < last:
                held[k][turn + 1] = move(held[k][turn], turn, turn + 1)
        own = solve(turn, came, strip_pairs, token, RETURNS if turn == last else 1)
        token = own[0]
        if turn < last:
            held[turn] = {turn: own[0], turn + 1: move(own[0], turn, turn + 1)}
        pieces[turn] = []
        for part in own:
            place = {turn: part}
            for z in range(turn - 1, -1, -1):
                place[z] = move(place[z + 1], z + 1, z) if turn == last else move(part, turn, z)
            pieces[turn].append(place)
        if turn == 0:
            strip_pairs = (near_a, lax.ppermute(tie(near_a, token), "col", cores))
        if turn == 1:
            far_a = lax.ppermute(
                strips(list(range(2, levels)), token), "row", [p for p in swap if p[0] >= 4])
            strip_pairs += (far_a, lax.ppermute(far_a, "col", cores))
        if turn == last - 1:
            for k in range(last - 1):
                pieces[k][0].update(held[k])
                shared = share(k, 0, [token])
                pieces[k] = [shared]
                token = shared[0]
    pieces[last - 1][0].update(held[last - 1])
    shared = share(last - 1, 0, [token])
    pieces[last - 1] = [shared]
    token = shared[0]
    return pieces, share, token


def shards(diag_block, z_panel, panel_below, z_trail, norm_sq):
    cols = lax.axis_size("col")
    levels = lax.axis_size("row") // 2
    last = levels - 1
    rows, wide = z_trail.shape
    width = 2 * diag_block.shape[0]
    tile = min(512, rows)
    depth = panel_below.shape[1]
    dma = pltpu.SemaphoreType.DMA

    def flipped(x, flip):
        return lax.ppermute(x, "col", [(i, i ^ flip) for i in range(cols)])

    crossed = {flip: flipped(panel_below, flip) for flip in range(2, cols, 2)}
    panels = {0: panel_below, 1: flipped(panel_below, 1)}
    pieces, share, token = forward_substitution(diag_block, z_panel)
    for flip, x in crossed.items():
        panels[flip] = tie(x, token)
        panels[flip ^ 1] = flipped(panels[flip], 1)
    flips = list(panels)
    slabs = [panels[flip] for flip in flips]

    def update(wanted, norm, out):
        plan, args = [], []
        for place, level in enumerate(wanted):
            line = 0
            for pair in pieces[level]:
                plan.append((level, place, line))
                args += pair
                line += pair[0].shape[0]
        first = out is z_trail
        span = width * len(wanted)
        aliases = {} if first else {len(args) + 1: 1}
        args += [norm, out, *slabs]
        line = pl.BlockSpec((1, wide), lambda i: (0, 0))
        whole = pl.BlockSpec((tile, wide), lambda i: (i, 0))
        return pl.pallas_call(
            lambda *refs: update_kernel(plan, flips, tile, len(args), *refs),
            grid=(rows // tile,),
            out_shape=(struct(1, wide), struct(rows, wide)),
            in_specs=[ANY] * (2 * len(plan)) + [line, whole] + [ANY] * len(slabs),
            out_specs=(line, whole),
            scratch_shapes=[
                pltpu.VMEM((wide, span), F32),
                pltpu.VMEM((span, wide), BF16),
                pltpu.VMEM((span, wide), BF16),
                pltpu.VMEM((span // depth, rows, depth), F32),
                dma((2 * len(plan),)),
                dma((rows // tile, span // depth)),
            ],
            input_output_aliases=aliases,
            compiler_params=params(),
            cost_estimate=TINY,
        )(*args)

    norm, out = update(range(last - 1), norm_sq.reshape(1, wide), z_trail)
    pairs = []
    for index in range(RETURNS):
        pairs.append(share(last, index, [token, norm]))
        token = pairs[-1][0]
    pieces[last] = pairs
    norm, out = update([last - 1], norm, out)
    norm, out = update([last], norm, out)
    return (norm.reshape(wide), out)


def solution(mesh):
    return jax.shard_map(
        shards,
        mesh=mesh,
        in_specs=(P("row", None), P("row", "col"), P("row", "col"), P("row", "col"), P("col")),
        out_specs=(P("col"), P("row", "col")),
        check_vma=False,
    )
```

time: 1010 us -> 185 us (0.18)
  waiting for transfers between devices: 676 us -> 84.4 us
  other arithmetic: 176 us -> 0 us
  matrix products: 81.8 us -> 0 us
  Pallas kernels: 0 us -> 61.1 us
  local copies, waits for them, and re-layouts: 60 us -> 6.4 us
  starting transfers between devices: 0.02 us -> 30.5 us
  between operations: 15.5 us -> 1.35 us
    psum x8 -> x0, waiting for transfers between devices: 578 us -> none  [advance(): received = lax.psum(masked, 'row')]
    another operation x24 -> x0, other arithmetic: 165 us -> none  [advance(): lax.linalg.triangular_solve(pivot_tile, z_panel - carried, left_side=True...]
    all_gather x1 -> x0, waiting for transfers between devices: 97.3 us -> none  [shards(): lax.all_gather(panel_below, 'col', axis=1, tiled=True)]
    ppermute x0 -> x30, waiting for transfers between devices: none -> 84.4 us  [the longest x15 53.2 us: move(): lax.ppermute(x, 'row', [(2 * source + y, 2 * target + y) for y in (0, 1)])]
    dot_general x9 -> x0, matrix products: 72 us -> none  [the longest x1 57.7 us: shards(): jnp.dot(lax.all_gather(panel_below, 'col', axis=1, tiled=True), solved, p...]
    pallas_call x0 -> x18, Pallas kernels: none -> 61.1 us  [the longest x3 33.8 us: update(): pl.pallas_call(lambda *refs: update_kernel(plan, flips, tile, len(args),...]
    another operation x56 -> x0, local copies, waits for them, and re-layouts: 31.6 us -> none
    ppermute x0 -> x30, starting transfers between devices: none -> 30.5 us  [the longest x15 17.1 us: move(): lax.ppermute(x, 'row', [(2 * source + y, 2 * target + y) for y in (0, 1)])]
  transfers between devices with their start and end apart: 9 -> 30, of which waited for: 9 -> 8; matrix products, arithmetic and copies ran while one was open for 1% -> 0% of each run, Pallas kernels for 0% -> 28%
where the time goes in v2:
time: 185 us; the launch traced here: 184 us
  waiting for transfers between devices  84.4 us (46%)
  Pallas kernels  61.1 us (33%)
  starting transfers between devices  30.5 us (16%)
  local copies, waits for them, and re-layouts  6.4 us (3%)
    ppermute x15, waiting for transfers between devices, move(): lax.ppermute(x, 'row', [(2 * source + y, 2 * target + y) for y in (0, 1)])  53.2 us
    pallas_call x3, Pallas kernels, update(): pl.pallas_call(lambda *refs: update_kernel(plan, flips, tile, len(args),...  33.8 us
    ppermute x5, waiting for transfers between devices, share(): return (mine, lax.ppermute(mine, 'row', swap))  17.8 us
    ppermute x15, starting transfers between devices, move(): lax.ppermute(x, 'row', [(2 * source + y, 2 * target + y) for y in (0, 1)])  17.1 us
    pallas_call x5, Pallas kernels, pick(): pl.pallas_call(lambda *refs: pick_kernel(levels, *refs), out_shape=struct...  8.96 us
    ppermute x1, waiting for transfers between devices, forward_substitution(): inv_other = lax.ppermute(inv, 'row', swap)  7.66 us
    unnamed x49, local copies, waits for them, and re-layouts  6.4 us
    pallas_call x1, Pallas kernels, forward_substitution(): pl.pallas_call(inverse_kernel, out_shape=struct(size, size), in_specs=[AN...  6.33 us
  transfers between devices with their start and end apart: 30, of which 8 were waited for; matrix products, arithmetic and copies ran while one was open for 0% of the time, Pallas kernels for 28%

profile of v2, /device:TPU:0, one launch (start us, length us, event | category | flops | bytes accessed | tf_op | source)
XLA Modules:
  0.0 183.7 jit_solution(7561004614108682802)
XLA Ops:
  0.6 3.0 %collective-permute-start.22 = (f32[2048,512]{1,0:T(8,128)}, f32[2048,512]{1,0:T(8,128)}, u32[]{:S(2)}, u32[]{:S(2)}) collective-permute-start(f32[2048,512]{1,0:T(8,128)} %refs_6_.11), channel_id=1, source_target_pairs={{0,2},{1,3},{2,0},{3,1},{4,6},{5,7},{6,4},{7,5},{8,10},{9,11},{10,... | collective-permute-start | bytes 12582920 | tf_op jit(solution)/shard_map/ppermute | solution.py:424
  3.6 2.2 %shard_map.68 = (f32[256,256]{1,0:T(8,128)}, f32[256,256]{1,0:T(8,128)}, f32[256,256]{1,0:T(8,128)}) custom-call(f32[256,512]{1,0:T(8,128)} %z_ref.1, f32[256,2048]{1,0:T(8,128)} %refs_6_.9), custom_call_target="tpu_custom_call" | custom-call | flops 1 | bytes 1 | tf_op jit(solution)/shard_map/pallas_call | solution.py:313
  5.9 1.6 collective-permute-start
  7.4 6.3 %shard_map.69.refs_2_ = f32[256,256]{1,0:T(8,128)} custom-call(f32[256,2048]{1,0:T(8,128)} %refs_6_.9, f32[256,256]{1,0:T(8,128)} %get-tuple-element.14.token_ref), custom_call_target="tpu_custom_call" | custom-call | flops 1 | bytes 1 | tf_op jit(solution)/shard_map/pallas_call | solution.py:324
  13.8 0.6 collective-permute-start.1
  14.4 1.3 collective-permute-start.2
  15.6 7.7 %collective-permute-done.1.refs_3_.refs_1_ = f32[256,256]{1,0:T(8,128)S(1)} collective-permute-done((f32[256,256]{1,0:T(8,128)}, f32[256,256]{1,0:T(8,128)S(1)}, u32[]{:S(2)}, u32[]{:S(2)}) %collective-permute-start.1) | collective-permute-done | bytes 262176 | tf_op jit(solution)/shard_map/ppermute | solution.py:333
  23.3 0.0 collective-permute-done.refs_1_.refs_2_
  23.3 3.9 %collective-permute-done.2.refs_5_.refs_3_ = f32[256,256]{1,0:T(8,128)S(1)} collective-permute-done((f32[256,256]{1,0:T(8,128)}, f32[256,256]{1,0:T(8,128)S(1)}, u32[]{:S(2)}, u32[]{:S(2)}) %collective-permute-start.2) | collective-permute-done | bytes 262176 | tf_op jit(solution)/shard_map/ppermute | solution.py:323
  27.2 0.7 copy-done.3
  27.9 1.7 shard_map.71
  29.5 0.7 collective-permute-start.4
  30.2 3.5 %shard_map.70.token_ref.refs_10_.refs_0_ = f32[256,512]{1,0:T(8,128)} custom-call(f32[256,256]{1,0:T(8,128)} %get-tuple-element.13.refs_0_, f32[256,256]{1,0:T(8,128)} %copy-done.1, f32[256,256]{1,0:T(8,128)} %shard_map.69.refs_2_, f32[256,256]{1,0:T(8,128)} %copy-done.2, f32[256,256]{1,0:T(8,128)} %get-tuple-element.15.refs_4_, f32[256,256]{1,0:T(8,128)} %copy-done.3, ...), custom_call_target="tpu_custom_call" | custom-call | flops 1 | bytes 1 | tf_op jit(solution)/shard_map/pallas_call | solution.py:342
  33.7 2.1 %collective-permute-start.3 = (f32[256,512]{1,0:T(8,128)}, f32[256,512]{1,0:T(8,128)S(1)}, u32[]{:S(2)}, u32[]{:S(2)}) collective-permute-start(f32[256,512]{1,0:T(8,128)} %shard_map.70.token_ref.refs_10_.refs_0_), channel_id=1, source_target_pairs={{0,8},{4,12},{1,9},{5,13},{2,10},{6,14},{3,11},{7,15}} | collective-permute-start | bytes 1572872 | tf_op jit(solution)/shard_map/ppermute | solution.py:300
  35.9 0.7 copy.11.x_ref
  36.6 1.7 collective-permute-done.5.refs_9_.refs_10_.refs_11_
  38.4 7.6 %collective-permute-done.3.refs_7_.refs_1_ = f32[256,512]{1,0:T(8,128)S(1)} collective-permute-done((f32[256,512]{1,0:T(8,128)}, f32[256,512]{1,0:T(8,128)S(1)}, u32[]{:S(2)}, u32[]{:S(2)}) %collective-permute-start.3) | collective-permute-done | bytes 524320 | tf_op jit(solution)/shard_map/ppermute | solution.py:300
  45.9 0.8 copy-done.12
  46.8 0.9 shard_map.73.refs_1_.refs_13_
  47.7 1.9 %shard_map.74 = f32[128,1024]{1,0:T(8,128)} custom-call(f32[256,2048]{1,0:T(8,128)} %refs_6_.9, f32[256,512]{1,0:T(8,128)} %shard_map.73.refs_1_.refs_13_), custom_call_target="tpu_custom_call" | custom-call | flops 1 | bytes 1 | tf_op jit(solution)/shard_map/pallas_call | solution.py:303
  49.6 0.7 collective-permute-start.8
  50.3 1.5 collective-permute-start.7
  51.8 0.7 collective-permute-start.6
  52.5 0.1 collective-permute-start.9
  52.6 1.3 collective-permute-start.13
  53.9 1.5 collective-permute-start.12
  55.4 1.4 collective-permute-start.11
  56.8 0.8 copy-done.9
  57.6 0.9 shard_map.75.refs_4_.refs_2_
  58.5 0.7 collective-permute-start.10
  59.2 15.1 %collective-permute-done.13.refs_0_ = f32[256,512]{1,0:T(8,128)} collective-permute-done((f32[256,512]{1,0:T(8,128)}, f32[256,512]{1,0:T(8,128)}, u32[]{:S(2)}, u32[]{:S(2)}) %collective-permute-start.13) | collective-permute-done | bytes 524320 | tf_op jit(solution)/shard_map/ppermute | solution.py:300
  74.4 0.7 collective-permute-start.18
  75.1 1.3 collective-permute-start.17
  76.4 1.9 %shard_map.76.refs_4_.refs_0_ = f32[256,512]{1,0:T(8,128)} custom-call(f32[256,512]{1,0:T(8,128)} %shard_map.70.token_ref.refs_10_.refs_0_, f32[256,512]{1,0:T(8,128)} %copy-done.12, f32[256,512]{1,0:T(8,128)} %collective-permute-done.7.refs_8_.refs_2_, f32[256,512]{1,0:T(8,128)} %collective-permute-done.12.refs_3_.refs_9_, f32[256,512]{1,0:T(8,128)} %shard_map.75.refs_4_.refs_2_), custom_call_target="tpu_custom_call" | custom-call | flops 1 | bytes 1 | tf_op jit(solution)/shard_map/pallas_call | solution.py:361
  78.3 0.1 collective-permute-start.21
  78.3 1.9 %shard_map.77.refs_14_.refs_2_ = f32[256,512]{1,0:T(8,128)} custom-call(f32[256,512]{1,0:T(8,128)} %collective-permute-done.13.refs_0_, f32[256,512]{1,0:T(8,128)} %shard_map.73.refs_1_.refs_13_, f32[256,512]{1,0:T(8,128)} %copy-done.10, f32[256,512]{1,0:T(8,128)} %collective-permute-done.11.refs_3_.refs_8_, f32[256,512]{1,0:T(8,128)} %shard_map.76.refs_4_.refs_0_), custom_call_target="tpu_custom_call" | custom-call | flops 1 | bytes 1 | tf_op jit(solution)/shard_map/pallas_call | solution.py:361
  80.2 0.0 copy-start.11
  80.2 0.8 copy-done.11
  81.0 0.9 shard_map.78
  82.0 30.5 %collective-permute-done.17.refs_0_ = f32[256,512]{1,0:T(8,128)} collective-permute-done((f32[256,512]{1,0:T(8,128)}, f32[256,512]{1,0:T(8,128)}, u32[]{:S(2)}, u32[]{:S(2)}) %collective-permute-start.17) | collective-permute-done | bytes 524320 | tf_op jit(solution)/shard_map/ppermute | solution.py:300
  112.5 1.9 %shard_map.79.token_ref.refs_4_.refs_0_ = f32[256,512]{1,0:T(8,128)} custom-call(f32[256,512]{1,0:T(8,128)} %collective-permute-done.17.refs_0_, f32[256,512]{1,0:T(8,128)} %copy-done.17, f32[256,512]{1,0:T(8,128)} %shard_map.75.refs_4_.refs_2_, f32[256,512]{1,0:T(8,128)} %copy-done.11, f32[128,512]{1,0:T(8,128)} %get-tuple-element.16.refs_4_.refs_3_), custom_call_target="tpu_custom_call" | custom-call | flops 1 | bytes 1 | tf_op jit(solution)/shard_map/pallas_call | solution.py:361
  114.5 0.1 collective-permute-start.23
  114.5 0.9 copy-done.4
  115.4 1.1 collective-permute-start.20
  116.6 0.7 collective-permute-start.14
  117.3 0.9 collective-permute-start.19
  118.2 12.1 %collective-permute-done.20.refs_3_ = f32[256,512]{1,0:T(8,128)S(1)} collective-permute-done((f32[256,512]{1,0:T(8,128)S(1)}, f32[256,512]{1,0:T(8,128)S(1)}, u32[]{:S(2)}, u32[]{:S(2)}) %collective-permute-start.20) | collective-permute-done | bytes 524320 | tf_op jit(solution)/shard_map/ppermute | solution.py:377
  130.3 0.7 collective-permute-start.25
  131.0 1.4 collective-permute-start.15
  132.4 0.7 collective-permute-start.26
  133.0 1.3 collective-permute-start.16
  134.3 5.8 %collective-permute-done.19.refs_1_ = f32[256,512]{1,0:T(8,128)S(1)} collective-permute-done((f32[256,512]{1,0:T(8,128)S(1)}, f32[256,512]{1,0:T(8,128)S(1)}, u32[]{:S(2)}, u32[]{:S(2)}) %collective-permute-start.19) | collective-permute-done | bytes 524320 | tf_op jit(solution)/shard_map/ppermute | solution.py:377
  140.1 1.1 collective-permute-start.29
  141.3 1.3 collective-permute-start.27
  142.6 14.4 %shard_map.81 = (f32[1,512]{1,0:T(1,128)}, f32[2048,512]{1,0:T(8,128)}) custom-call(f32[256,512]{1,0:T(8,128)} %shard_map.76.refs_4_.refs_0_, f32[256,512]{1,0:T(8,128)} %copy-done.15, f32[256,512]{1,0:T(8,128)} %shard_map.77.refs_14_.refs_2_, f32[256,512]{1,0:T(8,128)} %copy-done.14, f32[1,512]{1,0:T(1,128)} %bitcast.2, f32[2048,512]{1,0:T(8,128)} %refs_5_.1, ...), custom_call_target="tpu_custom_call" | custom-call | flops 1 | bytes 1 | tf_op jit(solution)/shard_map/pallas_call | solution.py:449
  157.0 1.7 shard_map.82.refs_4_.refs_0_
  158.7 1.7 shard_map.83.refs_2_
  160.4 0.9 collective-permute-start.28
  161.4 1.1 collective-permute-start.24
  162.5 0.8 copy-done.16
  163.3 9.9 %shard_map.84 = (f32[1,512]{1,0:T(1,128)}, f32[2048,512]{1,0:T(8,128)}) custom-call(f32[256,512]{1,0:T(8,128)} %shard_map.79.token_ref.refs_4_.refs_0_, f32[256,512]{1,0:T(8,128)} %copy-done.16, f32[1,512]{1,0:T(1,128)} %get-tuple-element.17.refs_5_.refs_2_, f32[2048,512]{1,0:T(8,128)} %get-tuple-element.19.refs_3_, ...), custom_call_target="tpu_custom_call", output_to_operand_aliasing={{1}: (3, {})} | custom-call | flops 1 | bytes 1 | tf_op jit(solution)/shard_map/pallas_call | solution.py:449
  173.2 0.7 copy-done.18
  173.9 0.1 copy-done.19
  174.0 9.6 %shard_map.85 = (f32[1,512]{1,0:T(1,128)}, f32[2048,512]{1,0:T(8,128)}) custom-call(f32[128,512]{1,0:T(8,128)} %shard_map.82.refs_4_.refs_0_, f32[128,512]{1,0:T(8,128)} %copy-done.19, f32[128,512]{1,0:T(8,128)} %shard_map.83.refs_2_, f32[128,512]{1,0:T(8,128)} %copy-done.18, f32[1,512]{1,0:T(1,128)} %get-tuple-element.20.refs_4_, ...), custom_call_target="tpu_custom_call", output_to_operand_aliasing={{1}: (5, {})} | custom-call | flops 1 | bytes 1 | tf_op jit(solution)/shard_map/pallas_call | solution.py:449
  (63 shorter events, 0.1 us)
Async XLA Ops:
  0.6 113.8 %collective-permute-start.22 = (f32[2048,512]{1,0:T(8,128)}, f32[2048,512]{1,0:T(8,128)}, u32[]{:S(2)}, u32[]{:S(2)}) collective-permute-start(f32[2048,512]{1,0:T(8,128)} %refs_6_.11), channel_id=1, source_target_pairs={{0,2},{1,3},{2,0},{3,1},{4,6},{5,7},{6,4},{7,5},{8,10},{9,11},{10,... | collective-permute-start | bytes 12582920 | tf_op jit(solution)/shard_map/ppermute | solution.py:424
  5.9 17.4 %collective-permute-start = (f32[256,256]{1,0:T(8,128)}, f32[256,256]{1,0:T(8,128)S(1)}, u32[]{:S(2)}, u32[]{:S(2)}) collective-permute-start(f32[256,256]{1,0:T(8,128)} %get-tuple-element.14.token_ref), channel_id=1, source_target_pairs={{0,4},{4,0},{8,12},{12,8},{16,20},{20,16},{24,28},{28,24},{1,5},{5... | collective-permute-start | bytes 786440 | tf_op jit(solution)/shard_map/ppermute | solution.py:322
  13.8 9.5 %collective-permute-start.1 = (f32[256,256]{1,0:T(8,128)}, f32[256,256]{1,0:T(8,128)S(1)}, u32[]{:S(2)}, u32[]{:S(2)}) collective-permute-start(f32[256,256]{1,0:T(8,128)} %shard_map.69.refs_2_), channel_id=1, source_target_pairs={{0,4},{4,0},{8,12},{12,8},{16,20},{20,16},{24,28},{28,24},{1,5},{5... | collective-permute-start | bytes 786440 | tf_op jit(solution)/shard_map/ppermute | solution.py:333
  14.4 12.8 %collective-permute-start.2 = (f32[256,256]{1,0:T(8,128)}, f32[256,256]{1,0:T(8,128)S(1)}, u32[]{:S(2)}, u32[]{:S(2)}) collective-permute-start(f32[256,256]{1,0:T(8,128)} %get-tuple-element.15.refs_4_), channel_id=1, source_target_pairs={{4,0},{12,8},{20,16},{28,24},{5,1},{13,9},{21,17},{29,25},{6,2},{1... | collective-permute-start | bytes 786440 | tf_op jit(solution)/shard_map/ppermute | solution.py:323
  23.3 3.9 %copy-start.2 = (f32[256,256]{1,0:T(8,128)}, f32[256,256]{1,0:T(8,128)S(1)}, u32[]{:S(2)}) copy-start(f32[256,256]{1,0:T(8,128)S(1)} %collective-permute-done.1.refs_3_.refs_1_) | copy-start | bytes 786436
  23.3 3.9 %copy-start.1 = (f32[256,256]{1,0:T(8,128)}, f32[256,256]{1,0:T(8,128)S(1)}, u32[]{:S(2)}) copy-start(f32[256,256]{1,0:T(8,128)S(1)} %collective-permute-done.refs_1_.refs_2_) | copy-start | bytes 786436
  27.2 0.7 copy-start.3
  29.5 6.3 %collective-permute-start.4 = (f32[128,512]{1,0:T(8,128)}, f32[128,512]{1,0:T(8,128)S(1)}, u32[]{:S(2)}, u32[]{:S(2)}) collective-permute-start(f32[128,512]{1,0:T(8,128)} %shard_map.71), channel_id=1, source_target_pairs={{8,12},{12,8},{16,20},{20,16},{24,28},{28,24},{9,13},{13,9},{17,21... | collective-permute-start | bytes 786440 | tf_op jit(solution)/shard_map/ppermute | solution.py:334
  33.7 12.2 %collective-permute-start.3 = (f32[256,512]{1,0:T(8,128)}, f32[256,512]{1,0:T(8,128)S(1)}, u32[]{:S(2)}, u32[]{:S(2)}) collective-permute-start(f32[256,512]{1,0:T(8,128)} %shard_map.70.token_ref.refs_10_.refs_0_), channel_id=1, source_target_pairs={{0,8},{4,12},{1,9},{5,13},{2,10},{6,14},{3,11},{7,15}} | collective-permute-start | bytes 1572872 | tf_op jit(solution)/shard_map/ppermute | solution.py:300
  35.9 10.1 %copy-start.6 = (f32[128,512]{1,0:T(8,128)}, f32[128,512]{1,0:T(8,128)S(1)}, u32[]{:S(2)}) copy-start(f32[128,512]{1,0:T(8,128)S(1)} %collective-permute-done.4.refs_8_.refs_9_.refs_10_) | copy-start | bytes 786436
  36.6 1.7 collective-permute-start.5
  38.4 7.6 %copy-start.7 = (f32[128,512]{1,0:T(8,128)}, f32[128,512]{1,0:T(8,128)S(1)}, u32[]{:S(2)}) copy-start(f32[128,512]{1,0:T(8,128)S(1)} %collective-permute-done.5.refs_9_.refs_10_.refs_11_) | copy-start | bytes 786436
  45.9 0.8 copy-start.12
  49.6 2.9 %collective-permute-start.8 = (f32[128,1024]{1,0:T(8,128)}, f32[128,1024]{1,0:T(8,128)S(1)}, u32[]{:S(2)}, u32[]{:S(2)}) collective-permute-start(f32[128,1024]{1,0:T(8,128)} %shard_map.74), channel_id=1, source_target_pairs={{16,20},{20,16},{24,28},{28,24},{17,21},{21,17},{25,29},{29,25},{1... | collective-permute-start | bytes 1572872 | tf_op jit(solution)/shard_map/ppermute | solution.py:397
  50.3 3.6 %collective-permute-start.7 = (f32[256,512]{1,0:T(8,128)}, f32[256,512]{1,0:T(8,128)}, u32[]{:S(2)}, u32[]{:S(2)}) collective-permute-start(f32[256,512]{1,0:T(8,128)} %copy-done.12), channel_id=1, source_target_pairs={{8,16},{12,20},{9,17},{13,21},{10,18},{14,22},{11,19},{15,23}} | collective-permute-start | bytes 1572872 | tf_op jit(solution)/shard_map/ppermute | solution.py:300
  51.8 3.6 %collective-permute-start.6 = (f32[256,512]{1,0:T(8,128)}, f32[256,512]{1,0:T(8,128)S(1)}, u32[]{:S(2)}, u32[]{:S(2)}) collective-permute-start(f32[256,512]{1,0:T(8,128)} %shard_map.73.refs_1_.refs_13_), channel_id=1, source_target_pairs={{8,16},{12,20},{9,17},{13,21},{10,18},{14,22},{11,19},{15,23}} | collective-permute-start | bytes 1572872 | tf_op jit(solution)/shard_map/ppermute | solution.py:300
  52.5 4.3 %copy-start.8 = (f32[128,1024]{1,0:T(8,128)}, f32[128,1024]{1,0:T(8,128)S(1)}, u32[]{:S(2)}) copy-start(f32[128,1024]{1,0:T(8,128)S(1)} %collective-permute-done.8.refs_11_.refs_12_) | copy-start | bytes 1572868
  52.5 4.3 %collective-permute-start.9 = (f32[128,1024]{1,0:T(8,128)S(1)}, f32[128,1024]{1,0:T(8,128)S(1)}, u32[]{:S(2)}, u32[]{:S(2)}) collective-permute-start(f32[128,1024]{1,0:T(8,128)S(1)} %collective-permute-done.8.refs_11_.refs_12_), channel_id=1, source_target_pairs={{0,1},{1,0},{2,3},{3,2},{4,5},{5,4},{6,7},{7,6},{8,9},{9,8},{10,11... | collective-permute-start | bytes 1572872 | tf_op jit(solution)/shard_map/ppermute | solution.py:399
  52.6 21.8 %collective-permute-start.13 = (f32[256,512]{1,0:T(8,128)}, f32[256,512]{1,0:T(8,128)}, u32[]{:S(2)}, u32[]{:S(2)}) collective-permute-start(f32[256,512]{1,0:T(8,128)} %shard_map.73.refs_1_.refs_13_), channel_id=1, source_target_pairs={{8,0},{12,4},{9,1},{13,5},{10,2},{14,6},{11,3},{15,7}} | collective-permute-start | bytes 1572872 | tf_op jit(solution)/shard_map/ppermute | solution.py:300
  53.9 21.2 %collective-permute-start.12 = (f32[256,512]{1,0:T(8,128)}, f32[256,512]{1,0:T(8,128)}, u32[]{:S(2)}, u32[]{:S(2)}) collective-permute-start(f32[256,512]{1,0:T(8,128)} %collective-permute-done.7.refs_8_.refs_2_), channel_id=1, source_target_pairs={{16,24},{20,28},{17,25},{21,29},{18,26},{22,30},{19,27},{23,31}} | collective-permute-start | bytes 1572872 | tf_op jit(solution)/shard_map/ppermute | solution.py:300
  55.4 1.5 copy-start.10
  55.4 22.9 %collective-permute-start.11 = (f32[256,512]{1,0:T(8,128)S(1)}, f32[256,512]{1,0:T(8,128)}, u32[]{:S(2)}, u32[]{:S(2)}) collective-permute-start(f32[256,512]{1,0:T(8,128)S(1)} %collective-permute-done.6.refs_7_.refs_2_), channel_id=1, source_target_pairs={{16,24},{20,28},{17,25},{21,29},{18,26},{22,30},{19,27},{23,31}} | collective-permute-start | bytes 1572872 | tf_op jit(solution)/shard_map/ppermute | solution.py:300
  56.8 0.8 copy-start.9
  58.5 21.7 %collective-permute-start.10 = (f32[256,512]{1,0:T(8,128)}, f32[256,512]{1,0:T(8,128)S(1)}, u32[]{:S(2)}, u32[]{:S(2)}) collective-permute-start(f32[256,512]{1,0:T(8,128)} %shard_map.75.refs_4_.refs_2_), channel_id=1, source_target_pairs={{16,24},{20,28},{17,25},{21,29},{18,26},{22,30},{19,27},{23,31}} | collective-permute-start | bytes 1572872 | tf_op jit(solution)/shard_map/ppermute | solution.py:300
  74.4 7.6 %collective-permute-start.18 = (f32[256,512]{1,0:T(8,128)}, f32[256,512]{1,0:T(8,128)S(1)}, u32[]{:S(2)}, u32[]{:S(2)}) collective-permute-start(f32[256,512]{1,0:T(8,128)} %shard_map.75.refs_4_.refs_2_), channel_id=1, source_target_pairs={{16,8},{20,12},{17,9},{21,13},{18,10},{22,14},{19,11},{23,15}} | collective-permute-start | bytes 1572872 | tf_op jit(solution)/shard_map/ppermute | solution.py:300
  75.1 37.4 %collective-permute-start.17 = (f32[256,512]{1,0:T(8,128)}, f32[256,512]{1,0:T(8,128)}, u32[]{:S(2)}, u32[]{:S(2)}) collective-permute-start(f32[256,512]{1,0:T(8,128)} %shard_map.75.refs_4_.refs_2_), channel_id=1, source_target_pairs={{16,0},{20,4},{17,1},{21,5},{18,2},{22,6},{19,3},{23,7}} | collective-permute-start | bytes 1572872 | tf_op jit(solution)/shard_map/ppermute | solution.py:300
  78.3 64.3 %collective-permute-start.21 = (f32[2048,512]{1,0:T(8,128)}, f32[2048,512]{1,0:T(8,128)}, u32[]{:S(2)}, u32[]{:S(2)}) collective-permute-start(f32[2048,512]{1,0:T(8,128)} %refs_6_.11), channel_id=1, source_target_pairs={{0,1},{1,0},{2,3},{3,2},{4,5},{5,4},{6,7},{7,6},{8,9},{9,8},{10,11... | collective-permute-start | bytes 12582920 | tf_op jit(solution)/shard_map/ppermute | solution.py:424
  80.2 0.8 copy-start.11
  82.0 30.5 %copy-start.17 = (f32[256,512]{1,0:T(8,128)}, f32[256,512]{1,0:T(8,128)S(1)}, u32[]{:S(2)}) copy-start(f32[256,512]{1,0:T(8,128)S(1)} %collective-permute-done.18.refs_1_) | copy-start | bytes 1572868
  114.4 1.0 copy-start.4
  114.4 2.2 %copy-start.13 = (f32[128,512]{1,0:T(8,128)S(1)}, f32[128,512]{1,0:T(8,128)}, u32[]{:S(2)}) copy-start(f32[128,512]{1,0:T(8,128)} %get-tuple-element.16.refs_4_.refs_3_) | copy-start | bytes 786436
  114.4 2.8 %copy-start.5 = (f32[256,512]{1,0:T(8,128)S(1)}, f32[256,512]{1,0:T(8,128)}, u32[]{:S(2)}) copy-start(f32[256,512]{1,0:T(8,128)} %shard_map.76.refs_4_.refs_0_) | copy-start | bytes 1572868
  114.4 15.9 %copy-start.20 = (f32[128,512]{1,0:T(8,128)S(1)}, f32[128,512]{1,0:T(8,128)}, u32[]{:S(2)}) copy-start(f32[128,512]{1,0:T(8,128)} %get-tuple-element.18.refs_3_) | copy-start | bytes 786436
  114.4 25.7 %copy-start = (f32[256,512]{1,0:T(8,128)S(1)}, f32[256,512]{1,0:T(8,128)}, u32[]{:S(2)}) copy-start(f32[256,512]{1,0:T(8,128)} %shard_map.79.token_ref.refs_4_.refs_0_) | copy-start | bytes 1572868
  114.5 28.1 %collective-permute-start.23 = (f32[2048,512]{1,0:T(8,128)}, f32[2048,512]{1,0:T(8,128)}, u32[]{:S(2)}, u32[]{:S(2)}) collective-permute-start(f32[2048,512]{1,0:T(8,128)} %shard_map.80.refs_8_.refs_6_), channel_id=1, source_target_pairs={{0,1},{1,0},{2,3},{3,2},{4,5},{5,4},{6,7},{7,6},{8,9},{9,8},{10,11... | collective-permute-start | bytes 12582920 | tf_op jit(solution)/shard_map/ppermute | solution.py:424
  115.4 14.8 %collective-permute-start.20 = (f32[256,512]{1,0:T(8,128)S(1)}, f32[256,512]{1,0:T(8,128)S(1)}, u32[]{:S(2)}, u32[]{:S(2)}) collective-permute-start(f32[256,512]{1,0:T(8,128)S(1)} %copy-done.4), channel_id=1, source_target_pairs={{0,4},{4,0},{8,12},{12,8},{16,20},{20,16},{24,28},{28,24},{1,5},{5... | collective-permute-start | bytes 1572872 | tf_op jit(solution)/shard_map/ppermute | solution.py:377
  116.6 14.4 %collective-permute-start.14 = (f32[128,512]{1,0:T(8,128)S(1)}, f32[128,512]{1,0:T(8,128)S(1)}, u32[]{:S(2)}, u32[]{:S(2)}) collective-permute-start(f32[128,512]{1,0:T(8,128)S(1)} %copy-done.13), channel_id=1, source_target_pairs={{24,16},{28,20},{25,17},{29,21},{26,18},{30,22},{27,19},{31,23}} | collective-permute-start | bytes 786440 | tf_op jit(solution)/shard_map/ppermute | solution.py:300
  117.3 22.8 %collective-permute-start.19 = (f32[256,512]{1,0:T(8,128)S(1)}, f32[256,512]{1,0:T(8,128)S(1)}, u32[]{:S(2)}, u32[]{:S(2)}) collective-permute-start(f32[256,512]{1,0:T(8,128)S(1)} %copy-done.5), channel_id=1, source_target_pairs={{0,4},{4,0},{8,12},{12,8},{16,20},{20,16},{24,28},{28,24},{1,5},{5... | collective-permute-start | bytes 1572872 | tf_op jit(solution)/shard_map/ppermute | solution.py:377
  130.3 12.3 %copy-start.14 = (f32[256,512]{1,0:T(8,128)}, f32[256,512]{1,0:T(8,128)S(1)}, u32[]{:S(2)}) copy-start(f32[256,512]{1,0:T(8,128)S(1)} %collective-permute-done.20.refs_3_) | copy-start | bytes 1572868
  130.3 2.1 %collective-permute-start.25 = (f32[128,512]{1,0:T(8,128)S(1)}, f32[128,512]{1,0:T(8,128)S(1)}, u32[]{:S(2)}, u32[]{:S(2)}) collective-permute-start(f32[128,512]{1,0:T(8,128)S(1)} %copy-done.20), channel_id=1, source_target_pairs={{24,16},{28,20},{25,17},{29,21},{26,18},{30,22},{27,19},{31,23}} | collective-permute-start | bytes 786440 | tf_op jit(solution)/shard_map/ppermute | solution.py:300
  131.0 10.3 %copy-start.21 = (f32[128,512]{1,0:T(8,128)}, f32[128,512]{1,0:T(8,128)S(1)}, u32[]{:S(2)}) copy-start(f32[128,512]{1,0:T(8,128)S(1)} %collective-permute-done.14.refs_2_) | copy-start | bytes 786436
  131.0 2.1 %collective-permute-start.15 = (f32[128,512]{1,0:T(8,128)S(1)}, f32[128,512]{1,0:T(8,128)}, u32[]{:S(2)}, u32[]{:S(2)}) collective-permute-start(f32[128,512]{1,0:T(8,128)S(1)} %collective-permute-done.14.refs_2_), channel_id=1, source_target_pairs={{16,8},{20,12},{17,9},{21,13},{18,10},{22,14},{19,11},{23,15}} | collective-permute-start | bytes 786440 | tf_op jit(solution)/shard_map/ppermute | solution.py:300
  132.3 10.2 %copy-start.22 = (f32[128,512]{1,0:T(8,128)}, f32[128,512]{1,0:T(8,128)S(1)}, u32[]{:S(2)}) copy-start(f32[128,512]{1,0:T(8,128)S(1)} %collective-permute-done.25.refs_2_) | copy-start | bytes 786436
  132.4 8.9 %collective-permute-start.26 = (f32[128,512]{1,0:T(8,128)S(1)}, f32[128,512]{1,0:T(8,128)S(1)}, u32[]{:S(2)}, u32[]{:S(2)}) collective-permute-start(f32[128,512]{1,0:T(8,128)S(1)} %collective-permute-done.25.refs_2_), channel_id=1, source_target_pairs={{16,8},{20,12},{17,9},{21,13},{18,10},{22,14},{19,11},{23,15}} | collective-permute-start | bytes 786440 | tf_op jit(solution)/shard_map/ppermute | solution.py:300
  133.0 24.0 %collective-permute-start.16 = (f32[128,512]{1,0:T(8,128)}, f32[128,512]{1,0:T(8,128)}, u32[]{:S(2)}, u32[]{:S(2)}) collective-permute-start(f32[128,512]{1,0:T(8,128)} %collective-permute-done.15.refs_1_), channel_id=1, source_target_pairs={{8,0},{12,4},{9,1},{13,5},{10,2},{14,6},{11,3},{15,7}} | collective-permute-start | bytes 786440 | tf_op jit(solution)/shard_map/ppermute | solution.py:300
  140.1 1.2 copy-start.15
  140.1 22.4 %collective-permute-start.29 = (f32[256,512]{1,0:T(8,128)S(1)}, f32[256,512]{1,0:T(8,128)S(1)}, u32[]{:S(2)}, u32[]{:S(2)}) collective-permute-start(f32[256,512]{1,0:T(8,128)S(1)} %copy-done), channel_id=1, source_target_pairs={{0,4},{4,0},{8,12},{12,8},{16,20},{20,16},{24,28},{28,24},{1,5},{5... | collective-permute-start | bytes 1572872 | tf_op jit(solution)/shard_map/ppermute | solution.py:377
  141.3 15.7 %copy-start.23 = (f32[128,512]{1,0:T(8,128)}, f32[128,512]{1,0:T(8,128)S(1)}, u32[]{:S(2)}) copy-start(f32[128,512]{1,0:T(8,128)S(1)} %collective-permute-done.26.refs_1_) | copy-start | bytes 786436
  141.3 17.5 %collective-permute-start.27 = (f32[128,512]{1,0:T(8,128)S(1)}, f32[128,512]{1,0:T(8,128)}, u32[]{:S(2)}, u32[]{:S(2)}) collective-permute-start(f32[128,512]{1,0:T(8,128)S(1)} %collective-permute-done.26.refs_1_), channel_id=1, source_target_pairs={{8,0},{12,4},{9,1},{13,5},{10,2},{14,6},{11,3},{15,7}} | collective-permute-start | bytes 786440 | tf_op jit(solution)/shard_map/ppermute | solution.py:300
  160.4 12.8 %collective-permute-start.28 = (f32[128,512]{1,0:T(8,128)}, f32[128,512]{1,0:T(8,128)S(1)}, u32[]{:S(2)}, u32[]{:S(2)}) collective-permute-start(f32[128,512]{1,0:T(8,128)} %shard_map.83.refs_2_), channel_id=1, source_target_pairs={{0,4},{4,0},{8,12},{12,8},{16,20},{20,16},{24,28},{28,24},{1,5},{5... | collective-permute-start | bytes 786440 | tf_op jit(solution)/shard_map/ppermute | solution.py:377
  161.4 11.8 %collective-permute-start.24 = (f32[128,512]{1,0:T(8,128)}, f32[128,512]{1,0:T(8,128)S(1)}, u32[]{:S(2)}, u32[]{:S(2)}) collective-permute-start(f32[128,512]{1,0:T(8,128)} %shard_map.82.refs_4_.refs_0_), channel_id=1, source_target_pairs={{0,4},{4,0},{8,12},{12,8},{16,20},{20,16},{24,28},{28,24},{1,5},{5... | collective-permute-start | bytes 786440 | tf_op jit(solution)/shard_map/ppermute | solution.py:377
  162.5 0.8 copy-start.16
  173.2 0.7 copy-start.18
  173.2 0.8 copy-start.19

commit v3 on v2

--- a/solution.py
+++ b/solution.py
@@ -15,8 +15,8 @@
 TINY = pl.CostEstimate(flops=1, bytes_accessed=1, transcendentals=0)
 
 
-def params():
-    return pltpu.CompilerParams(vmem_limit_bytes=LIMIT)
+def params(limit=LIMIT):
+    return pltpu.CompilerParams(vmem_limit_bytes=limit)
 
 
 def mul(a, b):
@@ -283,7 +283,7 @@
     return jax.ShapeDtypeStruct(shape, dtype)
 
 
-def forward_substitution(diag_block, z_panel):
+def forward_substitution(diag_block, z_panel, mate):
     rows = lax.axis_size("row")
     levels = rows // 2
     last = levels - 1
@@ -332,12 +332,12 @@
     )(diag_block, z_send)
     inv_other = lax.ppermute(inv, "row", swap)
     near_a = lax.ppermute(
-        strips([1], inv_other, z_other, corner_other), "row", [p for p in swap if p[0] >= 2])
+        strips([1], mate), "row", [p for p in swap if p[0] >= 2])
 
     def solve(turn, came, strip_pairs, token, n_out=1):
         args = [z_own, z_other, inv, inv_other, corner, corner_other, diag_block]
         args += [*came, *strip_pairs]
-        args += [token] if token is not None else []
+        args += token
         deep = max(turn, 1) * width
         return pl.pallas_call(
             lambda *refs: solve_kernel(turn, len(args), *refs),
@@ -364,13 +364,13 @@
             in_specs=[ANY] * (levels + len(tokens)),
             out_specs=VMEM,
             scratch_shapes=[dma((1,))],
-            compiler_params=params(),
+            compiler_params=params(8 * 1024 * 1024),
             cost_estimate=TINY,
         )(*args, *tokens)
 
     held, pieces = {}, {}
     strip_pairs = ()
-    token = None
+    token = []
 
     def share(level, index, tokens):
         mine = pick(pieces[level][index], *tokens)
@@ -382,32 +382,38 @@
             if turn < last:
                 held[k][turn + 1] = move(held[k][turn], turn, turn + 1)
         own = solve(turn, came, strip_pairs, token, RETURNS if turn == last else 1)
-        token = own[0]
+        token = [own[0]]
         if turn < last:
             held[turn] = {turn: own[0], turn + 1: move(own[0], turn, turn + 1)}
         pieces[turn] = []
         for part in own:
             place = {turn: part}
-            for z in range(turn - 1, -1, -1):
-                place[z] = move(place[z + 1], z + 1, z) if turn == last else move(part, turn, z)
+            if turn < last:
+                for z in range(turn - 1, -1, -1):
+                    place[z] = move(place[z + 1], z + 1, z)
             pieces[turn].append(place)
         if turn == 0:
-            strip_pairs = (near_a, lax.ppermute(tie(near_a, token), "col", cores))
+            strip_pairs = (near_a, lax.ppermute(tie(near_a, own[0]), "col", cores))
+            far_a = lax.ppermute(
+                strips(list(range(2, levels)), own[0]), "row", [p for p in swap if p[0] >= 4])
+            far_b = lax.ppermute(far_a, "col", cores)
         if turn == 1:
-            far_a = lax.ppermute(
-                strips(list(range(2, levels)), token), "row", [p for p in swap if p[0] >= 4])
-            strip_pairs += (far_a, lax.ppermute(far_a, "col", cores))
+            strip_pairs += (far_a, far_b)
         if turn == last - 1:
             for k in range(last - 1):
                 pieces[k][0].update(held[k])
-                shared = share(k, 0, [token])
+                shared = share(k, 0, token)
                 pieces[k] = [shared]
-                token = shared[0]
+                token = [shared[0]]
+            token.append(pieces[0][0][1])
+    for z in range(last - 1, -1, -1):
+        for place in pieces[last]:
+            place[z] = move(place[z + 1], z + 1, z)
     pieces[last - 1][0].update(held[last - 1])
-    shared = share(last - 1, 0, [token])
+    token.append(pieces[last - 2][0][1])
+    shared = share(last - 1, 0, token)
     pieces[last - 1] = [shared]
-    token = shared[0]
-    return pieces, share, token
+    return pieces, share, own[0], shared[1]
 
 
 def shards(diag_block, z_panel, panel_below, z_trail, norm_sq):
@@ -425,9 +431,9 @@
 
     crossed = {flip: flipped(panel_below, flip) for flip in range(2, cols, 2)}
     panels = {0: panel_below, 1: flipped(panel_below, 1)}
-    pieces, share, token = forward_substitution(diag_block, z_panel)
+    pieces, share, hold, token = forward_substitution(diag_block, z_panel, panels[1])
     for flip, x in crossed.items():
-        panels[flip] = tie(x, token)
+        panels[flip] = tie(x, hold)
         panels[flip ^ 1] = flipped(panels[flip], 1)
     flips = list(panels)
     slabs = [panels[flip] for flip in flips]
@@ -461,17 +467,16 @@
                 dma((rows // tile, span // depth)),
             ],
             input_output_aliases=aliases,
-            compiler_params=params(),
+            compiler_params=params(30 * 1024 * 1024),
             cost_estimate=TINY,
         )(*args)
 
-    norm, out = update(range(last - 1), norm_sq.reshape(1, wide), z_trail)
     pairs = []
     for index in range(RETURNS):
-        pairs.append(share(last, index, [token, norm]))
+        pairs.append(share(last, index, [token]))
         token = pairs[-1][0]
     pieces[last] = pairs
-    norm, out = update([last - 1], norm, out)
+    norm, out = update(range(last), norm_sq.reshape(1, wide), z_trail)
     norm, out = update([last], norm, out)
     return (norm.reshape(wide), out)
 

time: 185 us -> 172 us (0.930)
  Pallas kernels: 61.1 us -> 42.1 us
  waiting for transfers between devices: 84.4 us -> 88.9 us
    ppermute x3, waiting for transfers between devices: 0.01 us -> 17.4 us  [flipped(): return lax.ppermute(x, 'col', [(i, i ^ flip) for i in range(cols)])]
    ppermute x5, waiting for transfers between devices: 17.8 us -> 1.53 us  [share(): return (mine, lax.ppermute(mine, 'row', swap))]
    pallas_call x3 -> x2, Pallas kernels: 33.8 us -> 22.5 us  [update(): pl.pallas_call(lambda *refs: update_kernel(plan, flips, tile, len(args),...]
    pallas_call x5, Pallas kernels: 8.96 us -> 1.23 us  [pick(): pl.pallas_call(lambda *refs: pick_kernel(levels, *refs), out_shape=struct...]
    ppermute x15, waiting for transfers between devices: 53.2 us -> 56 us  [move(): lax.ppermute(x, 'row', [(2 * source + y, 2 * target + y) for y in (0, 1)])]
    unnamed x49 -> x37, local copies, waits for them, and re-layouts: 6.4 us -> 6.99 us
  transfers between devices with their start and end apart: 30 -> 30, of which waited for: 8 -> 10; matrix products, arithmetic and copies ran while one was open for 0% -> 0% of each run, Pallas kernels for 28% -> 20%
where the time goes in v3:
time: 172 us; the launch traced here: 171 us
  waiting for transfers between devices  88.9 us (52%)
  Pallas kernels  42.1 us (24%)
  starting transfers between devices  32.1 us (19%)
  local copies, waits for them, and re-layouts  6.99 us (4%)
    ppermute x15, waiting for transfers between devices, move(): lax.ppermute(x, 'row', [(2 * source + y, 2 * target + y) for y in (0, 1)])  56 us
    pallas_call x2, Pallas kernels, update(): pl.pallas_call(lambda *refs: update_kernel(plan, flips, tile, len(args),...  22.5 us
    ppermute x15, starting transfers between devices, move(): lax.ppermute(x, 'row', [(2 * source + y, 2 * target + y) for y in (0, 1)])  17.6 us
    ppermute x3, waiting for transfers between devices, flipped(): return lax.ppermute(x, 'col', [(i, i ^ flip) for i in range(cols)])  17.4 us
    ppermute x1, waiting for transfers between devices, forward_substitution(): inv_other = lax.ppermute(inv, 'row', swap)  7.61 us
    unnamed x37, local copies, waits for them, and re-layouts  6.99 us
    pallas_call x1, Pallas kernels, forward_substitution(): pl.pallas_call(inverse_kernel, out_shape=struct(size, size), in_specs=[AN...  6.33 us
    pallas_call x4, Pallas kernels, solve(): pl.pallas_call(lambda *refs: solve_kernel(turn, len(args), *refs), out_sh...  6.23 us
  transfers between devices with their start and end apart: 30, of which 10 were waited for; matrix products, arithmetic and copies ran while one was open for 0% of the time, Pallas kernels for 20%

profile of v3, /device:TPU:0, one launch (start us, length us, event | category | flops | bytes accessed | tf_op | source)
XLA Modules:
  0.0 171.2 jit_solution(13838637338185938918)
XLA Ops:
  0.6 0.5 collective-permute-start.4
  1.1 2.6 %collective-permute-start.28 = (f32[2048,512]{1,0:T(8,128)}, f32[2048,512]{1,0:T(8,128)}, u32[]{:S(2)}, u32[]{:S(2)}) collective-permute-start(f32[2048,512]{1,0:T(8,128)} %refs_6_.9), channel_id=1, source_target_pairs={{0,2},{1,3},{2,0},{3,1},{4,6},{5,7},{6,4},{7,5},{8,10},{9,11},{10,... | collective-permute-start | bytes 12582920 | tf_op jit(solution)/shard_map/ppermute | solution.py:430
  3.7 2.2 %shard_map.68 = (f32[256,256]{1,0:T(8,128)}, f32[256,256]{1,0:T(8,128)}, f32[256,256]{1,0:T(8,128)}) custom-call(f32[256,512]{1,0:T(8,128)} %z_ref.1, f32[256,2048]{1,0:T(8,128)} %refs_6_.8), custom_call_target="tpu_custom_call" | custom-call | flops 1 | bytes 1 | tf_op jit(solution)/shard_map/pallas_call | solution.py:313
  5.9 1.6 collective-permute-start
  7.5 6.3 %shard_map.69.refs_2_ = f32[256,256]{1,0:T(8,128)} custom-call(f32[256,2048]{1,0:T(8,128)} %refs_6_.8, f32[256,256]{1,0:T(8,128)} %get-tuple-element.12.token_ref), custom_call_target="tpu_custom_call" | custom-call | flops 1 | bytes 1 | tf_op jit(solution)/shard_map/pallas_call | solution.py:324
  13.9 0.6 collective-permute-start.1
  14.4 1.3 collective-permute-start.2
  15.7 7.6 %collective-permute-done.1.refs_3_ = f32[256,256]{1,0:T(8,128)S(1)} collective-permute-done((f32[256,256]{1,0:T(8,128)}, f32[256,256]{1,0:T(8,128)S(1)}, u32[]{:S(2)}, u32[]{:S(2)}) %collective-permute-start.1) | collective-permute-done | bytes 262176 | tf_op jit(solution)/shard_map/ppermute | solution.py:333
  23.3 0.0 collective-permute-done.refs_1_
  23.3 4.5 %collective-permute-done.2.refs_5_ = f32[256,256]{1,0:T(8,128)S(1)} collective-permute-done((f32[256,256]{1,0:T(8,128)}, f32[256,256]{1,0:T(8,128)S(1)}, u32[]{:S(2)}, u32[]{:S(2)}) %collective-permute-start.2) | collective-permute-done | bytes 262176 | tf_op jit(solution)/shard_map/ppermute | solution.py:323
  27.9 0.7 copy-done.15
  28.5 3.5 %shard_map.70.token_ref.refs_10_.refs_1_.refs_0_ = f32[256,512]{1,0:T(8,128)} custom-call(f32[256,256]{1,0:T(8,128)} %get-tuple-element.11.refs_0_, f32[256,256]{1,0:T(8,128)} %copy-done.13, f32[256,256]{1,0:T(8,128)} %shard_map.69.refs_2_, f32[256,256]{1,0:T(8,128)} %copy-done.14, f32[256,256]{1,0:T(8,128)} %get-tuple-element.13.refs_4_, ...), custom_call_target="tpu_custom_call" | custom-call | flops 1 | bytes 1 | tf_op jit(solution)/shard_map/pallas_call | solution.py:342
  32.0 2.1 %collective-permute-start.3 = (f32[256,512]{1,0:T(8,128)}, f32[256,512]{1,0:T(8,128)}, u32[]{:S(2)}, u32[]{:S(2)}) collective-permute-start(f32[256,512]{1,0:T(8,128)} %shard_map.70.token_ref.refs_10_.refs_1_.refs_0_), channel_id=1, source_target_pairs={{0,8},{4,12},{1,9},{5,13},{2,10},{6,14},{3,11},{7,15}} | collective-permute-start | bytes 1572872 | tf_op jit(solution)/shard_map/ppermute | solution.py:300
  34.1 1.7 shard_map.71
  35.8 0.7 collective-permute-start.5
  36.5 1.9 %shard_map.74 = f32[128,1024]{1,0:T(8,128)} custom-call(f32[256,2048]{1,0:T(8,128)} %refs_6_.8, f32[256,512]{1,0:T(8,128)} %shard_map.70.token_ref.refs_10_.refs_1_.refs_0_), custom_call_target="tpu_custom_call" | custom-call | flops 1 | bytes 1 | tf_op jit(solution)/shard_map/pallas_call | solution.py:303
  38.4 1.5 collective-permute-start.9
  39.9 4.5 %collective-permute-done.3.refs_7_.refs_1_ = f32[256,512]{1,0:T(8,128)} collective-permute-done((f32[256,512]{1,0:T(8,128)}, f32[256,512]{1,0:T(8,128)}, u32[]{:S(2)}, u32[]{:S(2)}) %collective-permute-start.3) | collective-permute-done | bytes 524320 | tf_op jit(solution)/shard_map/ppermute | solution.py:300
  44.4 0.7 collective-permute-start.8
  45.1 0.7 copy.10.x_ref
  45.8 1.7 %collective-permute-done.6.refs_9_.refs_10_.refs_11_ = f32[128,512]{1,0:T(8,128)S(1)} collective-permute-done((f32[128,512]{1,0:T(8,128)}, f32[128,512]{1,0:T(8,128)S(1)}, u32[]{:S(2)}, u32[]{:S(2)}) %collective-permute-start.6) | collective-permute-done | bytes 262176 | tf_op jit(solution)/shard_map/ppermute | solution.py:396
  47.6 0.7 copy-done.17
  48.3 0.9 shard_map.73.refs_13_.refs_1_
  49.1 0.0 copy-start.1
  49.2 1.6 collective-permute-start.7
  50.8 0.1 collective-permute-start.10
  51.0 1.4 collective-permute-start.13
  52.4 1.3 collective-permute-start.14
  53.7 1.5 collective-permute-start.12
  55.2 0.9 shard_map.75.refs_4_.refs_2_
  56.1 1.0 copy-done.8
  57.2 0.1 shard_map.76.refs_4_.refs_0_
  57.2 0.1 collective-permute-start.15
  57.3 1.5 collective-permute-start.11
  58.7 15.4 %collective-permute-done.14.refs_0_ = f32[256,512]{1,0:T(8,128)} collective-permute-done((f32[256,512]{1,0:T(8,128)}, f32[256,512]{1,0:T(8,128)}, u32[]{:S(2)}, u32[]{:S(2)}) %collective-permute-start.14) | collective-permute-done | bytes 524320 | tf_op jit(solution)/shard_map/ppermute | solution.py:300
  74.1 1.1 shard_map.77.refs_14_.refs_2_
  75.2 0.0 copy-start.3
  75.2 0.8 copy-done.3
  76.0 0.8 copy-done.9
  76.8 1.0 shard_map.78
  77.8 17.4 %collective-permute-done.28.x_ref = f32[2048,512]{1,0:T(8,128)} collective-permute-done((f32[2048,512]{1,0:T(8,128)}, f32[2048,512]{1,0:T(8,128)}, u32[]{:S(2)}, u32[]{:S(2)}) %collective-permute-start.28) | collective-permute-done | bytes 4194336 | tf_op jit(solution)/shard_map/ppermute | solution.py:430
  95.2 0.0 copy-start.12
  95.2 0.1 collective-permute-start.29
  95.3 0.8 collective-permute-start.19
  96.2 1.4 collective-permute-start.20
  97.6 1.9 %collective-permute-start.21 = (f32[256,512]{1,0:T(8,128)S(1)}, f32[256,512]{1,0:T(8,128)S(1)}, u32[]{:S(2)}, u32[]{:S(2)}) collective-permute-start(f32[256,512]{1,0:T(8,128)S(1)} %copy-done.4), channel_id=1, source_target_pairs={{0,4},{4,0},{8,12},{12,8},{16,20},{20,16},{24,28},{28,24},{1,5},{5... | collective-permute-start | bytes 1572872 | tf_op jit(solution)/shard_map/ppermute | solution.py:377
  99.4 0.7 collective-permute-start.16
  100.1 0.7 collective-permute-start.24
  100.8 0.7 collective-permute-start.17
  101.5 25.1 %collective-permute-done.20.refs_0_ = f32[256,512]{1,0:T(8,128)S(1)} collective-permute-done((f32[256,512]{1,0:T(8,128)S(1)}, f32[256,512]{1,0:T(8,128)S(1)}, u32[]{:S(2)}, u32[]{:S(2)}) %collective-permute-start.20) | collective-permute-done | bytes 524320 | tf_op jit(solution)/shard_map/ppermute | solution.py:300
  126.6 0.1 shard_map.79.refs_4_
  126.7 1.6 collective-permute-start.22
  128.3 0.7 collective-permute-start.25
  128.9 1.3 collective-permute-start.18
  130.2 1.3 collective-permute-start.26
  131.5 6.4 %collective-permute-done.18.refs_0_ = f32[128,512]{1,0:T(8,128)S(1)} collective-permute-done((f32[128,512]{1,0:T(8,128)S(1)}, f32[128,512]{1,0:T(8,128)S(1)}, u32[]{:S(2)}, u32[]{:S(2)}) %collective-permute-start.18) | collective-permute-done | bytes 262176 | tf_op jit(solution)/shard_map/ppermute | solution.py:300
  138.0 1.5 collective-permute-done.22.refs_4_.refs_5_
  139.6 4.6 %collective-permute-done.26.refs_0_ = f32[128,512]{1,0:T(8,128)S(1)} collective-permute-done((f32[128,512]{1,0:T(8,128)S(1)}, f32[128,512]{1,0:T(8,128)S(1)}, u32[]{:S(2)}, u32[]{:S(2)}) %collective-permute-start.26) | collective-permute-done | bytes 262176 | tf_op jit(solution)/shard_map/ppermute | solution.py:300
  144.2 0.6 collective-permute-start.27
  144.8 1.5 collective-permute-start.23
  146.3 0.0 copy-start.5
  146.4 2.2 %copy-done.5 = f32[2048,512]{1,0:T(8,128)S(1)} copy-done((f32[2048,512]{1,0:T(8,128)S(1)}, f32[2048,512]{1,0:T(8,128)}, u32[]{:S(2)}) %copy-start.5) | copy-done | bytes 4194328
  148.5 14.7 %shard_map.83 = (f32[1,512]{1,0:T(1,128)S(1)}, f32[2048,512]{1,0:T(8,128)}) custom-call(f32[256,512]{1,0:T(8,128)S(1)} %shard_map.76.refs_4_.refs_0_, f32[256,512]{1,0:T(8,128)S(1)} %copy-done.10, f32[256,512]{1,0:T(8,128)S(1)} %copy-done.4, f32[256,512]{1,0:T(8,128)S(1)} %collective-permute-done.21.refs_5_.refs_3_, f32[256,512]{1,0:T(8,128)S(1)} %shard_map.79.refs_4_, ...), custom_call_target="tpu_custom_call" | custom-call | flops 1 | bytes 1 | tf_op jit(solution)/shard_map/pallas_call | solution.py:455
  163.3 7.8 %shard_map.84 = (f32[1,512]{1,0:T(1,128)}, f32[2048,512]{1,0:T(8,128)}) custom-call(f32[128,512]{1,0:T(8,128)S(1)} %shard_map.80.refs_4_.refs_0_, f32[128,512]{1,0:T(8,128)S(1)} %collective-permute-done.23.refs_1_, f32[128,512]{1,0:T(8,128)S(1)} %shard_map.81.refs_2_, ...), custom_call_target="tpu_custom_call", output_to_operand_aliasing={{1}: (5, {})} | custom-call | flops 1 | bytes 1 | tf_op jit(solution)/shard_map/pallas_call | solution.py:455
  (50 shorter events, 0.2 us)
Async XLA Ops:
  0.6 33.5 %collective-permute-start.4 = (f32[2048,512]{1,0:T(8,128)}, f32[2048,512]{1,0:T(8,128)}, u32[]{:S(2)}, u32[]{:S(2)}) collective-permute-start(f32[2048,512]{1,0:T(8,128)} %refs_6_.9), channel_id=1, source_target_pairs={{0,1},{1,0},{2,3},{3,2},{4,5},{5,4},{6,7},{7,6},{8,9},{9,8},{10,11... | collective-permute-start | bytes 12582920 | tf_op jit(solution)/shard_map/ppermute | solution.py:430
  1.1 94.0 %collective-permute-start.28 = (f32[2048,512]{1,0:T(8,128)}, f32[2048,512]{1,0:T(8,128)}, u32[]{:S(2)}, u32[]{:S(2)}) collective-permute-start(f32[2048,512]{1,0:T(8,128)} %refs_6_.9), channel_id=1, source_target_pairs={{0,2},{1,3},{2,0},{3,1},{4,6},{5,7},{6,4},{7,5},{8,10},{9,11},{10,... | collective-permute-start | bytes 12582920 | tf_op jit(solution)/shard_map/ppermute | solution.py:430
  5.9 17.4 %collective-permute-start = (f32[256,256]{1,0:T(8,128)}, f32[256,256]{1,0:T(8,128)S(1)}, u32[]{:S(2)}, u32[]{:S(2)}) collective-permute-start(f32[256,256]{1,0:T(8,128)} %get-tuple-element.12.token_ref), channel_id=1, source_target_pairs={{0,4},{4,0},{8,12},{12,8},{16,20},{20,16},{24,28},{28,24},{1,5},{5... | collective-permute-start | bytes 786440 | tf_op jit(solution)/shard_map/ppermute | solution.py:322
  13.9 9.5 %collective-permute-start.1 = (f32[256,256]{1,0:T(8,128)}, f32[256,256]{1,0:T(8,128)S(1)}, u32[]{:S(2)}, u32[]{:S(2)}) collective-permute-start(f32[256,256]{1,0:T(8,128)} %shard_map.69.refs_2_), channel_id=1, source_target_pairs={{0,4},{4,0},{8,12},{12,8},{16,20},{20,16},{24,28},{28,24},{1,5},{5... | collective-permute-start | bytes 786440 | tf_op jit(solution)/shard_map/ppermute | solution.py:333
  14.4 13.4 %collective-permute-start.2 = (f32[256,256]{1,0:T(8,128)}, f32[256,256]{1,0:T(8,128)S(1)}, u32[]{:S(2)}, u32[]{:S(2)}) collective-permute-start(f32[256,256]{1,0:T(8,128)} %get-tuple-element.13.refs_4_), channel_id=1, source_target_pairs={{4,0},{12,8},{20,16},{28,24},{5,1},{13,9},{21,17},{29,25},{6,2},{1... | collective-permute-start | bytes 786440 | tf_op jit(solution)/shard_map/ppermute | solution.py:323
  23.3 4.5 %copy-start.14 = (f32[256,256]{1,0:T(8,128)}, f32[256,256]{1,0:T(8,128)S(1)}, u32[]{:S(2)}) copy-start(f32[256,256]{1,0:T(8,128)S(1)} %collective-permute-done.1.refs_3_) | copy-start | bytes 786436
  23.3 4.5 %copy-start.13 = (f32[256,256]{1,0:T(8,128)}, f32[256,256]{1,0:T(8,128)S(1)}, u32[]{:S(2)}) copy-start(f32[256,256]{1,0:T(8,128)S(1)} %collective-permute-done.refs_1_) | copy-start | bytes 786436
  27.8 0.7 copy-start.15
  32.0 12.3 %collective-permute-start.3 = (f32[256,512]{1,0:T(8,128)}, f32[256,512]{1,0:T(8,128)}, u32[]{:S(2)}, u32[]{:S(2)}) collective-permute-start(f32[256,512]{1,0:T(8,128)} %shard_map.70.token_ref.refs_10_.refs_1_.refs_0_), channel_id=1, source_target_pairs={{0,8},{4,12},{1,9},{5,13},{2,10},{6,14},{3,11},{7,15}} | collective-permute-start | bytes 1572872 | tf_op jit(solution)/shard_map/ppermute | solution.py:300
  35.8 9.3 %collective-permute-start.5 = (f32[128,512]{1,0:T(8,128)}, f32[128,512]{1,0:T(8,128)S(1)}, u32[]{:S(2)}, u32[]{:S(2)}) collective-permute-start(f32[128,512]{1,0:T(8,128)} %shard_map.71), channel_id=1, source_target_pairs={{8,12},{12,8},{16,20},{20,16},{24,28},{28,24},{9,13},{13,9},{17,21... | collective-permute-start | bytes 786440 | tf_op jit(solution)/shard_map/ppermute | solution.py:334
  38.4 12.4 %collective-permute-start.9 = (f32[128,1024]{1,0:T(8,128)}, f32[128,1024]{1,0:T(8,128)}, u32[]{:S(2)}, u32[]{:S(2)}) collective-permute-start(f32[128,1024]{1,0:T(8,128)} %shard_map.74), channel_id=1, source_target_pairs={{16,20},{20,16},{24,28},{28,24},{17,21},{21,17},{25,29},{29,25},{1... | collective-permute-start | bytes 1572872 | tf_op jit(solution)/shard_map/ppermute | solution.py:397
  44.4 6.6 %collective-permute-start.8 = (f32[256,512]{1,0:T(8,128)}, f32[256,512]{1,0:T(8,128)S(1)}, u32[]{:S(2)}, u32[]{:S(2)}) collective-permute-start(f32[256,512]{1,0:T(8,128)} %collective-permute-done.3.refs_7_.refs_1_), channel_id=1, source_target_pairs={{8,16},{12,20},{9,17},{13,21},{10,18},{14,22},{11,19},{15,23}} | collective-permute-start | bytes 1572872 | tf_op jit(solution)/shard_map/ppermute | solution.py:300
  45.1 2.5 %copy-start.16 = (f32[128,512]{1,0:T(8,128)}, f32[128,512]{1,0:T(8,128)S(1)}, u32[]{:S(2)}) copy-start(f32[128,512]{1,0:T(8,128)S(1)} %collective-permute-done.5.refs_8_.refs_9_.refs_10_) | copy-start | bytes 786436
  45.8 1.7 %collective-permute-start.6 = (f32[128,512]{1,0:T(8,128)}, f32[128,512]{1,0:T(8,128)S(1)}, u32[]{:S(2)}, u32[]{:S(2)}) collective-permute-start(f32[128,512]{1,0:T(8,128)} %shard_map.72), channel_id=1, source_target_pairs={{0,1},{1,0},{2,3},{3,2},{4,5},{5,4},{6,7},{7,6},{8,9},{9,8},{10,11... | collective-permute-start | bytes 786440 | tf_op jit(solution)/shard_map/ppermute | solution.py:396
  47.6 0.7 copy-start.17
  49.1 7.0 %copy-start.1 = (f32[256,512]{1,0:T(8,128)S(1)}, f32[256,512]{1,0:T(8,128)}, u32[]{:S(2)}) copy-start(f32[256,512]{1,0:T(8,128)} %shard_map.70.token_ref.refs_10_.refs_1_.refs_0_) | copy-start | bytes 1572868
  49.2 25.0 %copy-start.2 = (f32[256,512]{1,0:T(8,128)S(1)}, f32[256,512]{1,0:T(8,128)}, u32[]{:S(2)}) copy-start(f32[256,512]{1,0:T(8,128)} %shard_map.73.refs_13_.refs_1_) | copy-start | bytes 1572868
  49.2 4.5 %collective-permute-start.7 = (f32[256,512]{1,0:T(8,128)}, f32[256,512]{1,0:T(8,128)}, u32[]{:S(2)}, u32[]{:S(2)}) collective-permute-start(f32[256,512]{1,0:T(8,128)} %shard_map.73.refs_13_.refs_1_), channel_id=1, source_target_pairs={{8,16},{12,20},{9,17},{13,21},{10,18},{14,22},{11,19},{15,23}} | collective-permute-start | bytes 1572872 | tf_op jit(solution)/shard_map/ppermute | solution.py:300
  50.8 4.3 %collective-permute-start.10 = (f32[128,1024]{1,0:T(8,128)}, f32[128,1024]{1,0:T(8,128)}, u32[]{:S(2)}, u32[]{:S(2)}) collective-permute-start(f32[128,1024]{1,0:T(8,128)} %collective-permute-done.9.refs_11_.refs_12_), channel_id=1, source_target_pairs={{0,1},{1,0},{2,3},{3,2},{4,5},{5,4},{6,7},{7,6},{8,9},{9,8},{10,11... | collective-permute-start | bytes 1572872 | tf_op jit(solution)/shard_map/ppermute | solution.py:399
  51.0 4.2 %copy-start.7 = (f32[256,512]{1,0:T(8,128)}, f32[256,512]{1,0:T(8,128)S(1)}, u32[]{:S(2)}) copy-start(f32[256,512]{1,0:T(8,128)S(1)} %collective-permute-done.8.refs_8_.refs_2_) | copy-start | bytes 1572868
  51.0 5.1 %collective-permute-start.13 = (f32[256,512]{1,0:T(8,128)S(1)}, f32[256,512]{1,0:T(8,128)}, u32[]{:S(2)}, u32[]{:S(2)}) collective-permute-start(f32[256,512]{1,0:T(8,128)S(1)} %collective-permute-done.8.refs_8_.refs_2_), channel_id=1, source_target_pairs={{16,24},{20,28},{17,25},{21,29},{18,26},{22,30},{19,27},{23,31}} | collective-permute-start | bytes 1572872 | tf_op jit(solution)/shard_map/ppermute | solution.py:300
  52.4 21.7 %collective-permute-start.14 = (f32[256,512]{1,0:T(8,128)}, f32[256,512]{1,0:T(8,128)}, u32[]{:S(2)}, u32[]{:S(2)}) collective-permute-start(f32[256,512]{1,0:T(8,128)} %shard_map.73.refs_13_.refs_1_), channel_id=1, source_target_pairs={{8,0},{12,4},{9,1},{13,5},{10,2},{14,6},{11,3},{15,7}} | collective-permute-start | bytes 1572872 | tf_op jit(solution)/shard_map/ppermute | solution.py:300
  53.7 20.4 %collective-permute-start.12 = (f32[256,512]{1,0:T(8,128)}, f32[256,512]{1,0:T(8,128)}, u32[]{:S(2)}, u32[]{:S(2)}) collective-permute-start(f32[256,512]{1,0:T(8,128)} %collective-permute-done.7.refs_7_.refs_2_), channel_id=1, source_target_pairs={{16,24},{20,28},{17,25},{21,29},{18,26},{22,30},{19,27},{23,31}} | collective-permute-start | bytes 1572872 | tf_op jit(solution)/shard_map/ppermute | solution.py:300
  56.1 1.0 copy-start.8
  57.2 18.8 %collective-permute-start.15 = (f32[256,512]{1,0:T(8,128)S(1)}, f32[256,512]{1,0:T(8,128)S(1)}, u32[]{:S(2)}, u32[]{:S(2)}) collective-permute-start(f32[256,512]{1,0:T(8,128)S(1)} %shard_map.76.refs_4_.refs_0_), channel_id=1, source_target_pairs={{0,4},{4,0},{8,12},{12,8},{16,20},{20,16},{24,28},{28,24},{1,5},{5... | collective-permute-start | bytes 1572872 | tf_op jit(solution)/shard_map/ppermute | solution.py:377
  57.3 18.7 %collective-permute-start.11 = (f32[256,512]{1,0:T(8,128)}, f32[256,512]{1,0:T(8,128)}, u32[]{:S(2)}, u32[]{:S(2)}) collective-permute-start(f32[256,512]{1,0:T(8,128)} %shard_map.75.refs_4_.refs_2_), channel_id=1, source_target_pairs={{16,24},{20,28},{17,25},{21,29},{18,26},{22,30},{19,27},{23,31}} | collective-permute-start | bytes 1572872 | tf_op jit(solution)/shard_map/ppermute | solution.py:300
  75.2 0.8 copy-start.3
  76.0 0.8 copy-start.9
  95.2 2.4 %copy-start.4 = (f32[256,512]{1,0:T(8,128)S(1)}, f32[256,512]{1,0:T(8,128)}, u32[]{:S(2)}) copy-start(f32[256,512]{1,0:T(8,128)} %copy-done.3) | copy-start | bytes 1572868
  95.2 4.3 %copy-start.6 = (f32[128,512]{1,0:T(8,128)S(1)}, f32[128,512]{1,0:T(8,128)}, u32[]{:S(2)}) copy-start(f32[128,512]{1,0:T(8,128)} %get-tuple-element.14.refs_4_.refs_3_.token_ref) | copy-start | bytes 786436
  95.2 4.9 %copy-start.11 = (f32[128,512]{1,0:T(8,128)S(1)}, f32[128,512]{1,0:T(8,128)}, u32[]{:S(2)}) copy-start(f32[128,512]{1,0:T(8,128)} %get-tuple-element.15.refs_3_) | copy-start | bytes 786436
  95.2 51.1 %copy-start = (f32[2048,512]{1,0:T(8,128)S(1)}, f32[2048,512]{1,0:T(8,128)}, u32[]{:S(2)}) copy-start(f32[2048,512]{1,0:T(8,128)} %refs_6_.9) | copy-start | bytes 12582916
  95.2 51.1 %copy-start.10 = (f32[256,512]{1,0:T(8,128)S(1)}, f32[256,512]{1,0:T(8,128)}, u32[]{:S(2)}) copy-start(f32[256,512]{1,0:T(8,128)} %copy-done.9) | copy-start | bytes 1572868
  95.2 51.1 %copy-start.12 = (f32[512]{0:T(512)S(1)}, f32[512]{0:T(512)}, u32[]{:S(2)}) copy-start(f32[512]{0:T(512)} %param.9) | copy-start | bytes 6148
  95.2 51.1 %collective-permute-start.29 = (f32[2048,512]{1,0:T(8,128)}, f32[2048,512]{1,0:T(8,128)S(1)}, u32[]{:S(2)}, u32[]{:S(2)}) collective-permute-start(f32[2048,512]{1,0:T(8,128)} %shard_map.82.refs_10_.refs_8_), channel_id=1, source_target_pairs={{0,1},{1,0},{2,3},{3,2},{4,5},{5,4},{6,7},{7,6},{8,9},{9,8},{10,11... | collective-permute-start | bytes 12582920 | tf_op jit(solution)/shard_map/ppermute | solution.py:430
  95.3 0.8 collective-permute-start.19
  96.2 30.4 %collective-permute-start.20 = (f32[256,512]{1,0:T(8,128)S(1)}, f32[256,512]{1,0:T(8,128)S(1)}, u32[]{:S(2)}, u32[]{:S(2)}) collective-permute-start(f32[256,512]{1,0:T(8,128)S(1)} %collective-permute-done.19.refs_1_), channel_id=1, source_target_pairs={{8,0},{12,4},{9,1},{13,5},{10,2},{14,6},{11,3},{15,7}} | collective-permute-start | bytes 1572872 | tf_op jit(solution)/shard_map/ppermute | solution.py:300
  97.6 29.0 %collective-permute-start.21 = (f32[256,512]{1,0:T(8,128)S(1)}, f32[256,512]{1,0:T(8,128)S(1)}, u32[]{:S(2)}, u32[]{:S(2)}) collective-permute-start(f32[256,512]{1,0:T(8,128)S(1)} %copy-done.4), channel_id=1, source_target_pairs={{0,4},{4,0},{8,12},{12,8},{16,20},{20,16},{24,28},{28,24},{1,5},{5... | collective-permute-start | bytes 1572872 | tf_op jit(solution)/shard_map/ppermute | solution.py:377
  99.4 1.4 collective-permute-start.16
  100.1 28.1 %collective-permute-start.24 = (f32[128,512]{1,0:T(8,128)S(1)}, f32[128,512]{1,0:T(8,128)S(1)}, u32[]{:S(2)}, u32[]{:S(2)}) collective-permute-start(f32[128,512]{1,0:T(8,128)S(1)} %copy-done.11), channel_id=1, source_target_pairs={{24,16},{28,20},{25,17},{29,21},{26,18},{30,22},{27,19},{31,23}} | collective-permute-start | bytes 786440 | tf_op jit(solution)/shard_map/ppermute | solution.py:300
  100.8 28.1 %collective-permute-start.17 = (f32[128,512]{1,0:T(8,128)S(1)}, f32[128,512]{1,0:T(8,128)S(1)}, u32[]{:S(2)}, u32[]{:S(2)}) collective-permute-start(f32[128,512]{1,0:T(8,128)S(1)} %collective-permute-done.16.refs_2_), channel_id=1, source_target_pairs={{16,8},{20,12},{17,9},{21,13},{18,10},{22,14},{19,11},{23,15}} | collective-permute-start | bytes 786440 | tf_op jit(solution)/shard_map/ppermute | solution.py:300
  126.7 12.9 %collective-permute-start.22 = (f32[256,512]{1,0:T(8,128)S(1)}, f32[256,512]{1,0:T(8,128)S(1)}, u32[]{:S(2)}, u32[]{:S(2)}) collective-permute-start(f32[256,512]{1,0:T(8,128)S(1)} %shard_map.79.refs_4_), channel_id=1, source_target_pairs={{0,4},{4,0},{8,12},{12,8},{16,20},{20,16},{24,28},{28,24},{1,5},{5... | collective-permute-start | bytes 1572872 | tf_op jit(solution)/shard_map/ppermute | solution.py:377
  128.3 2.0 %collective-permute-start.25 = (f32[128,512]{1,0:T(8,128)S(1)}, f32[128,512]{1,0:T(8,128)S(1)}, u32[]{:S(2)}, u32[]{:S(2)}) collective-permute-start(f32[128,512]{1,0:T(8,128)S(1)} %collective-permute-done.24.refs_2_), channel_id=1, source_target_pairs={{16,8},{20,12},{17,9},{21,13},{18,10},{22,14},{19,11},{23,15}} | collective-permute-start | bytes 786440 | tf_op jit(solution)/shard_map/ppermute | solution.py:300
  128.9 9.1 %collective-permute-start.18 = (f32[128,512]{1,0:T(8,128)S(1)}, f32[128,512]{1,0:T(8,128)S(1)}, u32[]{:S(2)}, u32[]{:S(2)}) collective-permute-start(f32[128,512]{1,0:T(8,128)S(1)} %collective-permute-done.17.refs_1_), channel_id=1, source_target_pairs={{8,0},{12,4},{9,1},{13,5},{10,2},{14,6},{11,3},{15,7}} | collective-permute-start | bytes 786440 | tf_op jit(solution)/shard_map/ppermute | solution.py:300
  130.2 13.9 %collective-permute-start.26 = (f32[128,512]{1,0:T(8,128)S(1)}, f32[128,512]{1,0:T(8,128)S(1)}, u32[]{:S(2)}, u32[]{:S(2)}) collective-permute-start(f32[128,512]{1,0:T(8,128)S(1)} %collective-permute-done.25.refs_1_), channel_id=1, source_target_pairs={{8,0},{12,4},{9,1},{13,5},{10,2},{14,6},{11,3},{15,7}} | collective-permute-start | bytes 786440 | tf_op jit(solution)/shard_map/ppermute | solution.py:300
  144.2 19.1 %collective-permute-start.27 = (f32[128,512]{1,0:T(8,128)S(1)}, f32[128,512]{1,0:T(8,128)S(1)}, u32[]{:S(2)}, u32[]{:S(2)}) collective-permute-start(f32[128,512]{1,0:T(8,128)S(1)} %shard_map.81.refs_2_), channel_id=1, source_target_pairs={{0,4},{4,0},{8,12},{12,8},{16,20},{20,16},{24,28},{28,24},{1,5},{5... | collective-permute-start | bytes 786440 | tf_op jit(solution)/shard_map/ppermute | solution.py:377
  144.8 18.5 %collective-permute-start.23 = (f32[128,512]{1,0:T(8,128)S(1)}, f32[128,512]{1,0:T(8,128)S(1)}, u32[]{:S(2)}, u32[]{:S(2)}) collective-permute-start(f32[128,512]{1,0:T(8,128)S(1)} %shard_map.80.refs_4_.refs_0_), channel_id=1, source_target_pairs={{0,4},{4,0},{8,12},{12,8},{16,20},{20,16},{24,28},{28,24},{1,5},{5... | collective-permute-start | bytes 786440 | tf_op jit(solution)/shard_map/ppermute | solution.py:377
  146.3 2.2 %copy-start.5 = (f32[2048,512]{1,0:T(8,128)S(1)}, f32[2048,512]{1,0:T(8,128)}, u32[]{:S(2)}) copy-start(f32[2048,512]{1,0:T(8,128)} %refs_7_.1) | copy-start | bytes 12582916

commit v4 on v3

--- a/solution.py
+++ b/solution.py
@@ -52,6 +52,17 @@
     low, high = flipped[:width], flipped[width:]
     own_ref[...] = jnp.where(half == 0, low, high)
     send_ref[...] = jnp.where(half == 0, high, low)
+
+
+def mul_n3(a, b):
+    a_high, b_high = a.astype(BF16), b.astype(BF16)
+    a_low = (a - a_high.astype(F32)).astype(BF16)
+    b_low = (b - b_high.astype(F32)).astype(BF16)
+
+    def dot(x, y):
+        return jnp.dot(x, y, preferred_element_type=F32)
+
+    return dot(a_high, b_high) + dot(a_high, b_low) + dot(a_low, b_high)
 
 
 def inverse_of(tri):
@@ -79,7 +90,7 @@
         pair = (rows // (2 * step)) == (cols // (2 * step))
         below = ((rows // step) % 2 == 1) & ((cols // step) % 2 == 0)
         off = jnp.where(pair & below, tri, 0.0)
-        full = full - mul(full, mul(off, full))
+        full = full - mul_n3(full, mul_n3(off, full))
         step *= 2
     return full
 
@@ -422,7 +433,7 @@
     last = levels - 1
     rows, wide = z_trail.shape
     width = 2 * diag_block.shape[0]
-    tile = min(512, rows)
+    tile = min(1024, rows)
     depth = panel_below.shape[1]
     dma = pltpu.SemaphoreType.DMA
 

time: 172 us -> 172 us (level)
  transfers between devices with their start and end apart: 30 -> 30, of which waited for: 10 -> 10; matrix products, arithmetic and copies ran while one was open for 0% -> 0% of each run, Pallas kernels for 20% -> 19%
where the time goes in v4:
time: 172 us; the launch traced here: 171 us
  waiting for transfers between devices  90.1 us (52%)
  Pallas kernels  40.4 us (23%)
  starting transfers between devices  32.3 us (19%)
  local copies, waits for them, and re-layouts  6.99 us (4%)
    ppermute x15, waiting for transfers between devices, move(): lax.ppermute(x, 'row', [(2 * source + y, 2 * target + y) for y in (0, 1)])  55.9 us
    pallas_call x2, Pallas kernels, update(): pl.pallas_call(lambda *refs: update_kernel(plan, flips, tile, len(args),...  22.3 us
    ppermute x3, waiting for transfers between devices, flipped(): return lax.ppermute(x, 'col', [(i, i ^ flip) for i in range(cols)])  18.8 us
    ppermute x15, starting transfers between devices, move(): lax.ppermute(x, 'row', [(2 * source + y, 2 * target + y) for y in (0, 1)])  17.8 us
    ppermute x1, waiting for transfers between devices, forward_substitution(): inv_other = lax.ppermute(inv, 'row', swap)  7.6 us
    unnamed x37, local copies, waits for them, and re-layouts  6.99 us
    pallas_call x4, Pallas kernels, solve(): pl.pallas_call(lambda *refs: solve_kernel(turn, len(args), *refs), out_sh...  6.22 us
    ppermute x5, starting transfers between devices, share(): return (mine, lax.ppermute(mine, 'row', swap))  5.6 us
  transfers between devices with their start and end apart: 30, of which 10 were waited for; matrix products, arithmetic and copies ran while one was open for 0% of the time, Pallas kernels for 19%

profile of v4, /device:TPU:0, one launch (start us, length us, event | category | flops | bytes accessed | tf_op | source)
XLA Modules:
  0.0 171.0 jit_solution(17670306478138999659)
XLA Ops:
  0.6 0.5 collective-permute-start.4
  1.1 2.6 %collective-permute-start.28 = (f32[2048,512]{1,0:T(8,128)}, f32[2048,512]{1,0:T(8,128)}, u32[]{:S(2)}, u32[]{:S(2)}) collective-permute-start(f32[2048,512]{1,0:T(8,128)} %refs_6_.9), channel_id=1, source_target_pairs={{0,2},{1,3},{2,0},{3,1},{4,6},{5,7},{6,4},{7,5},{8,10},{9,11},{10,... | collective-permute-start | bytes 12582920 | tf_op jit(solution)/shard_map/ppermute | solution.py:441
  3.7 2.2 %shard_map.68 = (f32[256,256]{1,0:T(8,128)}, f32[256,256]{1,0:T(8,128)}, f32[256,256]{1,0:T(8,128)}) custom-call(f32[256,512]{1,0:T(8,128)} %z_ref.1, f32[256,2048]{1,0:T(8,128)} %refs_6_.8), custom_call_target="tpu_custom_call" | custom-call | flops 1 | bytes 1 | tf_op jit(solution)/shard_map/pallas_call | solution.py:324
  5.9 1.6 collective-permute-start
  7.5 4.9 %shard_map.69.refs_2_ = f32[256,256]{1,0:T(8,128)} custom-call(f32[256,2048]{1,0:T(8,128)} %refs_6_.8, f32[256,256]{1,0:T(8,128)} %get-tuple-element.12.token_ref), custom_call_target="tpu_custom_call" | custom-call | flops 1 | bytes 1 | tf_op jit(solution)/shard_map/pallas_call | solution.py:335
  12.4 0.6 collective-permute-start.1
  13.0 1.3 collective-permute-start.2
  14.3 7.6 %collective-permute-done.1.refs_3_ = f32[256,256]{1,0:T(8,128)S(1)} collective-permute-done((f32[256,256]{1,0:T(8,128)}, f32[256,256]{1,0:T(8,128)S(1)}, u32[]{:S(2)}, u32[]{:S(2)}) %collective-permute-start.1) | collective-permute-done | bytes 262176 | tf_op jit(solution)/shard_map/ppermute | solution.py:344
  21.9 4.5 %collective-permute-done.2.refs_5_ = f32[256,256]{1,0:T(8,128)S(1)} collective-permute-done((f32[256,256]{1,0:T(8,128)}, f32[256,256]{1,0:T(8,128)S(1)}, u32[]{:S(2)}, u32[]{:S(2)}) %collective-permute-start.2) | collective-permute-done | bytes 262176 | tf_op jit(solution)/shard_map/ppermute | solution.py:334
  26.4 0.7 copy-done.15
  27.1 3.4 %shard_map.70.token_ref.refs_10_.refs_1_.refs_0_ = f32[256,512]{1,0:T(8,128)} custom-call(f32[256,256]{1,0:T(8,128)} %get-tuple-element.11.refs_0_, f32[256,256]{1,0:T(8,128)} %copy-done.13, f32[256,256]{1,0:T(8,128)} %shard_map.69.refs_2_, f32[256,256]{1,0:T(8,128)} %copy-done.14, f32[256,256]{1,0:T(8,128)} %get-tuple-element.13.refs_4_, ...), custom_call_target="tpu_custom_call" | custom-call | flops 1 | bytes 1 | tf_op jit(solution)/shard_map/pallas_call | solution.py:353
  30.6 2.1 %collective-permute-start.3 = (f32[256,512]{1,0:T(8,128)}, f32[256,512]{1,0:T(8,128)}, u32[]{:S(2)}, u32[]{:S(2)}) collective-permute-start(f32[256,512]{1,0:T(8,128)} %shard_map.70.token_ref.refs_10_.refs_1_.refs_0_), channel_id=1, source_target_pairs={{0,8},{4,12},{1,9},{5,13},{2,10},{6,14},{3,11},{7,15}} | collective-permute-start | bytes 1572872 | tf_op jit(solution)/shard_map/ppermute | solution.py:311
  32.7 0.0 collective-permute-done.4.refs_1_.refs_9_.refs_7_
  32.7 1.7 shard_map.71
  34.3 0.7 collective-permute-start.5
  35.0 1.9 %shard_map.74 = f32[128,1024]{1,0:T(8,128)} custom-call(f32[256,2048]{1,0:T(8,128)} %refs_6_.8, f32[256,512]{1,0:T(8,128)} %shard_map.70.token_ref.refs_10_.refs_1_.refs_0_), custom_call_target="tpu_custom_call" | custom-call | flops 1 | bytes 1 | tf_op jit(solution)/shard_map/pallas_call | solution.py:314
  36.9 1.5 collective-permute-start.9
  38.4 4.5 %collective-permute-done.3.refs_7_.refs_1_ = f32[256,512]{1,0:T(8,128)} collective-permute-done((f32[256,512]{1,0:T(8,128)}, f32[256,512]{1,0:T(8,128)}, u32[]{:S(2)}, u32[]{:S(2)}) %collective-permute-start.3) | collective-permute-done | bytes 524320 | tf_op jit(solution)/shard_map/ppermute | solution.py:311
  42.9 0.7 collective-permute-start.8
  43.6 0.7 copy.10.x_ref
  44.4 1.7 %collective-permute-done.6.refs_9_.refs_10_.refs_11_ = f32[128,512]{1,0:T(8,128)S(1)} collective-permute-done((f32[128,512]{1,0:T(8,128)}, f32[128,512]{1,0:T(8,128)S(1)}, u32[]{:S(2)}, u32[]{:S(2)}) %collective-permute-start.6) | collective-permute-done | bytes 262176 | tf_op jit(solution)/shard_map/ppermute | solution.py:407
  46.1 0.7 copy-done.17
  46.8 0.9 shard_map.73.refs_13_.refs_1_
  47.7 0.0 copy-start.1
  47.7 1.6 collective-permute-start.7
  49.4 0.1 collective-permute-start.10
  49.5 1.4 collective-permute-start.13
  51.0 1.3 collective-permute-start.14
  52.3 1.5 collective-permute-start.12
  53.7 0.9 shard_map.75.refs_4_.refs_2_
  54.7 1.0 copy-done.8
  55.7 0.1 shard_map.76.refs_4_.refs_0_
  55.8 0.1 collective-permute-start.15
  55.9 1.5 collective-permute-start.11
  57.3 15.4 %collective-permute-done.14.refs_0_ = f32[256,512]{1,0:T(8,128)} collective-permute-done((f32[256,512]{1,0:T(8,128)}, f32[256,512]{1,0:T(8,128)}, u32[]{:S(2)}, u32[]{:S(2)}) %collective-permute-start.14) | collective-permute-done | bytes 524320 | tf_op jit(solution)/shard_map/ppermute | solution.py:311
  72.7 1.1 shard_map.77.refs_14_.refs_2_
  73.8 0.0 copy-start.3
  73.8 0.8 copy-done.3
  74.6 0.8 copy-done.9
  75.4 1.0 shard_map.78
  76.3 18.8 %collective-permute-done.28.x_ref = f32[2048,512]{1,0:T(8,128)} collective-permute-done((f32[2048,512]{1,0:T(8,128)}, f32[2048,512]{1,0:T(8,128)}, u32[]{:S(2)}, u32[]{:S(2)}) %collective-permute-start.28) | collective-permute-done | bytes 4194336 | tf_op jit(solution)/shard_map/ppermute | solution.py:441
  95.2 0.0 copy-start.12
  95.2 0.1 collective-permute-start.29
  95.3 0.8 collective-permute-start.19
  96.2 1.4 collective-permute-start.20
  97.6 1.9 %collective-permute-start.21 = (f32[256,512]{1,0:T(8,128)S(1)}, f32[256,512]{1,0:T(8,128)S(1)}, u32[]{:S(2)}, u32[]{:S(2)}) collective-permute-start(f32[256,512]{1,0:T(8,128)S(1)} %copy-done.4), channel_id=1, source_target_pairs={{0,4},{4,0},{8,12},{12,8},{16,20},{20,16},{24,28},{28,24},{1,5},{5... | collective-permute-start | bytes 1572872 | tf_op jit(solution)/shard_map/ppermute | solution.py:388
  99.4 0.7 collective-permute-start.16
  100.1 0.7 collective-permute-start.24
  100.8 0.9 collective-permute-start.17
  101.7 24.9 %collective-permute-done.20.refs_0_ = f32[256,512]{1,0:T(8,128)S(1)} collective-permute-done((f32[256,512]{1,0:T(8,128)S(1)}, f32[256,512]{1,0:T(8,128)S(1)}, u32[]{:S(2)}, u32[]{:S(2)}) %collective-permute-start.20) | collective-permute-done | bytes 524320 | tf_op jit(solution)/shard_map/ppermute | solution.py:311
  126.6 0.1 shard_map.79.refs_4_
  126.7 1.6 collective-permute-start.22
  128.3 0.7 collective-permute-start.25
  128.9 1.3 collective-permute-start.18
  130.2 1.3 collective-permute-start.26
  131.5 6.4 %collective-permute-done.18.refs_0_ = f32[128,512]{1,0:T(8,128)S(1)} collective-permute-done((f32[128,512]{1,0:T(8,128)S(1)}, f32[128,512]{1,0:T(8,128)S(1)}, u32[]{:S(2)}, u32[]{:S(2)}) %collective-permute-start.18) | collective-permute-done | bytes 262176 | tf_op jit(solution)/shard_map/ppermute | solution.py:311
  138.0 1.5 collective-permute-done.22.refs_4_.refs_5_
  139.6 4.6 %collective-permute-done.26.refs_0_ = f32[128,512]{1,0:T(8,128)S(1)} collective-permute-done((f32[128,512]{1,0:T(8,128)S(1)}, f32[128,512]{1,0:T(8,128)S(1)}, u32[]{:S(2)}, u32[]{:S(2)}) %collective-permute-start.26) | collective-permute-done | bytes 262176 | tf_op jit(solution)/shard_map/ppermute | solution.py:311
  144.2 0.6 collective-permute-start.27
  144.8 1.5 collective-permute-start.23
  146.3 0.0 copy-start.5
  146.4 2.2 %copy-done.5 = f32[2048,512]{1,0:T(8,128)S(1)} copy-done((f32[2048,512]{1,0:T(8,128)S(1)}, f32[2048,512]{1,0:T(8,128)}, u32[]{:S(2)}) %copy-start.5) | copy-done | bytes 4194328
  148.5 14.9 %shard_map.83 = (f32[1,512]{1,0:T(1,128)S(1)}, f32[2048,512]{1,0:T(8,128)}) custom-call(f32[256,512]{1,0:T(8,128)S(1)} %shard_map.76.refs_4_.refs_0_, f32[256,512]{1,0:T(8,128)S(1)} %copy-done.10, f32[256,512]{1,0:T(8,128)S(1)} %copy-done.4, f32[256,512]{1,0:T(8,128)S(1)} %collective-permute-done.21.refs_5_.refs_3_, f32[256,512]{1,0:T(8,128)S(1)} %shard_map.79.refs_4_, ...), custom_call_target="tpu_custom_call" | custom-call | flops 1 | bytes 1 | tf_op jit(solution)/shard_map/pallas_call | solution.py:466
  163.5 7.4 %shard_map.84 = (f32[1,512]{1,0:T(1,128)}, f32[2048,512]{1,0:T(8,128)}) custom-call(f32[128,512]{1,0:T(8,128)S(1)} %shard_map.80.refs_4_.refs_0_, f32[128,512]{1,0:T(8,128)S(1)} %collective-permute-done.23.refs_1_, f32[128,512]{1,0:T(8,128)S(1)} %shard_map.81.refs_2_, ...), custom_call_target="tpu_custom_call", output_to_operand_aliasing={{1}: (5, {})} | custom-call | flops 1 | bytes 1 | tf_op jit(solution)/shard_map/pallas_call | solution.py:466
  (50 shorter events, 0.2 us)
Async XLA Ops:
  0.6 32.0 %collective-permute-start.4 = (f32[2048,512]{1,0:T(8,128)}, f32[2048,512]{1,0:T(8,128)}, u32[]{:S(2)}, u32[]{:S(2)}) collective-permute-start(f32[2048,512]{1,0:T(8,128)} %refs_6_.9), channel_id=1, source_target_pairs={{0,1},{1,0},{2,3},{3,2},{4,5},{5,4},{6,7},{7,6},{8,9},{9,8},{10,11... | collective-permute-start | bytes 12582920 | tf_op jit(solution)/shard_map/ppermute | solution.py:441
  1.1 94.0 %collective-permute-start.28 = (f32[2048,512]{1,0:T(8,128)}, f32[2048,512]{1,0:T(8,128)}, u32[]{:S(2)}, u32[]{:S(2)}) collective-permute-start(f32[2048,512]{1,0:T(8,128)} %refs_6_.9), channel_id=1, source_target_pairs={{0,2},{1,3},{2,0},{3,1},{4,6},{5,7},{6,4},{7,5},{8,10},{9,11},{10,... | collective-permute-start | bytes 12582920 | tf_op jit(solution)/shard_map/ppermute | solution.py:441
  5.9 16.0 %collective-permute-start = (f32[256,256]{1,0:T(8,128)}, f32[256,256]{1,0:T(8,128)S(1)}, u32[]{:S(2)}, u32[]{:S(2)}) collective-permute-start(f32[256,256]{1,0:T(8,128)} %get-tuple-element.12.token_ref), channel_id=1, source_target_pairs={{0,4},{4,0},{8,12},{12,8},{16,20},{20,16},{24,28},{28,24},{1,5},{5... | collective-permute-start | bytes 786440 | tf_op jit(solution)/shard_map/ppermute | solution.py:333
  12.4 9.5 %collective-permute-start.1 = (f32[256,256]{1,0:T(8,128)}, f32[256,256]{1,0:T(8,128)S(1)}, u32[]{:S(2)}, u32[]{:S(2)}) collective-permute-start(f32[256,256]{1,0:T(8,128)} %shard_map.69.refs_2_), channel_id=1, source_target_pairs={{0,4},{4,0},{8,12},{12,8},{16,20},{20,16},{24,28},{28,24},{1,5},{5... | collective-permute-start | bytes 786440 | tf_op jit(solution)/shard_map/ppermute | solution.py:344
  13.0 13.4 %collective-permute-start.2 = (f32[256,256]{1,0:T(8,128)}, f32[256,256]{1,0:T(8,128)S(1)}, u32[]{:S(2)}, u32[]{:S(2)}) collective-permute-start(f32[256,256]{1,0:T(8,128)} %get-tuple-element.13.refs_4_), channel_id=1, source_target_pairs={{4,0},{12,8},{20,16},{28,24},{5,1},{13,9},{21,17},{29,25},{6,2},{1... | collective-permute-start | bytes 786440 | tf_op jit(solution)/shard_map/ppermute | solution.py:334
  21.9 4.5 %copy-start.14 = (f32[256,256]{1,0:T(8,128)}, f32[256,256]{1,0:T(8,128)S(1)}, u32[]{:S(2)}) copy-start(f32[256,256]{1,0:T(8,128)S(1)} %collective-permute-done.1.refs_3_) | copy-start | bytes 786436
  21.9 4.5 %copy-start.13 = (f32[256,256]{1,0:T(8,128)}, f32[256,256]{1,0:T(8,128)S(1)}, u32[]{:S(2)}) copy-start(f32[256,256]{1,0:T(8,128)S(1)} %collective-permute-done.refs_1_) | copy-start | bytes 786436
  26.4 0.7 copy-start.15
  30.6 12.3 %collective-permute-start.3 = (f32[256,512]{1,0:T(8,128)}, f32[256,512]{1,0:T(8,128)}, u32[]{:S(2)}, u32[]{:S(2)}) collective-permute-start(f32[256,512]{1,0:T(8,128)} %shard_map.70.token_ref.refs_10_.refs_1_.refs_0_), channel_id=1, source_target_pairs={{0,8},{4,12},{1,9},{5,13},{2,10},{6,14},{3,11},{7,15}} | collective-permute-start | bytes 1572872 | tf_op jit(solution)/shard_map/ppermute | solution.py:311
  34.3 9.3 %collective-permute-start.5 = (f32[128,512]{1,0:T(8,128)}, f32[128,512]{1,0:T(8,128)S(1)}, u32[]{:S(2)}, u32[]{:S(2)}) collective-permute-start(f32[128,512]{1,0:T(8,128)} %shard_map.71), channel_id=1, source_target_pairs={{8,12},{12,8},{16,20},{20,16},{24,28},{28,24},{9,13},{13,9},{17,21... | collective-permute-start | bytes 786440 | tf_op jit(solution)/shard_map/ppermute | solution.py:345
  36.9 12.4 %collective-permute-start.9 = (f32[128,1024]{1,0:T(8,128)}, f32[128,1024]{1,0:T(8,128)}, u32[]{:S(2)}, u32[]{:S(2)}) collective-permute-start(f32[128,1024]{1,0:T(8,128)} %shard_map.74), channel_id=1, source_target_pairs={{16,20},{20,16},{24,28},{28,24},{17,21},{21,17},{25,29},{29,25},{1... | collective-permute-start | bytes 1572872 | tf_op jit(solution)/shard_map/ppermute | solution.py:408
  42.9 6.6 %collective-permute-start.8 = (f32[256,512]{1,0:T(8,128)}, f32[256,512]{1,0:T(8,128)S(1)}, u32[]{:S(2)}, u32[]{:S(2)}) collective-permute-start(f32[256,512]{1,0:T(8,128)} %collective-permute-done.3.refs_7_.refs_1_), channel_id=1, source_target_pairs={{8,16},{12,20},{9,17},{13,21},{10,18},{14,22},{11,19},{15,23}} | collective-permute-start | bytes 1572872 | tf_op jit(solution)/shard_map/ppermute | solution.py:311
  43.6 2.5 %copy-start.16 = (f32[128,512]{1,0:T(8,128)}, f32[128,512]{1,0:T(8,128)S(1)}, u32[]{:S(2)}) copy-start(f32[128,512]{1,0:T(8,128)S(1)} %collective-permute-done.5.refs_8_.refs_9_.refs_10_) | copy-start | bytes 786436
  44.4 1.7 %collective-permute-start.6 = (f32[128,512]{1,0:T(8,128)}, f32[128,512]{1,0:T(8,128)S(1)}, u32[]{:S(2)}, u32[]{:S(2)}) collective-permute-start(f32[128,512]{1,0:T(8,128)} %shard_map.72), channel_id=1, source_target_pairs={{0,1},{1,0},{2,3},{3,2},{4,5},{5,4},{6,7},{7,6},{8,9},{9,8},{10,11... | collective-permute-start | bytes 786440 | tf_op jit(solution)/shard_map/ppermute | solution.py:407
  46.1 0.7 copy-start.17
  47.7 7.0 %copy-start.1 = (f32[256,512]{1,0:T(8,128)S(1)}, f32[256,512]{1,0:T(8,128)}, u32[]{:S(2)}) copy-start(f32[256,512]{1,0:T(8,128)} %shard_map.70.token_ref.refs_10_.refs_1_.refs_0_) | copy-start | bytes 1572868
  47.7 25.0 %copy-start.2 = (f32[256,512]{1,0:T(8,128)S(1)}, f32[256,512]{1,0:T(8,128)}, u32[]{:S(2)}) copy-start(f32[256,512]{1,0:T(8,128)} %shard_map.73.refs_13_.refs_1_) | copy-start | bytes 1572868
  47.7 4.5 %collective-permute-start.7 = (f32[256,512]{1,0:T(8,128)}, f32[256,512]{1,0:T(8,128)}, u32[]{:S(2)}, u32[]{:S(2)}) collective-permute-start(f32[256,512]{1,0:T(8,128)} %shard_map.73.refs_13_.refs_1_), channel_id=1, source_target_pairs={{8,16},{12,20},{9,17},{13,21},{10,18},{14,22},{11,19},{15,23}} | collective-permute-start | bytes 1572872 | tf_op jit(solution)/shard_map/ppermute | solution.py:311
  49.4 4.3 %collective-permute-start.10 = (f32[128,1024]{1,0:T(8,128)}, f32[128,1024]{1,0:T(8,128)}, u32[]{:S(2)}, u32[]{:S(2)}) collective-permute-start(f32[128,1024]{1,0:T(8,128)} %collective-permute-done.9.refs_11_.refs_12_), channel_id=1, source_target_pairs={{0,1},{1,0},{2,3},{3,2},{4,5},{5,4},{6,7},{7,6},{8,9},{9,8},{10,11... | collective-permute-start | bytes 1572872 | tf_op jit(solution)/shard_map/ppermute | solution.py:410
  49.5 4.2 %copy-start.7 = (f32[256,512]{1,0:T(8,128)}, f32[256,512]{1,0:T(8,128)S(1)}, u32[]{:S(2)}) copy-start(f32[256,512]{1,0:T(8,128)S(1)} %collective-permute-done.8.refs_8_.refs_2_) | copy-start | bytes 1572868
  49.5 5.1 %collective-permute-start.13 = (f32[256,512]{1,0:T(8,128)S(1)}, f32[256,512]{1,0:T(8,128)}, u32[]{:S(2)}, u32[]{:S(2)}) collective-permute-start(f32[256,512]{1,0:T(8,128)S(1)} %collective-permute-done.8.refs_8_.refs_2_), channel_id=1, source_target_pairs={{16,24},{20,28},{17,25},{21,29},{18,26},{22,30},{19,27},{23,31}} | collective-permute-start | bytes 1572872 | tf_op jit(solution)/shard_map/ppermute | solution.py:311
  51.0 21.7 %collective-permute-start.14 = (f32[256,512]{1,0:T(8,128)}, f32[256,512]{1,0:T(8,128)}, u32[]{:S(2)}, u32[]{:S(2)}) collective-permute-start(f32[256,512]{1,0:T(8,128)} %shard_map.73.refs_13_.refs_1_), channel_id=1, source_target_pairs={{8,0},{12,4},{9,1},{13,5},{10,2},{14,6},{11,3},{15,7}} | collective-permute-start | bytes 1572872 | tf_op jit(solution)/shard_map/ppermute | solution.py:311
  52.3 20.4 %collective-permute-start.12 = (f32[256,512]{1,0:T(8,128)}, f32[256,512]{1,0:T(8,128)}, u32[]{:S(2)}, u32[]{:S(2)}) collective-permute-start(f32[256,512]{1,0:T(8,128)} %collective-permute-done.7.refs_7_.refs_2_), channel_id=1, source_target_pairs={{16,24},{20,28},{17,25},{21,29},{18,26},{22,30},{19,27},{23,31}} | collective-permute-start | bytes 1572872 | tf_op jit(solution)/shard_map/ppermute | solution.py:311
  54.7 1.0 copy-start.8
  55.8 18.8 %collective-permute-start.15 = (f32[256,512]{1,0:T(8,128)S(1)}, f32[256,512]{1,0:T(8,128)S(1)}, u32[]{:S(2)}, u32[]{:S(2)}) collective-permute-start(f32[256,512]{1,0:T(8,128)S(1)} %shard_map.76.refs_4_.refs_0_), channel_id=1, source_target_pairs={{0,4},{4,0},{8,12},{12,8},{16,20},{20,16},{24,28},{28,24},{1,5},{5... | collective-permute-start | bytes 1572872 | tf_op jit(solution)/shard_map/ppermute | solution.py:388
  55.9 18.7 %collective-permute-start.11 = (f32[256,512]{1,0:T(8,128)}, f32[256,512]{1,0:T(8,128)}, u32[]{:S(2)}, u32[]{:S(2)}) collective-permute-start(f32[256,512]{1,0:T(8,128)} %shard_map.75.refs_4_.refs_2_), channel_id=1, source_target_pairs={{16,24},{20,28},{17,25},{21,29},{18,26},{22,30},{19,27},{23,31}} | collective-permute-start | bytes 1572872 | tf_op jit(solution)/shard_map/ppermute | solution.py:311
  73.8 0.8 copy-start.3
  74.6 0.8 copy-start.9
  95.2 2.4 %copy-start.4 = (f32[256,512]{1,0:T(8,128)S(1)}, f32[256,512]{1,0:T(8,128)}, u32[]{:S(2)}) copy-start(f32[256,512]{1,0:T(8,128)} %copy-done.3) | copy-start | bytes 1572868
  95.2 4.3 %copy-start.6 = (f32[128,512]{1,0:T(8,128)S(1)}, f32[128,512]{1,0:T(8,128)}, u32[]{:S(2)}) copy-start(f32[128,512]{1,0:T(8,128)} %get-tuple-element.14.refs_4_.refs_3_.token_ref) | copy-start | bytes 786436
  95.2 4.9 %copy-start.11 = (f32[128,512]{1,0:T(8,128)S(1)}, f32[128,512]{1,0:T(8,128)}, u32[]{:S(2)}) copy-start(f32[128,512]{1,0:T(8,128)} %get-tuple-element.15.refs_3_) | copy-start | bytes 786436
  95.2 51.1 %copy-start = (f32[2048,512]{1,0:T(8,128)S(1)}, f32[2048,512]{1,0:T(8,128)}, u32[]{:S(2)}) copy-start(f32[2048,512]{1,0:T(8,128)} %refs_6_.9) | copy-start | bytes 12582916
  95.2 51.1 %copy-start.10 = (f32[256,512]{1,0:T(8,128)S(1)}, f32[256,512]{1,0:T(8,128)}, u32[]{:S(2)}) copy-start(f32[256,512]{1,0:T(8,128)} %copy-done.9) | copy-start | bytes 1572868
  95.2 51.1 %copy-start.12 = (f32[512]{0:T(512)S(1)}, f32[512]{0:T(512)}, u32[]{:S(2)}) copy-start(f32[512]{0:T(512)} %param.9) | copy-start | bytes 6148
  95.2 51.1 %collective-permute-start.29 = (f32[2048,512]{1,0:T(8,128)}, f32[2048,512]{1,0:T(8,128)S(1)}, u32[]{:S(2)}, u32[]{:S(2)}) collective-permute-start(f32[2048,512]{1,0:T(8,128)} %shard_map.82.refs_10_.refs_8_), channel_id=1, source_target_pairs={{0,1},{1,0},{2,3},{3,2},{4,5},{5,4},{6,7},{7,6},{8,9},{9,8},{10,11... | collective-permute-start | bytes 12582920 | tf_op jit(solution)/shard_map/ppermute | solution.py:441
  95.3 0.8 collective-permute-start.19
  96.2 30.4 %collective-permute-start.20 = (f32[256,512]{1,0:T(8,128)S(1)}, f32[256,512]{1,0:T(8,128)S(1)}, u32[]{:S(2)}, u32[]{:S(2)}) collective-permute-start(f32[256,512]{1,0:T(8,128)S(1)} %collective-permute-done.19.refs_1_), channel_id=1, source_target_pairs={{8,0},{12,4},{9,1},{13,5},{10,2},{14,6},{11,3},{15,7}} | collective-permute-start | bytes 1572872 | tf_op jit(solution)/shard_map/ppermute | solution.py:311
  97.6 29.0 %collective-permute-start.21 = (f32[256,512]{1,0:T(8,128)S(1)}, f32[256,512]{1,0:T(8,128)S(1)}, u32[]{:S(2)}, u32[]{:S(2)}) collective-permute-start(f32[256,512]{1,0:T(8,128)S(1)} %copy-done.4), channel_id=1, source_target_pairs={{0,4},{4,0},{8,12},{12,8},{16,20},{20,16},{24,28},{28,24},{1,5},{5... | collective-permute-start | bytes 1572872 | tf_op jit(solution)/shard_map/ppermute | solution.py:388
  99.4 1.4 collective-permute-start.16
  100.1 28.1 %collective-permute-start.24 = (f32[128,512]{1,0:T(8,128)S(1)}, f32[128,512]{1,0:T(8,128)S(1)}, u32[]{:S(2)}, u32[]{:S(2)}) collective-permute-start(f32[128,512]{1,0:T(8,128)S(1)} %copy-done.11), channel_id=1, source_target_pairs={{24,16},{28,20},{25,17},{29,21},{26,18},{30,22},{27,19},{31,23}} | collective-permute-start | bytes 786440 | tf_op jit(solution)/shard_map/ppermute | solution.py:311
  100.8 28.1 %collective-permute-start.17 = (f32[128,512]{1,0:T(8,128)S(1)}, f32[128,512]{1,0:T(8,128)S(1)}, u32[]{:S(2)}, u32[]{:S(2)}) collective-permute-start(f32[128,512]{1,0:T(8,128)S(1)} %collective-permute-done.16.refs_2_), channel_id=1, source_target_pairs={{16,8},{20,12},{17,9},{21,13},{18,10},{22,14},{19,11},{23,15}} | collective-permute-start | bytes 786440 | tf_op jit(solution)/shard_map/ppermute | solution.py:311
  126.7 12.9 %collective-permute-start.22 = (f32[256,512]{1,0:T(8,128)S(1)}, f32[256,512]{1,0:T(8,128)S(1)}, u32[]{:S(2)}, u32[]{:S(2)}) collective-permute-start(f32[256,512]{1,0:T(8,128)S(1)} %shard_map.79.refs_4_), channel_id=1, source_target_pairs={{0,4},{4,0},{8,12},{12,8},{16,20},{20,16},{24,28},{28,24},{1,5},{5... | collective-permute-start | bytes 1572872 | tf_op jit(solution)/shard_map/ppermute | solution.py:388
  128.3 2.0 %collective-permute-start.25 = (f32[128,512]{1,0:T(8,128)S(1)}, f32[128,512]{1,0:T(8,128)S(1)}, u32[]{:S(2)}, u32[]{:S(2)}) collective-permute-start(f32[128,512]{1,0:T(8,128)S(1)} %collective-permute-done.24.refs_2_), channel_id=1, source_target_pairs={{16,8},{20,12},{17,9},{21,13},{18,10},{22,14},{19,11},{23,15}} | collective-permute-start | bytes 786440 | tf_op jit(solution)/shard_map/ppermute | solution.py:311
  128.9 9.1 %collective-permute-start.18 = (f32[128,512]{1,0:T(8,128)S(1)}, f32[128,512]{1,0:T(8,128)S(1)}, u32[]{:S(2)}, u32[]{:S(2)}) collective-permute-start(f32[128,512]{1,0:T(8,128)S(1)} %collective-permute-done.17.refs_1_), channel_id=1, source_target_pairs={{8,0},{12,4},{9,1},{13,5},{10,2},{14,6},{11,3},{15,7}} | collective-permute-start | bytes 786440 | tf_op jit(solution)/shard_map/ppermute | solution.py:311
  130.2 13.9 %collective-permute-start.26 = (f32[128,512]{1,0:T(8,128)S(1)}, f32[128,512]{1,0:T(8,128)S(1)}, u32[]{:S(2)}, u32[]{:S(2)}) collective-permute-start(f32[128,512]{1,0:T(8,128)S(1)} %collective-permute-done.25.refs_1_), channel_id=1, source_target_pairs={{8,0},{12,4},{9,1},{13,5},{10,2},{14,6},{11,3},{15,7}} | collective-permute-start | bytes 786440 | tf_op jit(solution)/shard_map/ppermute | solution.py:311
  144.2 19.2 %collective-permute-start.27 = (f32[128,512]{1,0:T(8,128)S(1)}, f32[128,512]{1,0:T(8,128)S(1)}, u32[]{:S(2)}, u32[]{:S(2)}) collective-permute-start(f32[128,512]{1,0:T(8,128)S(1)} %shard_map.81.refs_2_), channel_id=1, source_target_pairs={{0,4},{4,0},{8,12},{12,8},{16,20},{20,16},{24,28},{28,24},{1,5},{5... | collective-permute-start | bytes 786440 | tf_op jit(solution)/shard_map/ppermute | solution.py:388
  144.8 18.7 %collective-permute-start.23 = (f32[128,512]{1,0:T(8,128)S(1)}, f32[128,512]{1,0:T(8,128)S(1)}, u32[]{:S(2)}, u32[]{:S(2)}) collective-permute-start(f32[128,512]{1,0:T(8,128)S(1)} %shard_map.80.refs_4_.refs_0_), channel_id=1, source_target_pairs={{0,4},{4,0},{8,12},{12,8},{16,20},{20,16},{24,28},{28,24},{1,5},{5... | collective-permute-start | bytes 786440 | tf_op jit(solution)/shard_map/ppermute | solution.py:388
  146.3 2.2 %copy-start.5 = (f32[2048,512]{1,0:T(8,128)S(1)}, f32[2048,512]{1,0:T(8,128)}, u32[]{:S(2)}) copy-start(f32[2048,512]{1,0:T(8,128)} %refs_7_.1) | copy-start | bytes 12582916
